TPU v7x, 32 devices: a whole 2x2x4 slice. The times are simulated.
32 devices in a mesh: scale: 2 (over y), dp: 16 (over z, x, core).
Axes of the slice: x: 2, y: 2, z: 4, core: 2. Of those that a mesh axis runs over, the one named last changes fastest.
Arguments:
- tokens: bfloat16 [147456, 128], P(('scale', 'dp')), may hold values from -6 to 6
- cotangent: bfloat16 [147456, 128], P(('scale', 'dp')), may hold values from -6 to 6
- item_mask: int32 [2, 384], P('scale'), may hold values 0 or 1
- ln_gain: float32 [2, 128], replicated, may hold values from 0.5 to 1.5
- ln_bias: float32 [2, 128], replicated, may hold values from -3 to 3
- season_in: bfloat16 [2, 84, 96], replicated, may hold values from -0.875 to 0.875
- season_out: bfloat16 [2, 84, 48], replicated, may hold values from -1.25 to 1.25
- trend_in: bfloat16 [2, 168, 48], replicated, may hold values from -1.25 to 1.25
- trend_out: bfloat16 [2, 168, 96], replicated, may hold values from -0.875 to 0.875
- ffn_in: bfloat16 [2, 128, 256], replicated, may hold values from -0.5 to 0.5
- ffn_bias: float32 [2, 256], replicated, may hold values from -3 to 3
- ffn_out: bfloat16 [2, 256, 128], replicated, may hold values from -0.5 to 0.5
Outputs:
- mixed_out: bfloat16 [147456, 128], P(('scale', 'dp'))
- input_grad: bfloat16 [147456, 128], P(('scale', 'dp'))
- gain_grad: float32 [2, 128], replicated
- bias_grad: float32 [2, 128], replicated
- season_in_grad: float32 [2, 84, 96], replicated
- season_out_grad: float32 [2, 84, 48], replicated
- trend_in_grad: float32 [2, 168, 48], replicated
- trend_out_grad: float32 [2, 168, 96], replicated
- ffn_in_grad: float32 [2, 128, 256], replicated
- ffn_bias_grad: float32 [2, 256], replicated
- ffn_out_grad: float32 [2, 256, 128], replicated
All inputs are finite; a program needn't handle non-finite values. No bound on the sum of `item_mask` on one device may be relied on, other than what follows from the above.
Results may differ from a plain program's by a relative error of at most 0.017.
Values may be sent and summed in bfloat16 or wider, within the bound.
A program may use at most 192 MiB of HBM per device.

v0:
```python
import jax
import jax.numpy as jnp
from jax import lax
from jax.sharding import PartitionSpec as P

L0 = 96
KERNEL = 25
NL = 2
SEASON_ROWS = 84
TREND_ROWS = 168
HALF_L = 48


EPS = 1e-05


def shifted(array, axis, by):
    size = lax.axis_size(axis)
    pairs = [(i, i + by) for i in range(size) if 0 <= i + by < size]
    return lax.ppermute(array, axis, pairs)


def moving_matrix(length):
    half_width = (KERNEL - 1) // 2
    shifts = jnp.arange(-half_width, half_width + 1, dtype=jnp.int32)[:, None, None]
    row_place = jnp.arange(length, dtype=jnp.int32)[None, :, None]
    column_place = jnp.arange(length, dtype=jnp.int32)[None, None, :]
    matches = (jnp.clip(row_place + shifts, 0, length - 1) == column_place).astype(jnp.float32)
    return jnp.sum(matches, 0) / KERNEL


def gelu_slope(values):
    cumulative = 0.5 * (1.0 + lax.erf(values * 0.7071067811865476))
    return cumulative + values * jnp.exp(-0.5 * values * values) * 0.3989422804014327


def norm_forward(rows_in, gain_row, offset_row):
    mean_row = jnp.mean(rows_in, -1, keepdims=True)
    centered = rows_in - mean_row
    inverse = lax.rsqrt(jnp.mean(centered * centered, -1, keepdims=True) + EPS)
    unit_rows = centered * inverse
    return (unit_rows * gain_row + offset_row, unit_rows, inverse)


def apply_moving(moving, rows_in):
    blocks = rows_in.reshape(-1, L0, rows_in.shape[-1])
    result = jnp.einsum("tu,bud->btd", moving, blocks, precision=lax.Precision.HIGHEST)
    return result.reshape(rows_in.shape)


def apply_moving_back(moving, rows_in):
    blocks = rows_in.reshape(-1, L0, rows_in.shape[-1])
    result = jnp.einsum("tu,btd->bud", moving, blocks, precision=lax.Precision.HIGHEST)
    return result.reshape(rows_in.shape)


def mix_forward(first_weight, second_weight, source):
    features = source.shape[-1]
    sequences = source.reshape(-1, first_weight.shape[1], features)
    inner_act = jnp.einsum(
        "ts,bsd->btd", first_weight, sequences, preferred_element_type=jnp.float32
    )
    hidden = jax.nn.gelu(inner_act, approximate=False).astype(jnp.bfloat16)
    result = jnp.einsum("ts,bsd->btd", second_weight, hidden, preferred_element_type=jnp.float32)
    return result.reshape(-1, features).astype(jnp.bfloat16)


def mix_backward(first_weight, second_weight, source, gradient):
    features = source.shape[-1]
    sequences = source.reshape(-1, first_weight.shape[1], features)
    incoming = gradient.reshape(-1, first_weight.shape[0], features)
    inner_act = jnp.einsum(
        "ts,bsd->btd", first_weight, sequences, preferred_element_type=jnp.float32
    )
    hidden = jax.nn.gelu(inner_act, approximate=False).astype(jnp.bfloat16)
    grad_second = jnp.einsum("btd,bsd->ts", incoming, hidden, preferred_element_type=jnp.float32)
    grad_hidden = jnp.einsum(
        "ts,btd->bsd", second_weight, incoming, preferred_element_type=jnp.float32
    )
    grad_inner = (grad_hidden * gelu_slope(inner_act)).astype(jnp.bfloat16)
    grad_first = jnp.einsum(
        "btd,bsd->ts", grad_inner, sequences, preferred_element_type=jnp.float32
    )
    grad_source = jnp.einsum(
        "ts,btd->bsd", first_weight, grad_inner, preferred_element_type=jnp.float32
    )
    return (grad_first, grad_second, grad_source.astype(jnp.bfloat16).reshape(-1, features))


def link_parts(groups, coarse):
    bounds = [0, groups // 2, 3 * groups // 4, 7 * groups // 8, groups]
    fine_start = bounds[coarse - 1]
    fine_size = bounds[coarse] - fine_start
    pieces = 2 if coarse < 3 else 1
    result = []
    for part_number in range(pieces):
        lowest = fine_start + part_number * (fine_size // pieces)
        result.append((bounds[coarse] - lowest, lowest, lowest + fine_size // pieces))
    return result


def season_pair(season_in, season_out, layer_index, coarse):
    length_out = L0 >> coarse
    length_in = L0 >> coarse - 1
    row_start = L0 - length_in
    first_weight = season_in[layer_index, row_start : row_start + length_out, :length_in]
    second_weight = season_out[layer_index, row_start : row_start + length_out, :length_out]
    return (first_weight, second_weight, row_start)


def trend_pair(trend_in, trend_out, layer_index, coarse):
    length_out = L0 >> coarse - 1
    length_in = L0 >> coarse
    row_start = 2 * L0 - 2 * length_out
    first_weight = trend_in[layer_index, row_start : row_start + length_out, :length_in]
    second_weight = trend_out[layer_index, row_start : row_start + length_out, :length_out]
    return (first_weight, second_weight, row_start)


def row_weights(item_mask, groups, position, scale_id, bounds, total_rows, per_device):
    lengths = jnp.array([L0, L0 // 2, L0 // 4, L0 // 8], jnp.int32)
    starts = jnp.array(bounds[:4], jnp.int32)
    offsets_table = jnp.array(
        [
            [0, 0, 0, 0],
            [0, groups // 4, 0, 0],
            [0, groups // 4, groups // 8, 3 * groups // 8],
            [0, groups // 4, groups // 8, 3 * groups // 8],
        ],
        jnp.int32,
    )
    row_place = jnp.arange(total_rows, dtype=jnp.int32)
    item_local = row_place // lengths[scale_id]
    block_number = item_local // per_device
    within_block = item_local % per_device
    offset_row = offsets_table[scale_id]
    chosen = jnp.sum(
        jnp.where(
            block_number[:, None] == jnp.arange(4, dtype=jnp.int32)[None, :], offset_row[None, :], 0
        ),
        1,
    )
    item_global = (position - starts[scale_id] + chosen) * per_device + within_block
    item_global = jnp.clip(item_global, 0, item_mask.shape[1] - 1)
    used_rows = jnp.where(scale_id == 3, total_rows // 2, total_rows)
    weights = jnp.take(item_mask[0], item_global) * (row_place < used_rows).astype(jnp.int32)
    return weights.astype(jnp.float32)[:, None]


def body(
    tokens,
    cotangent,
    item_mask,
    ln_gain,
    ln_bias,
    season_in,
    season_out,
    trend_in,
    trend_out,
    ffn_in,
    ffn_bias,
    ffn_out,
):
    groups = lax.axis_size("dp")
    position = lax.axis_index("dp")
    bounds = [0, groups // 2, 3 * groups // 4, 7 * groups // 8, groups]
    scale_id = (
        (position >= bounds[1]).astype(jnp.int32)
        + (position >= bounds[2]).astype(jnp.int32)
        + (position >= bounds[3]).astype(jnp.int32)
    )
    total_rows, features = tokens.shape
    per_device = total_rows // L0
    half_rows = total_rows // 2
    live_rows = row_weights(item_mask, groups, position, scale_id, bounds, total_rows, per_device)
    moving = jnp.stack(
        [
            jnp.kron(jnp.eye(1 << level_index, dtype=jnp.float32), moving_matrix(L0 >> level_index))
            for level_index in range(4)
        ]
    )[scale_id]

    def pad_rows(block_rows):
        missing = total_rows - block_rows.shape[0]
        if missing == 0:
            return block_rows
        return jnp.concatenate([block_rows, jnp.zeros((missing, features), block_rows.dtype)], 0)

    field_rows = tokens.astype(jnp.float32)
    kept_layers = []
    for layer_index in range(NL):
        normed, forward_unit_rows, forward_inverse = norm_forward(
            field_rows, ln_gain[layer_index], ln_bias[layer_index]
        )
        forward_trend_rows = apply_moving(moving, normed)
        forward_season = normed - forward_trend_rows
        for forward_coarse in (1, 2, 3):
            forward_first_weight, forward_second_weight, forward_row_start = season_pair(
                season_in, season_out, layer_index, forward_coarse
            )
            mixed_rows = mix_forward(
                forward_first_weight, forward_second_weight, forward_season.astype(jnp.bfloat16)
            )
            arrived = []
            for forward_by_value, forward_lowest, forward_highest in link_parts(
                groups, forward_coarse
            ):
                arrived.append(shifted(mixed_rows, "dp", forward_by_value))
            incoming = pad_rows(jnp.concatenate(arrived, 0)).astype(jnp.float32)
            forward_season = forward_season + jnp.where(scale_id == forward_coarse, incoming, 0.0)
        forward_states = {}
        for forward_coarse in (3, 2, 1):
            forward_first_weight, forward_second_weight, forward_row_start = trend_pair(
                trend_in, trend_out, layer_index, forward_coarse
            )
            forward_valid_rows = half_rows if forward_coarse == 3 else total_rows
            forward_part_list = link_parts(groups, forward_coarse)
            source = forward_trend_rows[:forward_valid_rows].astype(jnp.bfloat16)
            mixed_rows = mix_forward(forward_first_weight, forward_second_weight, source)
            forward_share_rows = mixed_rows.shape[0] // len(forward_part_list)
            incoming = jnp.zeros((total_rows, features), jnp.float32)
            for forward_part_number, (
                forward_by_value,
                forward_lowest,
                forward_highest,
            ) in enumerate(forward_part_list):
                forward_portion = mixed_rows[
                    forward_part_number
                    * forward_share_rows : (forward_part_number + 1)
                    * forward_share_rows
                ]
                forward_arrival = shifted(forward_portion, "dp", -forward_by_value)
                forward_inside = (position >= forward_lowest) & (position < forward_highest)
                incoming = jnp.where(forward_inside, forward_arrival.astype(jnp.float32), incoming)
            forward_trend_rows = forward_trend_rows + jnp.where(
                scale_id == forward_coarse - 1, incoming, 0.0
            )
        forward_mixed_in = (forward_season + forward_trend_rows).astype(jnp.bfloat16)
        forward_inner_act = (
            jnp.dot(forward_mixed_in, ffn_in[layer_index], preferred_element_type=jnp.float32)
            + ffn_bias[layer_index]
        )
        forward_hidden = jax.nn.gelu(forward_inner_act, approximate=False).astype(jnp.bfloat16)
        branch = jnp.dot(forward_hidden, ffn_out[layer_index], preferred_element_type=jnp.float32)
        field_rows, kept = (
            field_rows + live_rows * branch,
            (
                forward_unit_rows,
                forward_inverse,
                forward_season,
                forward_trend_rows,
                forward_states,
            ),
        )
        kept_layers.append(kept)
    mixed_out = field_rows.astype(jnp.bfloat16)
    grad_rows = cotangent.astype(jnp.float32)
    layer_grads = [None] * NL
    for layer_index in reversed(range(NL)):
        backward_kept = kept_layers[layer_index]
        unit_rows, inverse, season, trend_rows, states = backward_kept
        mixed_in = (season + trend_rows).astype(jnp.bfloat16)
        inner_act = (
            jnp.dot(mixed_in, ffn_in[layer_index], preferred_element_type=jnp.float32)
            + ffn_bias[layer_index]
        )
        hidden = jax.nn.gelu(inner_act, approximate=False).astype(jnp.bfloat16)
        grad_branch = (live_rows * grad_rows).astype(jnp.bfloat16)
        grad_ffn_out = jnp.einsum(
            "rf,rd->fd", hidden, grad_branch, preferred_element_type=jnp.float32
        )
        grad_hidden = jnp.einsum(
            "rd,fd->rf", grad_branch, ffn_out[layer_index], preferred_element_type=jnp.float32
        )
        grad_inner = (grad_hidden * gelu_slope(inner_act)).astype(jnp.bfloat16)
        grad_ffn_bias = jnp.sum(grad_inner.astype(jnp.float32), 0)
        grad_ffn_in = jnp.einsum(
            "rd,rf->df", mixed_in, grad_inner, preferred_element_type=jnp.float32
        )
        grad_mixed = jnp.einsum(
            "rf,df->rd", grad_inner, ffn_in[layer_index], preferred_element_type=jnp.float32
        )
        grad_season = grad_mixed
        grad_trend = grad_mixed
        season_in_grad = jnp.zeros((SEASON_ROWS, L0), jnp.float32)
        season_out_grad = jnp.zeros((SEASON_ROWS, HALF_L), jnp.float32)
        trend_in_grad = jnp.zeros((TREND_ROWS, HALF_L), jnp.float32)
        trend_out_grad = jnp.zeros((TREND_ROWS, L0), jnp.float32)
        for coarse in (1, 2, 3):
            first_weight, second_weight, row_start = trend_pair(
                trend_in, trend_out, layer_index, coarse
            )
            valid_rows = half_rows if coarse == 3 else total_rows
            part_list = link_parts(groups, coarse)
            outgoing = grad_trend.astype(jnp.bfloat16)
            collected = []
            for by_value, lowest, highest in part_list:
                collected.append(shifted(outgoing, "dp", by_value))
            grad_first, grad_second, grad_source = mix_backward(
                first_weight,
                second_weight,
                trend_rows[:valid_rows].astype(jnp.bfloat16),
                jnp.concatenate(collected, 0),
            )
            owner_flag = (scale_id == coarse).astype(jnp.float32)
            grad_trend = grad_trend + owner_flag * pad_rows(grad_source.astype(jnp.float32))
            trend_in_grad = trend_in_grad.at[
                row_start : row_start + first_weight.shape[0], : first_weight.shape[1]
            ].add(owner_flag * grad_first)
            trend_out_grad = trend_out_grad.at[
                row_start : row_start + second_weight.shape[0], : second_weight.shape[1]
            ].add(owner_flag * grad_second)
        for coarse in (3, 2, 1):
            first_weight, second_weight, row_start = season_pair(
                season_in, season_out, layer_index, coarse
            )
            valid_rows = half_rows if coarse == 3 else total_rows
            part_list = link_parts(groups, coarse)
            share_rows = valid_rows // len(part_list)
            outgoing = grad_season[:valid_rows].astype(jnp.bfloat16)
            received = jnp.zeros((share_rows, features), jnp.bfloat16)
            for part_number, (by_value, lowest, highest) in enumerate(part_list):
                portion = outgoing[part_number * share_rows : (part_number + 1) * share_rows]
                arrival = shifted(portion, "dp", -by_value)
                inside = (position >= lowest) & (position < highest)
                received = jnp.where(inside, arrival, received)
            grad_first, grad_second, grad_source = mix_backward(
                first_weight, second_weight, season.astype(jnp.bfloat16), received
            )
            owner_flag = (scale_id == coarse - 1).astype(jnp.float32)
            grad_season = grad_season + owner_flag * grad_source.astype(jnp.float32)
            season_in_grad = season_in_grad.at[
                row_start : row_start + first_weight.shape[0], : first_weight.shape[1]
            ].add(owner_flag * grad_first)
            season_out_grad = season_out_grad.at[
                row_start : row_start + second_weight.shape[0], : second_weight.shape[1]
            ].add(owner_flag * grad_second)
        grad_normed = grad_season + apply_moving_back(moving, grad_trend - grad_season)
        grad_gain = jnp.sum(grad_normed * unit_rows, 0)
        grad_bias = jnp.sum(grad_normed, 0)
        grad_unit = grad_normed * ln_gain[layer_index]
        grad_field = inverse * (
            grad_unit
            - jnp.mean(grad_unit, -1, keepdims=True)
            - unit_rows * jnp.mean(grad_unit * unit_rows, -1, keepdims=True)
        )
        grad_rows, found = (
            grad_rows + grad_field,
            (
                grad_gain,
                grad_bias,
                season_in_grad,
                season_out_grad,
                trend_in_grad,
                trend_out_grad,
                grad_ffn_in,
                grad_ffn_bias,
                grad_ffn_out,
            ),
        )
        layer_grads[layer_index] = found
    stacked = [
        jnp.stack([layer_grads[layer_index][member] for layer_index in range(NL)])
        for member in range(9)
    ]
    stacked = lax.psum(
        (
            stacked[0],
            stacked[1],
            stacked[2],
            stacked[3],
            stacked[4],
            stacked[5],
            stacked[6],
            stacked[7],
            stacked[8],
        ),
        ("scale", "dp"),
    )
    return (
        mixed_out,
        grad_rows.astype(jnp.bfloat16),
        stacked[0],
        stacked[1],
        stacked[2],
        stacked[3],
        stacked[4],
        stacked[5],
        stacked[6],
        stacked[7],
        stacked[8],
    )


def solution(mesh):
    placed = (
        P(("scale", "dp"), None),
        P(("scale", "dp"), None),
        P("scale", None),
        P(),
        P(),
        P(),
        P(),
        P(),
        P(),
        P(),
        P(),
        P(),
    )
    return jax.shard_map(
        body,
        mesh=mesh,
        in_specs=placed,
        out_specs=(
            P(("scale", "dp"), None),
            P(("scale", "dp"), None),
            P(),
            P(),
            P(),
            P(),
            P(),
            P(),
            P(),
            P(),
            P(),
        ),
        check_vma=False,
    )
```

profile of v0, /device:TPU:0, one launch (start us, length us, event | category | flops | bytes accessed | tf_op | source)
XLA Modules:
  0.0 1418.8 jit_solution(9432860776444249928)
XLA Ops:
  21.6 7.4 fusion.410
  30.7 29.4 %collective-permute-done.5 = bf16[4608,128]{1,0:T(8,128)(2,1)S(1)} collective-permute-done((bf16[4608,128]{1,0:T(8,128)(2,1)}, bf16[4608,128]{1,0:T(8,128)(2,1)S(1)}, u32[]{:S(2)}, u32[]{:S(2)}) %collective-permute-start.5) | collective-permute-done | bytes 1179680 | tf_op jit(solution)/shard_map/ppermute | solution.py:20
  63.2 13.9 convert_bitcast_fusion.3
  86.6 25.1 %collective-permute-done.7 = bf16[4608,128]{1,0:T(8,128)(2,1)} collective-permute-done((bf16[4608,128]{1,0:T(8,128)(2,1)}, bf16[4608,128]{1,0:T(8,128)(2,1)}, u32[]{:S(2)}, u32[]{:S(2)}) %collective-permute-start.7) | collective-permute-done | bytes 1179680 | tf_op jit(solution)/shard_map/ppermute | solution.py:20
  111.8 6.4 fusion.1757
  122.5 24.9 %collective-permute-start.1 = (bf16[2304,128]{1,0:T(8,128)(2,1)S(1)}, bf16[2304,128]{1,0:T(8,128)(2,1)S(1)}, u32[]{:S(2)}, u32[]{:S(2)}) collective-permute-start(bf16[2304,128]{1,0:T(8,128)(2,1)S(1)} %bitcast.2112), channel_id=1, source_target_pairs={{0,4},{1,5},{2,6},{3,7},{4,8},{5,9},{6,10},{7,11},{8,12},{9,13},{1... | collective-permute-start | bytes 1769480 | tf_op jit(solution)/shard_map/ppermute | solution.py:20
  155.4 5.8 collective-permute-done.1
  161.1 10.0 collective-permute-done
  171.1 8.3 fusion.412
  179.4 5.0 convolution_convert_fusion.15
  184.5 5.1 collective-permute-start.3
  189.6 16.9 %collective-permute-start.2 = (bf16[2304,128]{1,0:T(8,128)(2,1)}, bf16[2304,128]{1,0:T(8,128)(2,1)}, u32[]{:S(2)}, u32[]{:S(2)}) collective-permute-start(bf16[2304,128]{1,0:T(8,128)(2,1)} %bitcast.2115), channel_id=1, source_target_pairs={{0,4},{1,5},{2,6},{3,7},{4,8},{5,9},{6,10},{7,11},{8,12},{9,13},{1... | collective-permute-start | bytes 1769480 | tf_op jit(solution)/shard_map/ppermute | solution.py:20
  206.5 13.9 convert_bitcast_fusion.2
  226.5 8.5 fusion.1758
  235.0 5.2 fusion.433
  244.6 27.8 %gather_fusion = s32[4608]{0:T(1024)S(1)} fusion(s32[384]{0:T(512)S(1)} %reduce.48, s32[5120]{0:T(1024)S(1)} %pad_clamp_fusion), kind=kCustom, calls=%fused_computation | custom fusion | bytes 55296 | tf_op jit(solution)/shard_map/jit(_take)/gather | solution.py:146
  276.8 5.4 fusion.760
  282.2 12.2 fusion.13
  306.2 8.0 fusion.411
  315.7 27.1 %collective-permute-done.15 = bf16[4608,128]{1,0:T(8,128)(2,1)S(1)} collective-permute-done((bf16[4608,128]{1,0:T(8,128)(2,1)}, bf16[4608,128]{1,0:T(8,128)(2,1)S(1)}, u32[]{:S(2)}, u32[]{:S(2)}) %collective-permute-start.15) | collective-permute-done | bytes 1179680 | tf_op jit(solution)/shard_map/ppermute | solution.py:20
  346.3 13.9 convert_bitcast_fusion.1
  374.8 43.8 %collective-permute-done.17 = bf16[4608,128]{1,0:T(8,128)(2,1)} collective-permute-done((bf16[4608,128]{1,0:T(8,128)(2,1)}, bf16[4608,128]{1,0:T(8,128)(2,1)}, u32[]{:S(2)}, u32[]{:S(2)}) %collective-permute-start.17) | collective-permute-done | bytes 1179680 | tf_op jit(solution)/shard_map/ppermute | solution.py:20
  418.7 5.6 fusion.1755
  424.3 5.2 convolution_convert_fusion.12
  429.5 25.3 %collective-permute-start.11 = (bf16[2304,128]{1,0:T(8,128)(2,1)}, bf16[2304,128]{1,0:T(8,128)(2,1)S(1)}, u32[]{:S(2)}, u32[]{:S(2)}) collective-permute-start(bf16[2304,128]{1,0:T(8,128)(2,1)} %bitcast.2118), channel_id=1, source_target_pairs={{0,4},{1,5},{2,6},{3,7},{4,8},{5,9},{6,10},{7,11},{8,12},{9,13},{1... | collective-permute-start | bytes 1769480 | tf_op jit(solution)/shard_map/ppermute | solution.py:20
  464.1 4.7 collective-permute-done.11
  468.8 10.2 collective-permute-done.10
  479.0 7.3 fusion.414
  486.3 5.0 convolution_convert_fusion.14
  491.3 6.1 collective-permute-start.13
  497.4 14.8 %collective-permute-start.12 = (bf16[2304,128]{1,0:T(8,128)(2,1)}, bf16[2304,128]{1,0:T(8,128)(2,1)}, u32[]{:S(2)}, u32[]{:S(2)}) collective-permute-start(bf16[2304,128]{1,0:T(8,128)(2,1)} %bitcast.2117), channel_id=1, source_target_pairs={{0,4},{1,5},{2,6},{3,7},{4,8},{5,9},{6,10},{7,11},{8,12},{9,13},{1... | collective-permute-start | bytes 1769480 | tf_op jit(solution)/shard_map/ppermute | solution.py:20
  512.2 13.9 convert_bitcast_fusion
  532.5 8.6 fusion.1756
  541.1 6.1 fusion.432
  556.5 25.8 %collective-permute-done.19 = bf16[4608,128]{1,0:T(8,128)(2,1)} collective-permute-done((bf16[4608,128]{1,0:T(8,128)(2,1)}, bf16[4608,128]{1,0:T(8,128)(2,1)}, u32[]{:S(2)}, u32[]{:S(2)}) %collective-permute-start.19) | collective-permute-done | bytes 1179680 | tf_op jit(solution)/shard_map/ppermute | solution.py:20
  586.3 12.2 fusion.22
  598.5 4.7 convert_reduce_fusion
  608.9 27.4 %collective-permute-start.26 = (bf16[4608,128]{1,0:T(8,128)(2,1)}, bf16[4608,128]{1,0:T(8,128)(2,1)}, u32[]{:S(2)}, u32[]{:S(2)}) collective-permute-start(bf16[4608,128]{1,0:T(8,128)(2,1)} %get-tuple-element.409), channel_id=1, source_target_pairs={{0,4},{1,5},{2,6},{3,7},{4,8},{5,9},{6,10},{7,11},{8,12},{9,13},{1... | collective-permute-start | bytes 3538952 | tf_op jit(solution)/shard_map/ppermute | solution.py:20
  663.2 11.4 collective-permute-done.20
  677.5 5.1 fusion.685
  699.5 10.4 fusion.632
  709.9 5.7 collective-permute-start.28
  715.6 27.5 %collective-permute-start.27 = (bf16[4608,128]{1,0:T(8,128)(2,1)}, bf16[4608,128]{1,0:T(8,128)(2,1)}, u32[]{:S(2)}, u32[]{:S(2)}) collective-permute-start(bf16[4608,128]{1,0:T(8,128)(2,1)} %get-tuple-element.372), channel_id=1, source_target_pairs={{0,4},{1,5},{2,6},{3,7},{4,8},{5,9},{6,10},{7,11},{8,12},{9,13},{1... | collective-permute-start | bytes 3538952 | tf_op jit(solution)/shard_map/ppermute | solution.py:20
  751.5 4.9 fusion.674
  760.1 6.2 collective-permute-done.27
  783.8 11.1 fusion.660
  794.9 26.3 %collective-permute-start.29 = (bf16[4608,128]{1,0:T(8,128)(2,1)}, bf16[4608,128]{1,0:T(8,128)(2,1)}, u32[]{:S(2)}, u32[]{:S(2)}) collective-permute-start(bf16[4608,128]{1,0:T(8,128)(2,1)} %get-tuple-element.370), channel_id=1, source_target_pairs={{0,2},{1,3},{2,4},{3,5},{4,6},{5,7},{6,8},{7,9},{8,10},{9,11},{10,... | collective-permute-start | bytes 3538952 | tf_op jit(solution)/shard_map/ppermute | solution.py:20
  850.9 5.2 add_subtract_fusion.1
  876.5 6.5 collective-permute-start.36
  883.0 6.2 collective-permute-start.35
  889.2 7.1 fusion.924
  909.9 8.6 collective-permute-done.30
  919.6 5.1 fusion.684
  942.8 10.4 fusion.635
  953.2 15.7 %collective-permute-start.38 = (bf16[4608,128]{1,0:T(8,128)(2,1)}, bf16[4608,128]{1,0:T(8,128)(2,1)}, u32[]{:S(2)}, u32[]{:S(2)}) collective-permute-start(bf16[4608,128]{1,0:T(8,128)(2,1)} %get-tuple-element.369), channel_id=1, source_target_pairs={{0,2},{1,3},{2,4},{3,5},{4,6},{5,7},{6,8},{7,9},{8,10},{9,11},{10,... | collective-permute-start | bytes 3538952 | tf_op jit(solution)/shard_map/ppermute | solution.py:20
  968.9 28.2 %collective-permute-start.37 = (bf16[4608,128]{1,0:T(8,128)(2,1)}, bf16[4608,128]{1,0:T(8,128)(2,1)}, u32[]{:S(2)}, u32[]{:S(2)}) collective-permute-start(bf16[4608,128]{1,0:T(8,128)(2,1)} %get-tuple-element.369), channel_id=1, source_target_pairs={{0,4},{1,5},{2,6},{3,7},{4,8},{5,9},{6,10},{7,11},{8,12},{9,13},{1... | collective-permute-start | bytes 3538952 | tf_op jit(solution)/shard_map/ppermute | solution.py:20
  1005.5 4.9 fusion.675
  1014.2 4.7 collective-permute-done.37
  1036.3 11.1 fusion.663
  1047.4 17.9 %collective-permute-start.39 = (bf16[4608,128]{1,0:T(8,128)(2,1)}, bf16[4608,128]{1,0:T(8,128)(2,1)}, u32[]{:S(2)}, u32[]{:S(2)}) collective-permute-start(bf16[4608,128]{1,0:T(8,128)(2,1)} %get-tuple-element.367), channel_id=1, source_target_pairs={{0,2},{1,3},{2,4},{3,5},{4,6},{5,7},{6,8},{7,9},{8,10},{9,11},{10,... | collective-permute-start | bytes 3538952 | tf_op jit(solution)/shard_map/ppermute | solution.py:20
  1089.3 6.6 fusion.925
  1116.3 6.6 fusion.208
  1122.9 141.6 %all-reduce.17.cloned.1.call-done = (f32[2,128]{1,0:T(2,128)}, f32[2,128]{1,0:T(2,128)}, f32[2,84,96]{2,1,0:T(8,128)}, f32[2,84,48]{1,2,0:T(8,128)}, f32[2,168,48]{1,2,0:T(8,128)}, /*index=5*/f32[2,256]{1,0:T(2,128)}) async-done(((f32[2,128]{1,0:T(2,128)}, f32[2,128]{1,0:T(2,128)}, f32[2,84,96]{2,1,0:T(8,128)}, f32[2,84,48]{1,2,0:T(8,128)}, f32[2,168,48]{1,2,0:T(8,128)}, /*index=5*/f32[2,256]{1,0:T(2,128)}), ...) | async-done | bytes 165392 | tf_op jit(solution)/shard_map/psum | solution.py:366
  1266.0 134.1 %all-reduce.19.cloned.1.call-done = (f32[2,168,96]{2,1,0:T(8,128)}, f32[2,128,256]{2,1,0:T(8,128)}, f32[2,256,128]{2,1,0:T(8,128)}) async-done(((f32[2,168,96]{2,1,0:T(8,128)}, f32[2,128,256]{2,1,0:T(8,128)}, f32[2,256,128]{2,1,0:T(8,128)}), (f32[2,168,96]{2,1,0:T(8,128)}, f32[2,128,256]{2,1,0:T(8,128)}, f32[2,256,128]{2,1,0:T(8,128)})) %all-reduce.19.cloned.1.call-update) | async-done | bytes 653328 | tf_op jit(solution)/shard_map/psum | solution.py:366
  (583 shorter events, 365.3 us)
Async XLA Ops:
  7.2 146.8 %copy-start = (s32[1,384]{1,0:T(1,128)S(1)}, s32[1,384]{1,0:T(1,128)}, u32[]{:S(2)}) copy-start(s32[1,384]{1,0:T(1,128)} %param.65) | copy-start | bytes 4612
  7.2 1257.2 %all-reduce.17.cloned.1.call-start = ((), (), s32[]{:S(2)}) async-start(), calls=%async_computation | async-start | bytes 483328 | tf_op jit(solution)/shard_map/psum | solution.py:366
  9.7 216.8 %copy-start.68 = (f32[4608]{0:T(1024)}, f32[4608]{0:T(1024)S(1)}, u32[]{:S(2)}) copy-start(f32[4608]{0:T(1024)S(1)} %broadcast_multiply_fusion.9) | copy-start | bytes 55300
  13.5 213.0 %copy-start.84 = (f32[4608]{0:T(1024)}, f32[4608]{0:T(1024)S(1)}, u32[]{:S(2)}) copy-start(f32[4608]{0:T(1024)S(1)} %add_rsqrt_fusion.1) | copy-start | bytes 55300
  15.3 211.2 %copy-start.131 = (f32[128]{0:T(128)}, f32[128]{0:T(128)S(1)}, u32[]{:S(2)}) copy-start(f32[128]{0:T(128)S(1)} %get-tuple-element.417) | copy-start | bytes 1540
  29.1 31.0 %collective-permute-start.5 = (bf16[4608,128]{1,0:T(8,128)(2,1)}, bf16[4608,128]{1,0:T(8,128)(2,1)S(1)}, u32[]{:S(2)}, u32[]{:S(2)}) collective-permute-start(bf16[4608,128]{1,0:T(8,128)(2,1)} %bitcast.2110), channel_id=1, source_target_pairs={{2,0},{3,1},{4,2},{5,3},{6,4},{7,5},{8,6},{9,7},{10,8},{11,9},{12,... | collective-permute-start | bytes 3538952 | tf_op jit(solution)/shard_map/ppermute | solution.py:20
  80.5 31.1 %collective-permute-start.7 = (bf16[4608,128]{1,0:T(8,128)(2,1)}, bf16[4608,128]{1,0:T(8,128)(2,1)}, u32[]{:S(2)}, u32[]{:S(2)}) collective-permute-start(bf16[4608,128]{1,0:T(8,128)(2,1)} %bitcast.57), channel_id=1, source_target_pairs={{4,0},{5,1},{6,2},{7,3},{8,4},{9,5},{10,6},{11,7},{12,8},{13,9},{1... | collective-permute-start | bytes 3538952 | tf_op jit(solution)/shard_map/ppermute | solution.py:20
  81.8 29.9 %collective-permute-start.6 = (bf16[4608,128]{1,0:T(8,128)(2,1)}, bf16[4608,128]{1,0:T(8,128)(2,1)}, u32[]{:S(2)}, u32[]{:S(2)}) collective-permute-start(bf16[4608,128]{1,0:T(8,128)(2,1)} %bitcast.56), channel_id=1, source_target_pairs={{2,0},{3,1},{4,2},{5,3},{6,4},{7,5},{8,6},{9,7},{10,8},{11,9},{12,... | collective-permute-start | bytes 3538952 | tf_op jit(solution)/shard_map/ppermute | solution.py:20
  85.9 284.3 %copy-start.128 = (bf16[1,12,24]{2,0,1:T(2,128)(2,1)}, bf16[1,12,24]{2,0,1:T(2,128)(2,1)S(1)}, u32[]{:S(2)}) copy-start(bf16[1,12,24]{2,0,1:T(2,128)(2,1)S(1)} %get-tuple-element.392) | copy-start | bytes 1732
  86.6 31.6 %copy-start.118 = (bf16[1,48,96]{2,0,1:T(2,128)(2,1)}, bf16[1,48,96]{2,0,1:T(2,128)(2,1)S(1)}, u32[]{:S(2)}) copy-start(bf16[1,48,96]{2,0,1:T(2,128)(2,1)S(1)} %get-tuple-element.396) | copy-start | bytes 27652
  86.6 31.6 %copy-start.146 = (bf16[2,84,48]{1,2,0:T(8,128)(2,1)S(1)}, bf16[2,84,48]{1,2,0:T(8,128)(2,1)}, u32[]{:S(2)}) copy-start(bf16[2,84,48]{1,2,0:T(8,128)(2,1)} %param.69) | copy-start | bytes 48388
  118.2 34.5 %copy-start.147 = (s32[4]{0:T(128)S(1)}, s32[4]{0:T(128)}, u32[]{:S(2)}) copy-start(s32[4]{0:T(128)} %constant.887.clone) | copy-start | bytes 52
  122.5 38.6 %collective-permute-start.1 = (bf16[2304,128]{1,0:T(8,128)(2,1)S(1)}, bf16[2304,128]{1,0:T(8,128)(2,1)S(1)}, u32[]{:S(2)}, u32[]{:S(2)}) collective-permute-start(bf16[2304,128]{1,0:T(8,128)(2,1)S(1)} %bitcast.2112), channel_id=1, source_target_pairs={{0,4},{1,5},{2,6},{3,7},{4,8},{5,9},{6,10},{7,11},{8,12},{9,13},{1... | collective-permute-start | bytes 1769480 | tf_op jit(solution)/shard_map/ppermute | solution.py:20
  147.4 23.7 %collective-permute-start = (bf16[2304,128]{1,0:T(8,128)(2,1)S(1)}, bf16[2304,128]{1,0:T(8,128)(2,1)S(1)}, u32[]{:S(2)}, u32[]{:S(2)}) collective-permute-start(bf16[2304,128]{1,0:T(8,128)(2,1)S(1)} %bitcast.2113), channel_id=1, source_target_pairs={{0,8},{1,9},{2,10},{3,11},{4,12},{5,13},{6,14},{7,15},{16,24},{17,... | collective-permute-start | bytes 1769480 | tf_op jit(solution)/shard_map/ppermute | solution.py:20
  184.5 41.9 %collective-permute-start.3 = (bf16[2304,128]{1,0:T(8,128)(2,1)}, bf16[2304,128]{1,0:T(8,128)(2,1)S(1)}, u32[]{:S(2)}, u32[]{:S(2)}) collective-permute-start(bf16[2304,128]{1,0:T(8,128)(2,1)} %bitcast.2114), channel_id=1, source_target_pairs={{0,2},{1,3},{2,4},{3,5},{4,6},{5,7},{6,8},{7,9},{8,10},{9,11},{10,... | collective-permute-start | bytes 1769480 | tf_op jit(solution)/shard_map/ppermute | solution.py:20
  189.6 36.9 %collective-permute-start.2 = (bf16[2304,128]{1,0:T(8,128)(2,1)}, bf16[2304,128]{1,0:T(8,128)(2,1)}, u32[]{:S(2)}, u32[]{:S(2)}) collective-permute-start(bf16[2304,128]{1,0:T(8,128)(2,1)} %bitcast.2115), channel_id=1, source_target_pairs={{0,4},{1,5},{2,6},{3,7},{4,8},{5,9},{6,10},{7,11},{8,12},{9,13},{1... | collective-permute-start | bytes 1769480 | tf_op jit(solution)/shard_map/ppermute | solution.py:20
  223.6 51.8 %collective-permute-start.9 = (bf16[4608,128]{1,0:T(8,128)(2,1)}, bf16[4608,128]{1,0:T(8,128)(2,1)}, u32[]{:S(2)}, u32[]{:S(2)}) collective-permute-start(bf16[4608,128]{1,0:T(8,128)(2,1)} %bitcast.67), channel_id=1, source_target_pairs={{8,0},{9,1},{10,2},{11,3},{12,4},{13,5},{14,6},{15,7},{24,16},{25,... | collective-permute-start | bytes 3538952 | tf_op jit(solution)/shard_map/ppermute | solution.py:20
  224.9 51.9 %collective-permute-start.8 = (bf16[4608,128]{1,0:T(8,128)(2,1)}, bf16[4608,128]{1,0:T(8,128)(2,1)}, u32[]{:S(2)}, u32[]{:S(2)}) collective-permute-start(bf16[4608,128]{1,0:T(8,128)(2,1)} %bitcast.66), channel_id=1, source_target_pairs={{4,0},{5,1},{6,2},{7,3},{8,4},{9,5},{10,6},{11,7},{12,8},{13,9},{1... | collective-permute-start | bytes 3538952 | tf_op jit(solution)/shard_map/ppermute | solution.py:20
  240.4 36.5 %collective-permute-start.4 = (bf16[2304,128]{1,0:T(8,128)(2,1)S(1)}, bf16[2304,128]{1,0:T(8,128)(2,1)S(1)}, u32[]{:S(2)}, u32[]{:S(2)}) collective-permute-start(bf16[2304,128]{1,0:T(8,128)(2,1)S(1)} %convert_element_type.600), channel_id=1, source_target_pairs={{0,2},{1,3},{2,4},{3,5},{4,6},{5,7},{6,8},{7,9},{8,10},{9,11},{10,... | collective-permute-start | bytes 1769480 | tf_op jit(solution)/shard_map/ppermute | solution.py:20
  244.6 28.4 %copy-start.104 = (s32[4608]{0:T(1024)S(1)}, s32[4608]{0:T(1024)}, u32[]{:S(2)}) copy-start(s32[4608]{0:T(1024)} %copy-done.103) | copy-start | bytes 55300
  314.2 28.6 %collective-permute-start.15 = (bf16[4608,128]{1,0:T(8,128)(2,1)}, bf16[4608,128]{1,0:T(8,128)(2,1)S(1)}, u32[]{:S(2)}, u32[]{:S(2)}) collective-permute-start(bf16[4608,128]{1,0:T(8,128)(2,1)} %bitcast.2111), channel_id=1, source_target_pairs={{2,0},{3,1},{4,2},{5,3},{6,4},{7,5},{8,6},{9,7},{10,8},{11,9},{12,... | collective-permute-start | bytes 3538952 | tf_op jit(solution)/shard_map/ppermute | solution.py:20
  363.6 55.0 %collective-permute-start.17 = (bf16[4608,128]{1,0:T(8,128)(2,1)}, bf16[4608,128]{1,0:T(8,128)(2,1)}, u32[]{:S(2)}, u32[]{:S(2)}) collective-permute-start(bf16[4608,128]{1,0:T(8,128)(2,1)} %bitcast.122), channel_id=1, source_target_pairs={{4,0},{5,1},{6,2},{7,3},{8,4},{9,5},{10,6},{11,7},{12,8},{13,9},{1... | collective-permute-start | bytes 3538952 | tf_op jit(solution)/shard_map/ppermute | solution.py:20
  365.0 53.6 %collective-permute-start.16 = (bf16[4608,128]{1,0:T(8,128)(2,1)}, bf16[4608,128]{1,0:T(8,128)(2,1)}, u32[]{:S(2)}, u32[]{:S(2)}) collective-permute-start(bf16[4608,128]{1,0:T(8,128)(2,1)} %bitcast.121), channel_id=1, source_target_pairs={{2,0},{3,1},{4,2},{5,3},{6,4},{7,5},{8,6},{9,7},{10,8},{11,9},{12,... | collective-permute-start | bytes 3538952 | tf_op jit(solution)/shard_map/ppermute | solution.py:20
  370.3 48.4 %copy-start.5 = (f32[48,128,96]{1,2,0:T(8,128)S(1)}, f32[48,128,96]{1,2,0:T(8,128)}, u32[]{:S(2)}) copy-start(f32[48,128,96]{1,2,0:T(8,128)} %copy-done.4) | copy-start | bytes 7077892
  370.3 48.4 %copy-start.48 = (bf16[4608,128]{1,0:T(8,128)(2,1)S(1)}, bf16[4608,128]{1,0:T(8,128)(2,1)}, u32[]{:S(2)}) copy-start(bf16[4608,128]{1,0:T(8,128)(2,1)} %copy-done.47) | copy-start | bytes 3538948
  370.3 48.4 %copy-start.64 = (f32[4608]{0:T(1024)S(1)}, f32[4608]{0:T(1024)}, u32[]{:S(2)}) copy-start(f32[4608]{0:T(1024)} %copy-done.63) | copy-start | bytes 55300
  370.3 48.4 %copy-start.80 = (f32[4608]{0:T(1024)S(1)}, f32[4608]{0:T(1024)}, u32[]{:S(2)}) copy-start(f32[4608]{0:T(1024)} %copy-done.79) | copy-start | bytes 55300
  429.4 30.7 %copy-start.18 = (bf16[4608,128]{1,0:T(8,128)(2,1)S(1)}, bf16[4608,128]{1,0:T(8,128)(2,1)}, u32[]{:S(2)}) copy-start(bf16[4608,128]{1,0:T(8,128)(2,1)} %get-tuple-element.361) | copy-start | bytes 3538948
  429.5 39.3 %collective-permute-start.11 = (bf16[2304,128]{1,0:T(8,128)(2,1)}, bf16[2304,128]{1,0:T(8,128)(2,1)S(1)}, u32[]{:S(2)}, u32[]{:S(2)}) collective-permute-start(bf16[2304,128]{1,0:T(8,128)(2,1)} %bitcast.2118), channel_id=1, source_target_pairs={{0,4},{1,5},{2,6},{3,7},{4,8},{5,9},{6,10},{7,11},{8,12},{9,13},{1... | collective-permute-start | bytes 1769480 | tf_op jit(solution)/shard_map/ppermute | solution.py:20
  454.7 24.2 %collective-permute-start.10 = (bf16[2304,128]{1,0:T(8,128)(2,1)}, bf16[2304,128]{1,0:T(8,128)(2,1)S(1)}, u32[]{:S(2)}, u32[]{:S(2)}) collective-permute-start(bf16[2304,128]{1,0:T(8,128)(2,1)} %bitcast.2119), channel_id=1, source_target_pairs={{0,8},{1,9},{2,10},{3,11},{4,12},{5,13},{6,14},{7,15},{16,24},{17,... | collective-permute-start | bytes 1769480 | tf_op jit(solution)/shard_map/ppermute | solution.py:20
  491.3 41.1 %collective-permute-start.13 = (bf16[2304,128]{1,0:T(8,128)(2,1)}, bf16[2304,128]{1,0:T(8,128)(2,1)}, u32[]{:S(2)}, u32[]{:S(2)}) collective-permute-start(bf16[2304,128]{1,0:T(8,128)(2,1)} %bitcast.2116), channel_id=1, source_target_pairs={{0,2},{1,3},{2,4},{3,5},{4,6},{5,7},{6,8},{7,9},{8,10},{9,11},{10,... | collective-permute-start | bytes 1769480 | tf_op jit(solution)/shard_map/ppermute | solution.py:20
  497.4 35.0 %collective-permute-start.12 = (bf16[2304,128]{1,0:T(8,128)(2,1)}, bf16[2304,128]{1,0:T(8,128)(2,1)}, u32[]{:S(2)}, u32[]{:S(2)}) collective-permute-start(bf16[2304,128]{1,0:T(8,128)(2,1)} %bitcast.2117), channel_id=1, source_target_pairs={{0,4},{1,5},{2,6},{3,7},{4,8},{5,9},{6,10},{7,11},{8,12},{9,13},{1... | collective-permute-start | bytes 1769480 | tf_op jit(solution)/shard_map/ppermute | solution.py:20
  529.5 52.8 %collective-permute-start.19 = (bf16[4608,128]{1,0:T(8,128)(2,1)}, bf16[4608,128]{1,0:T(8,128)(2,1)}, u32[]{:S(2)}, u32[]{:S(2)}) collective-permute-start(bf16[4608,128]{1,0:T(8,128)(2,1)} %bitcast.132), channel_id=1, source_target_pairs={{8,0},{9,1},{10,2},{11,3},{12,4},{13,5},{14,6},{15,7},{24,16},{25,... | collective-permute-start | bytes 3538952 | tf_op jit(solution)/shard_map/ppermute | solution.py:20
  531.2 52.4 %collective-permute-start.18 = (bf16[4608,128]{1,0:T(8,128)(2,1)}, bf16[4608,128]{1,0:T(8,128)(2,1)}, u32[]{:S(2)}, u32[]{:S(2)}) collective-permute-start(bf16[4608,128]{1,0:T(8,128)(2,1)} %bitcast.131), channel_id=1, source_target_pairs={{4,0},{5,1},{6,2},{7,3},{8,4},{9,5},{10,6},{11,7},{12,8},{13,9},{1... | collective-permute-start | bytes 3538952 | tf_op jit(solution)/shard_map/ppermute | solution.py:20
  549.2 34.3 %collective-permute-start.14 = (bf16[2304,128]{1,0:T(8,128)(2,1)}, bf16[2304,128]{1,0:T(8,128)(2,1)S(1)}, u32[]{:S(2)}, u32[]{:S(2)}) collective-permute-start(bf16[2304,128]{1,0:T(8,128)(2,1)} %convert_element_type.638), channel_id=1, source_target_pairs={{0,2},{1,3},{2,4},{3,5},{4,6},{5,7},{6,8},{7,9},{8,10},{9,11},{10,... | collective-permute-start | bytes 1769480 | tf_op jit(solution)/shard_map/ppermute | solution.py:20
  552.7 30.9 %copy-start.37 = (f32[4608,128]{1,0:T(8,128)S(1)}, f32[4608,128]{1,0:T(8,128)}, u32[]{:S(2)}) copy-start(f32[4608,128]{1,0:T(8,128)} %get-tuple-element.354) | copy-start | bytes 7077892
  552.7 30.9 %copy-start.38 = (f32[4608,128]{1,0:T(8,128)S(1)}, f32[4608,128]{1,0:T(8,128)}, u32[]{:S(2)}) copy-start(f32[4608,128]{1,0:T(8,128)} %get-tuple-element.356) | copy-start | bytes 7077892
  586.2 52.6 %copy-start.21 = (bf16[4608,128]{1,0:T(8,128)(2,1)}, bf16[4608,128]{1,0:T(8,128)(2,1)S(1)}, u32[]{:S(2)}) copy-start(bf16[4608,128]{1,0:T(8,128)(2,1)S(1)} %get-tuple-element.363) | copy-start | bytes 3538948
  608.9 77.5 %collective-permute-start.26 = (bf16[4608,128]{1,0:T(8,128)(2,1)}, bf16[4608,128]{1,0:T(8,128)(2,1)}, u32[]{:S(2)}, u32[]{:S(2)}) collective-permute-start(bf16[4608,128]{1,0:T(8,128)(2,1)} %get-tuple-element.409), channel_id=1, source_target_pairs={{0,4},{1,5},{2,6},{3,7},{4,8},{5,9},{6,10},{7,11},{8,12},{9,13},{1... | collective-permute-start | bytes 3538952 | tf_op jit(solution)/shard_map/ppermute | solution.py:20
  636.3 50.1 %collective-permute-start.25 = (bf16[4608,128]{1,0:T(8,128)(2,1)}, bf16[4608,128]{1,0:T(8,128)(2,1)}, u32[]{:S(2)}, u32[]{:S(2)}) collective-permute-start(bf16[4608,128]{1,0:T(8,128)(2,1)} %get-tuple-element.409), channel_id=1, source_target_pairs={{0,8},{1,9},{2,10},{3,11},{4,12},{5,13},{6,14},{7,15},{16,24},{17,... | collective-permute-start | bytes 3538952 | tf_op jit(solution)/shard_map/ppermute | solution.py:20
  657.8 16.9 %collective-permute-start.20 = (bf16[2304,128]{1,0:T(8,128)(2,1)S(1)}, bf16[2304,128]{1,0:T(8,128)(2,1)S(1)}, u32[]{:S(2)}, u32[]{:S(2)}) collective-permute-start(bf16[2304,128]{1,0:T(8,128)(2,1)S(1)} %copy-done.92), channel_id=1, source_target_pairs={{2,0},{3,1},{4,2},{5,3},{6,4},{7,5},{8,6},{9,7},{10,8},{11,9},{12,... | collective-permute-start | bytes 1769480 | tf_op jit(solution)/shard_map/ppermute | solution.py:20
  696.6 48.7 %collective-permute-start.22 = (bf16[2304,128]{1,0:T(8,128)(2,1)S(1)}, bf16[2304,128]{1,0:T(8,128)(2,1)S(1)}, u32[]{:S(2)}, u32[]{:S(2)}) collective-permute-start(bf16[2304,128]{1,0:T(8,128)(2,1)S(1)} %get-tuple-element.389), channel_id=1, source_target_pairs={{4,0},{5,1},{6,2},{7,3},{8,4},{9,5},{10,6},{11,7},{12,8},{13,9},{1... | collective-permute-start | bytes 1769480 | tf_op jit(solution)/shard_map/ppermute | solution.py:20
  697.9 45.2 %copy-start.23 = (bf16[4608,128]{1,0:T(8,128)(2,1)S(1)}, bf16[4608,128]{1,0:T(8,128)(2,1)}, u32[]{:S(2)}) copy-start(bf16[4608,128]{1,0:T(8,128)(2,1)} %copy-done.21) | copy-start | bytes 3538948
  697.9 47.4 %collective-permute-start.21 = (bf16[2304,128]{1,0:T(8,128)(2,1)S(1)}, bf16[2304,128]{1,0:T(8,128)(2,1)S(1)}, u32[]{:S(2)}, u32[]{:S(2)}) collective-permute-start(bf16[2304,128]{1,0:T(8,128)(2,1)S(1)} %get-tuple-element.390), channel_id=1, source_target_pairs={{2,0},{3,1},{4,2},{5,3},{6,4},{7,5},{8,6},{9,7},{10,8},{11,9},{12,... | collective-permute-start | bytes 1769480 | tf_op jit(solution)/shard_map/ppermute | solution.py:20
  709.9 35.5 %copy-start.75 = (f32[96,24,128]{2,1,0:T(8,128)S(1)}, f32[96,24,128]{2,1,0:T(8,128)}, u32[]{:S(2)}) copy-start(f32[96,24,128]{2,1,0:T(8,128)} %convolution_bitcast_fusion.5) | copy-start | bytes 3538948
  709.9 50.2 %collective-permute-start.28 = (bf16[4608,128]{1,0:T(8,128)(2,1)}, bf16[4608,128]{1,0:T(8,128)(2,1)}, u32[]{:S(2)}, u32[]{:S(2)}) collective-permute-start(bf16[4608,128]{1,0:T(8,128)(2,1)} %get-tuple-element.372), channel_id=1, source_target_pairs={{0,2},{1,3},{2,4},{3,5},{4,6},{5,7},{6,8},{7,9},{8,10},{9,11},{10,... | collective-permute-start | bytes 3538952 | tf_op jit(solution)/shard_map/ppermute | solution.py:20
  715.6 50.7 %collective-permute-start.27 = (bf16[4608,128]{1,0:T(8,128)(2,1)}, bf16[4608,128]{1,0:T(8,128)(2,1)}, u32[]{:S(2)}, u32[]{:S(2)}) collective-permute-start(bf16[4608,128]{1,0:T(8,128)(2,1)} %get-tuple-element.372), channel_id=1, source_target_pairs={{0,4},{1,5},{2,6},{3,7},{4,8},{5,9},{6,10},{7,11},{8,12},{9,13},{1... | collective-permute-start | bytes 3538952 | tf_op jit(solution)/shard_map/ppermute | solution.py:20
  781.0 48.0 %collective-permute-start.24 = (bf16[2304,128]{1,0:T(8,128)(2,1)}, bf16[2304,128]{1,0:T(8,128)(2,1)}, u32[]{:S(2)}, u32[]{:S(2)}) collective-permute-start(bf16[2304,128]{1,0:T(8,128)(2,1)} %get-tuple-element.387), channel_id=1, source_target_pairs={{8,0},{9,1},{10,2},{11,3},{12,4},{13,5},{14,6},{15,7},{24,16},{25,... | collective-permute-start | bytes 1769480 | tf_op jit(solution)/shard_map/ppermute | solution.py:20
  782.3 46.7 %collective-permute-start.23 = (bf16[2304,128]{1,0:T(8,128)(2,1)}, bf16[2304,128]{1,0:T(8,128)(2,1)}, u32[]{:S(2)}, u32[]{:S(2)}) collective-permute-start(bf16[2304,128]{1,0:T(8,128)(2,1)} %get-tuple-element.388), channel_id=1, source_target_pairs={{4,0},{5,1},{6,2},{7,3},{8,4},{9,5},{10,6},{11,7},{12,8},{13,9},{1... | collective-permute-start | bytes 1769480 | tf_op jit(solution)/shard_map/ppermute | solution.py:20
  794.9 49.5 %collective-permute-start.29 = (bf16[4608,128]{1,0:T(8,128)(2,1)}, bf16[4608,128]{1,0:T(8,128)(2,1)}, u32[]{:S(2)}, u32[]{:S(2)}) collective-permute-start(bf16[4608,128]{1,0:T(8,128)(2,1)} %get-tuple-element.370), channel_id=1, source_target_pairs={{0,2},{1,3},{2,4},{3,5},{4,6},{5,7},{6,8},{7,9},{8,10},{9,11},{10,... | collective-permute-start | bytes 3538952 | tf_op jit(solution)/shard_map/ppermute | solution.py:20
  876.5 52.2 %collective-permute-start.36 = (bf16[4608,128]{1,0:T(8,128)(2,1)}, bf16[4608,128]{1,0:T(8,128)(2,1)}, u32[]{:S(2)}, u32[]{:S(2)}) collective-permute-start(bf16[4608,128]{1,0:T(8,128)(2,1)} %get-tuple-element.411), channel_id=1, source_target_pairs={{0,4},{1,5},{2,6},{3,7},{4,8},{5,9},{6,10},{7,11},{8,12},{9,13},{1... | collective-permute-start | bytes 3538952 | tf_op jit(solution)/shard_map/ppermute | solution.py:20
  883.0 47.6 %collective-permute-start.35 = (bf16[4608,128]{1,0:T(8,128)(2,1)}, bf16[4608,128]{1,0:T(8,128)(2,1)}, u32[]{:S(2)}, u32[]{:S(2)}) collective-permute-start(bf16[4608,128]{1,0:T(8,128)(2,1)} %get-tuple-element.411), channel_id=1, source_target_pairs={{0,8},{1,9},{2,10},{3,11},{4,12},{5,13},{6,14},{7,15},{16,24},{17,... | collective-permute-start | bytes 3538952 | tf_op jit(solution)/shard_map/ppermute | solution.py:20
  897.5 21.1 %collective-permute-start.30 = (bf16[2304,128]{1,0:T(8,128)(2,1)}, bf16[2304,128]{1,0:T(8,128)(2,1)S(1)}, u32[]{:S(2)}, u32[]{:S(2)}) collective-permute-start(bf16[2304,128]{1,0:T(8,128)(2,1)} %slice.812), channel_id=1, source_target_pairs={{2,0},{3,1},{4,2},{5,3},{6,4},{7,5},{8,6},{9,7},{10,8},{11,9},{12,... | collective-permute-start | bytes 1769480 | tf_op jit(solution)/shard_map/ppermute | solution.py:20
  939.9 59.4 %collective-permute-start.32 = (bf16[2304,128]{1,0:T(8,128)(2,1)S(1)}, bf16[2304,128]{1,0:T(8,128)(2,1)S(1)}, u32[]{:S(2)}, u32[]{:S(2)}) collective-permute-start(bf16[2304,128]{1,0:T(8,128)(2,1)S(1)} %get-tuple-element.385), channel_id=1, source_target_pairs={{4,0},{5,1},{6,2},{7,3},{8,4},{9,5},{10,6},{11,7},{12,8},{13,9},{1... | collective-permute-start | bytes 1769480 | tf_op jit(solution)/shard_map/ppermute | solution.py:20
  941.2 56.0 %copy-start.20 = (bf16[4608,128]{1,0:T(8,128)(2,1)S(1)}, bf16[4608,128]{1,0:T(8,128)(2,1)}, u32[]{:S(2)}) copy-start(bf16[4608,128]{1,0:T(8,128)(2,1)} %get-tuple-element.361) | copy-start | bytes 3538948
  941.2 58.1 %collective-permute-start.31 = (bf16[2304,128]{1,0:T(8,128)(2,1)S(1)}, bf16[2304,128]{1,0:T(8,128)(2,1)S(1)}, u32[]{:S(2)}, u32[]{:S(2)}) collective-permute-start(bf16[2304,128]{1,0:T(8,128)(2,1)S(1)} %get-tuple-element.386), channel_id=1, source_target_pairs={{2,0},{3,1},{4,2},{5,3},{6,4},{7,5},{8,6},{9,7},{10,8},{11,9},{12,... | collective-permute-start | bytes 1769480 | tf_op jit(solution)/shard_map/ppermute | solution.py:20
  953.2 46.2 %copy-start.74 = (f32[96,24,128]{2,1,0:T(8,128)S(1)}, f32[96,24,128]{2,1,0:T(8,128)}, u32[]{:S(2)}) copy-start(f32[96,24,128]{2,1,0:T(8,128)} %convolution_bitcast_fusion.4) | copy-start | bytes 3538948
  953.2 61.0 %collective-permute-start.38 = (bf16[4608,128]{1,0:T(8,128)(2,1)}, bf16[4608,128]{1,0:T(8,128)(2,1)}, u32[]{:S(2)}, u32[]{:S(2)}) collective-permute-start(bf16[4608,128]{1,0:T(8,128)(2,1)} %get-tuple-element.369), channel_id=1, source_target_pairs={{0,2},{1,3},{2,4},{3,5},{4,6},{5,7},{6,8},{7,9},{8,10},{9,11},{10,... | collective-permute-start | bytes 3538952 | tf_op jit(solution)/shard_map/ppermute | solution.py:20
  968.9 49.9 %collective-permute-start.37 = (bf16[4608,128]{1,0:T(8,128)(2,1)}, bf16[4608,128]{1,0:T(8,128)(2,1)}, u32[]{:S(2)}, u32[]{:S(2)}) collective-permute-start(bf16[4608,128]{1,0:T(8,128)(2,1)} %get-tuple-element.369), channel_id=1, source_target_pairs={{0,4},{1,5},{2,6},{3,7},{4,8},{5,9},{6,10},{7,11},{8,12},{9,13},{1... | collective-permute-start | bytes 3538952 | tf_op jit(solution)/shard_map/ppermute | solution.py:20
  1033.3 39.7 %collective-permute-start.34 = (bf16[2304,128]{1,0:T(8,128)(2,1)}, bf16[2304,128]{1,0:T(8,128)(2,1)}, u32[]{:S(2)}, u32[]{:S(2)}) collective-permute-start(bf16[2304,128]{1,0:T(8,128)(2,1)} %get-tuple-element.383), channel_id=1, source_target_pairs={{8,0},{9,1},{10,2},{11,3},{12,4},{13,5},{14,6},{15,7},{24,16},{25,... | collective-permute-start | bytes 1769480 | tf_op jit(solution)/shard_map/ppermute | solution.py:20
  1034.6 38.4 %collective-permute-start.33 = (bf16[2304,128]{1,0:T(8,128)(2,1)}, bf16[2304,128]{1,0:T(8,128)(2,1)}, u32[]{:S(2)}, u32[]{:S(2)}) collective-permute-start(bf16[2304,128]{1,0:T(8,128)(2,1)} %get-tuple-element.384), channel_id=1, source_target_pairs={{4,0},{5,1},{6,2},{7,3},{8,4},{9,5},{10,6},{11,7},{12,8},{13,9},{1... | collective-permute-start | bytes 1769480 | tf_op jit(solution)/shard_map/ppermute | solution.py:20
  1047.4 39.4 %collective-permute-start.39 = (bf16[4608,128]{1,0:T(8,128)(2,1)}, bf16[4608,128]{1,0:T(8,128)(2,1)}, u32[]{:S(2)}, u32[]{:S(2)}) collective-permute-start(bf16[4608,128]{1,0:T(8,128)(2,1)} %get-tuple-element.367), channel_id=1, source_target_pairs={{0,2},{1,3},{2,4},{3,5},{4,6},{5,7},{6,8},{7,9},{8,10},{9,11},{10,... | collective-permute-start | bytes 3538952 | tf_op jit(solution)/shard_map/ppermute | solution.py:20
  1115.5 284.6 %all-reduce.19.cloned.1.call-start = ((), (), s32[]{:S(2)}) async-start(), calls=%async_computation.1 | async-start | bytes 1392640 | tf_op jit(solution)/shard_map/psum | solution.py:366
  1116.3 295.5 %copy-start.1 = (s32[1,384]{1,0:T(1,128)S(1)}, s32[1,384]{1,0:T(1,128)}, u32[]{:S(2)}) copy-start(s32[1,384]{1,0:T(1,128)} %param.65) | copy-start | bytes 4612
  (137 other events, 862.0 us)
Sparse Core Ops, SparseCore 0:
  1115.6 148.7 all-reduce.16
  1271.2 128.8 all-reduce.18
where the time goes:
time: 1430 us; the launch traced here: 1420 us
  waiting for transfers between devices  498 us (35%)
  matrix products  337 us (24%)
  starting transfers between devices  297 us (21%)
  other arithmetic  139 us (10%)
  local copies, waits for them, and re-layouts  130 us (9%)
  between operations  18.1 us (1%)
    ppermute x40, starting transfers between devices, shifted(): return lax.ppermute(array, axis, pairs)  297 us
    psum x2, waiting for transfers between devices, body(): lax.psum((stacked[0], stacked[1], stacked[2], stacked[3], stacked[4], sta...  276 us
    ppermute x40, waiting for transfers between devices, shifted(): return lax.ppermute(array, axis, pairs)  223 us
    dot_general x12, matrix products, mix_forward(): jnp.einsum('ts,bsd->btd', second_weight, hidden, preferred_element_type=j...  102 us
    dot_general x12, matrix products, mix_backward(): jnp.einsum('btd,bsd->ts', incoming, hidden, preferred_element_type=jnp.fl...  85.7 us
    convert_element_type x4, other arithmetic, body(): forward_season.astype(jnp.bfloat16)  32.6 us
    dot_general x12, matrix products, mix_backward(): jnp.einsum('ts,bsd->btd', first_weight, sequences, preferred_element_type...  30.8 us
    dot_general x12, matrix products, mix_backward(): jnp.einsum('ts,btd->bsd', second_weight, incoming, preferred_element_type...  30 us
  transfers between devices with their start and end apart: 42, of which 21 were waited for; matrix products, arithmetic and copies ran while one was open for 22% of the time, Pallas kernels for 0%

commit v1 on v0

v1 whole, which is shorter than its diff:
```python
import functools

import jax
import jax.numpy as jnp
from jax import lax
from jax.experimental import pallas as pl
from jax.experimental.pallas import tpu as pltpu
from jax.sharding import PartitionSpec as P

L0 = 96
KERNEL = 25
NL = 2
SEASON_ROWS = 84
TREND_ROWS = 168
EPS = 1e-05
LANES = 128
ITEMS = 8
PAIR = 4
MESH = pl.DeviceIdType.MESH
F32 = jnp.float32
BF16 = jnp.bfloat16

LENGTHS = [L0 >> i for i in range(4)]
SIZES = [ITEMS * n for n in LENGTHS]
STARTS = [sum(SIZES[:i]) for i in range(4)]
CHUNK = sum(SIZES)
SLOTS = [1, 2, 4, 4]
SELF = [(0, 0), (0, 1), (1, 1), (3, 1)]
TILE = 480

AT_SMALL, AT_SEASON_IN, AT_TREND_IN, AT_TREND_OUT = 0, 8, 96, 264
AT_FFN_IN, AT_FFN_OUT, LAYER_ROWS = 432, 688, 944
SEASON_OUT_LANE = 48


def dot(a, b):
    return jnp.dot(a, b, preferred_element_type=F32)


def dot_nt(a, b):
    return lax.dot_general(a, b, (((1,), (1,)), ((), ())), preferred_element_type=F32)


def dot_tn(a, b):
    return lax.dot_general(a, b, (((0,), (0,)), ((), ())), preferred_element_type=F32)


def dot_exact(a, b):
    return jnp.dot(a, b, preferred_element_type=F32, precision=lax.Precision.HIGHEST)


def gelu_parts(v):
    cumulative = 0.5 * (1.0 + lax.erf(v * 0.7071067811865476))
    density = jnp.exp(-0.5 * (v * v)) * 0.3989422804014327
    return v * cumulative, cumulative + v * density


def iota(shape, dim):
    return lax.broadcasted_iota(jnp.int32, shape, dim)


def selection(rows, columns, count, length, base, turned=False):
    shape = (columns, rows) if turned else (rows, columns)
    r = iota(shape, 1 if turned else 0)
    c = iota(shape, 0 if turned else 1)
    found = jnp.zeros(shape, jnp.bool_)
    for k in range(count):
        found = found | ((c == r - (k * length - base)) & (r >= k * length) & (r < (k + 1) * length))
    return found.astype(F32)


def block_mask(count, height, width, turned=False):
    shape = (count * width, count * height) if turned else (count * height, count * width)
    r = iota(shape, 1 if turned else 0)
    c = iota(shape, 0 if turned else 1)
    found = jnp.zeros(shape, jnp.bool_)
    for k in range(count):
        found = found | (
            (r >= k * height) & (r < (k + 1) * height) & (c >= k * width) & (c < (k + 1) * width)
        )
    return found.astype(F32)


def moving_counts(count, length, turned):
    size = count * length
    t = iota((size, size), 1 if turned else 0)
    u = iota((size, size), 0 if turned else 1)
    total = jnp.zeros((size, size), F32)
    half = (KERNEL - 1) // 2
    for k in range(count):
        low, high = k * length, (k + 1) * length - 1
        inside = (t >= low) & (t <= high) & (u >= low) & (u <= high)
        near = (jnp.abs(t - u) <= half).astype(F32)
        first = jnp.where(u == low, jnp.maximum(half - (t - low), 0), 0).astype(F32)
        last = jnp.where(u == high, jnp.maximum(half - (high - t), 0), 0).astype(F32)
        total = total + jnp.where(inside, near + first + last, 0.0)
    return total


def pair_of(ref, start, half, height):
    return jnp.concatenate(
        [ref[start : start + height, :], ref[start + half : start + half + height, :]], 1
    )


def fold_rows(value):
    return jnp.sum(value.reshape(-1, 8, value.shape[-1]), 0)


class Names:
    pass


def group_of(groups, scale, slot, position):
    bounds = [0, groups // 2, 3 * groups // 4, 7 * groups // 8]
    offsets = [0, groups // 4, groups // 8, 3 * groups // 8]
    return position - bounds[scale] + offsets[slot]


def home_of(groups, scale, group):
    if scale == 0:
        return group, 0
    if scale == 1:
        return groups // 2 + lax.rem(group, groups // 4), lax.div(group, groups // 4)
    part = lax.div(group, groups // 8)
    slot = jnp.where(part == 1, 2, jnp.where(part == 2, 1, part))
    first = 3 * groups // 4 if scale == 2 else 7 * groups // 8
    return first + lax.rem(group, groups // 8), slot


def kernel_body(
    groups,
    n_scale,
    per_device,
    pack_rows,
    tokens,
    cotangent,
    item_mask,
    ln_gain,
    ln_bias,
    season_in,
    season_out,
    trend_in,
    trend_out,
    ffn_in,
    ffn_bias,
    ffn_out,
    mixed_out,
    input_grad,
    packed_out,
    tok_buf,
    cot_buf,
    out_buf,
    grad_buf,
    live,
    field,
    grad,
    dz,
    unit,
    inverse,
    z_keep,
    hidden,
    slope,
    season_src,
    trend_src,
    season_hid,
    season_slope,
    trend_hid,
    trend_slope,
    sa,
    sb,
    ta,
    tb,
    sa_t,
    sb_t,
    ta_t,
    tb_t,
    moving,
    moving_t,
    moving3,
    moving3_t,
    win_t,
    wout_t,
    d_sa,
    d_sb,
    d_ta,
    d_tb,
    d_win,
    d_wout,
    d_bias,
    d_gain,
    d_off,
    pack,
    half_in,
    half_bf,
    plane_in,
    plane_bf,
    depth_in,
    in_send,
    in_recv,
    out_send,
    out_recv,
    pad_sem,
    ar_send,
    ar_recv,
):
    scale_index = lax.axis_index("scale")
    position = lax.axis_index("dp")
    worker_group = lax.rem(position, groups // 2)
    worker_half = lax.div(position, groups // 2)
    half_items = per_device // 2
    chunks = half_items // ITEMS
    bounds = [0, groups // 2, 3 * groups // 4, 7 * groups // 8, groups]

    barrier = pltpu.get_barrier_semaphore()

    def greet(k, carry):
        other = lax.rem(scale_index * groups + position + k, n_scale * groups)
        pl.semaphore_signal(
            barrier,
            inc=1,
            device_id=(lax.div(other, groups), lax.rem(other, groups)),
            device_id_type=MESH,
        )
        return carry

    lax.fori_loop(1, n_scale * groups, greet, 0)
    pl.semaphore_wait(barrier, n_scale * groups - 1)

    def inbound(kind, scale, slot, half, chunk):
        source = (tokens, cotangent)[kind]
        target = (tok_buf, cot_buf)[kind]
        length, size = LENGTHS[scale], SIZES[scale]
        first = (slot * per_device + half * half_items + chunk * ITEMS) * length
        src = source.at[pl.ds(pl.multiple_of(first, 16), size)]
        dst = target.at[chunk, pl.ds(STARTS[scale], size)]
        recv = in_recv.at[kind, chunk, scale]
        if (slot, half) == SELF[scale]:
            return pltpu.make_async_copy(src, dst, recv), False
        owner = half * (groups // 2) + group_of(groups, scale, slot, position)
        return (
            pltpu.make_async_remote_copy(
                src_ref=src,
                dst_ref=dst,
                send_sem=in_send.at[kind, chunk, slot * 2 + half],
                recv_sem=recv,
                device_id=(scale_index, owner),
                device_id_type=MESH,
            ),
            True,
        )

    def each_inbound(act):
        for scale in range(4):

            @pl.when((position >= bounds[scale]) & (position < bounds[scale + 1]))
            def _():
                def one_chunk(chunk, carry):
                    for kind in range(2):
                        for slot in range(SLOTS[scale]):
                            for half in (1, 0):
                                act(*inbound(kind, scale, slot, half, chunk))
                    return carry

                lax.fori_loop(0, chunks, one_chunk, 0)

    each_inbound(lambda copy, remote: copy.start())

    def inbound_wait(kind, chunk):
        target = (tok_buf, cot_buf)[kind]
        for scale in range(4):
            ref = target.at[chunk, pl.ds(STARTS[scale], SIZES[scale])]
            pltpu.make_async_copy(ref, ref, in_recv.at[kind, chunk, scale]).wait()

    pad_rows = SLOTS[3] * per_device * LENGTHS[3]

    def pad_copies():
        return [
            pltpu.make_async_copy(
                source.at[pl.ds(pad_rows, pad_rows)], target.at[pl.ds(pad_rows, pad_rows)], pad_sem.at[k]
            )
            for k, (source, target) in enumerate(((tokens, mixed_out), (cotangent, input_grad)))
        ]

    @pl.when(position >= bounds[3])
    def _():
        for copy in pad_copies():
            copy.start()

    def outbound(kind, scale, chunk):
        source = (out_buf, grad_buf)[kind]
        target = (mixed_out, input_grad)[kind]
        home, slot = home_of(groups, scale, worker_group)
        length, size = LENGTHS[scale], SIZES[scale]
        first = (slot * per_device + worker_half * half_items + chunk * ITEMS) * length
        src = source.at[chunk, pl.ds(STARTS[scale], size)]
        dst = target.at[pl.ds(pl.multiple_of(first, 16), size)]
        recv = out_recv.at[kind, chunk, slot * 2 + worker_half]
        local = pltpu.make_async_copy(src, dst, recv)
        remote = pltpu.make_async_remote_copy(
            src_ref=src,
            dst_ref=dst,
            send_sem=out_send.at[kind, chunk, scale],
            recv_sem=recv,
            device_id=(scale_index, home),
            device_id_type=MESH,
        )
        return home, local, remote

    def outbound_start(kind, chunk):
        for scale in range(4):
            home, local, remote = outbound(kind, scale, chunk)

            @pl.when(home == position)
            def _():
                local.start()

            @pl.when(home != position)
            def _():
                remote.start()

    for layer in range(NL):
        for c in (1, 2, 3):
            count = 1 << (c - 1)
            fine, coarse = LENGTHS[c - 1], LENGTHS[c]
            at_season = L0 - fine
            at_trend = 2 * L0 - 2 * fine
            for source, normal, turned, height, width, base in (
                (season_in, sa, sa_t, coarse, fine, at_season),
                (season_out, sb, sb_t, coarse, coarse, at_season),
                (trend_in, ta, ta_t, fine, coarse, at_trend),
                (trend_out, tb, tb_t, fine, fine, at_trend),
            ):
                whole = source[layer]
                rows = selection(count * height, whole.shape[0], count, height, base).astype(BF16)
                columns = selection(count * width, whole.shape[1], count, width, 0).astype(BF16)
                tall = dot(rows, whole).astype(BF16)
                normal[layer, c - 1] = (
                    dot_nt(tall, columns) * block_mask(count, height, width)
                ).astype(BF16)
                turned[layer, c - 1] = (
                    dot_nt(columns, tall) * block_mask(count, height, width, True)
                ).astype(BF16)
        eye_in = selection(ffn_in.shape[2], ffn_in.shape[2], 1, ffn_in.shape[2], 0).astype(BF16)
        eye_out = selection(LANES, LANES, 1, LANES, 0).astype(BF16)
        win_t[layer] = dot_nt(eye_in, ffn_in[layer]).astype(BF16)
        wout_t[layer] = dot_nt(eye_out, ffn_out[layer]).astype(BF16)
    for i in range(3):
        moving[i] = moving_counts(1 << i, LENGTHS[i], False).astype(BF16)
        moving_t[i] = moving_counts(1 << i, LENGTHS[i], True).astype(BF16)
    moving3[...] = moving_counts(PAIR, LENGTHS[3], False).astype(BF16)
    moving3_t[...] = moving_counts(PAIR, LENGTHS[3], True).astype(BF16)

    mask_rows = jnp.broadcast_to(item_mask[...].astype(F32), (LANES, item_mask.shape[1])).astype(BF16)
    first_item = worker_group * per_device + worker_half * half_items
    chosen = iota((32, item_mask.shape[1]), 1) == iota((32, item_mask.shape[1]), 0) + first_item
    item_live = dot_nt(chosen.astype(F32).astype(BF16), mask_rows).astype(BF16)
    for chunk in range(chunks):
        for i in range(4):
            place = (iota((SIZES[i], 32), 0).astype(F32) + 0.5) * (1.0 / LENGTHS[i])
            column = iota((SIZES[i], 32), 1).astype(F32) - float(chunk * ITEMS)
            one = ((place >= column) & (place < column + 1.0)).astype(F32).astype(BF16)
            live[chunk, STARTS[i] : STARTS[i] + SIZES[i], :] = dot(one, item_live)

    for total in (d_sa, d_sb, d_ta, d_tb, d_win, d_wout, d_bias, d_gain, d_off, pack):
        total[...] = jnp.zeros(total.shape, F32)

    taps = 1.0 / KERNEL
    slabs = [(0, 96, 4), (1, 96, 2), (2, 96, 1), (3, 48, 1)]

    def count_matrix(scale, turned):
        if scale == 3:
            return (moving3_t if turned else moving3)[...]
        return (moving_t if turned else moving)[scale]

    def forward(layer, carry):
        gain = ln_gain[pl.ds(layer, 1), :]
        offset = ln_bias[pl.ds(layer, 1), :]
        offset_pair = jnp.concatenate([offset, offset], 1)
        scaled = [[], [], [], []]
        season_part = [[], [], [], []]
        trend_part = [[], [], [], []]
        for scale, height, number in slabs:
            half = SIZES[scale] // 2
            for j in range(number):
                parts = []
                for side in range(2):
                    start = STARTS[scale] + side * half + j * height
                    x = field[start : start + height, :]
                    mean = jnp.mean(x, -1, keepdims=True)
                    centered = x - mean
                    inv = lax.rsqrt(jnp.mean(centered * centered, -1, keepdims=True) + EPS)
                    n = centered * inv
                    unit[layer, start : start + height, :] = n
                    inverse[layer, start : start + height, :] = jnp.broadcast_to(inv, n.shape)
                    parts.append(n * gain)
                both = jnp.concatenate(parts, 1)
                average = dot(count_matrix(scale, False), both.astype(BF16)) * taps
                scaled[scale].append(both + offset_pair)
                season_part[scale].append(both - average)
                trend_part[scale].append(average + offset_pair)

        season_mixed = [None, [], [], []]
        unit_number = 0
        sources = season_part[0]
        for c in (1, 2, 3):
            halves = []
            for j in range(PAIR >> (c - 1)):
                a = sources[j].astype(BF16)
                season_src[layer, unit_number] = a
                h, s = gelu_parts(dot(sa[layer, c - 1], a))
                h = h.astype(BF16)
                season_hid[layer, unit_number] = h
                season_slope[layer, unit_number] = s.astype(BF16)
                halves.append(dot(sb[layer, c - 1], h))
                unit_number += 1
            if c < 3:
                season_mixed[c] = [
                    jnp.concatenate(halves[2 * j : 2 * j + 2], 0) for j in range(len(halves) // 2)
                ]
            else:
                season_mixed[c] = halves
            sources = [e + m for e, m in zip(season_part[c], season_mixed[c])]

        trend_mixed = [[], [], [], None]
        sources = trend_part[3]
        for c in (3, 2, 1):
            base = {1: 0, 2: 4, 3: 6}[c]
            for j in range(PAIR >> (c - 1)):
                a = sources[j].astype(BF16)
                trend_src[layer, base + j] = a
                h, s = gelu_parts(dot(ta[layer, c - 1], a))
                h = h.astype(BF16)
                trend_hid[layer, base + j] = h
                trend_slope[layer, base + j] = s.astype(BF16)
                trend_mixed[c - 1].append(dot(tb[layer, c - 1], h))
            if c > 1:
                wide = [r + m for r, m in zip(trend_part[c - 1], trend_mixed[c - 1])]
                sources = []
                for value in wide:
                    sources.append(value[:48])
                    sources.append(value[48:])

        for scale, height, number in slabs:
            half = SIZES[scale] // 2
            for j in range(number):
                value = scaled[scale][j]
                if season_mixed[scale] is not None:
                    value = value + season_mixed[scale][j]
                if trend_mixed[scale] is not None:
                    value = value + trend_mixed[scale][j]
                value = value.astype(BF16)
                for side in range(2):
                    start = STARTS[scale] + side * half + j * height
                    z_keep[layer, start : start + height, :] = value[:, side * LANES : (side + 1) * LANES]
        return carry

    def ffn_forward(layer, live_chunk):
        bias = ffn_bias[pl.ds(layer, 1), :]
        for t in range(0, CHUNK, TILE):
            a = dot(z_keep[layer, t : t + TILE, :], ffn_in[layer]) + bias
            h, s = gelu_parts(a)
            h = h.astype(BF16)
            hidden[layer, t : t + TILE, :] = h
            slope[layer, t : t + TILE, :] = s.astype(BF16)
            f = dot(h, ffn_out[layer])
            field[t : t + TILE, :] = field[t : t + TILE, :] + live_chunk[t : t + TILE, :] * f

    def backward(layer, live_chunk):
        for t in range(0, CHUNK, TILE):
            df = (live_chunk[t : t + TILE, :] * grad[t : t + TILE, :]).astype(BF16)
            da = (dot(df, wout_t[layer]) * slope[layer, t : t + TILE, :].astype(F32)).astype(BF16)
            dz[t : t + TILE, :] = dot(da, win_t[layer])
            d_win[layer] += dot_tn(z_keep[layer, t : t + TILE, :], da)
            d_wout[layer] += dot_tn(df, hidden[layer, t : t + TILE, :])
            d_bias[layer] += fold_rows(da.astype(F32))

        def slab_of(scale, height, j):
            return pair_of(dz, STARTS[scale] + j * height, SIZES[scale] // 2, height)

        gathered = [[slab_of(scale, height, j) for j in range(number)] for scale, height, number in slabs]

        trend_grad = [None, [], [], []]
        incoming = gathered[0]
        for c in (1, 2, 3):
            base = {1: 0, 2: 4, 3: 6}[c]
            sum_b = sum_a = None
            for j in range(PAIR >> (c - 1)):
                g = incoming[j].astype(BF16)
                part_b = dot_nt(g, trend_hid[layer, base + j])
                dp = (dot(tb_t[layer, c - 1], g) * trend_slope[layer, base + j].astype(F32)).astype(BF16)
                part_a = dot_nt(dp, trend_src[layer, base + j])
                sum_b = part_b if sum_b is None else sum_b + part_b
                sum_a = part_a if sum_a is None else sum_a + part_a
                trend_grad[c].append(dot(ta_t[layer, c - 1], dp))
            d_tb[layer, c - 1] += sum_b
            d_ta[layer, c - 1] += sum_a
            if c < 3:
                trend_grad[c] = [
                    jnp.concatenate(trend_grad[c][2 * j : 2 * j + 2], 0)
                    for j in range(len(trend_grad[c]) // 2)
                ]
                incoming = [z + g for z, g in zip(gathered[c], trend_grad[c])]

        season_grad = [[], [], [], None]
        incoming = gathered[3]
        for c in (3, 2, 1):
            base = {1: 0, 2: 4, 3: 6}[c]
            sum_b = sum_a = None
            for j in range(PAIR >> (c - 1)):
                g = incoming[j].astype(BF16)
                part_b = dot_nt(g, season_hid[layer, base + j])
                dp = (dot(sb_t[layer, c - 1], g) * season_slope[layer, base + j].astype(F32)).astype(BF16)
                part_a = dot_nt(dp, season_src[layer, base + j])
                sum_b = part_b if sum_b is None else sum_b + part_b
                sum_a = part_a if sum_a is None else sum_a + part_a
                season_grad[c - 1].append(dot(sa_t[layer, c - 1], dp))
            d_sb[layer, c - 1] += sum_b
            d_sa[layer, c - 1] += sum_a
            if c > 1:
                wide = [z + g for z, g in zip(gathered[c - 1], season_grad[c - 1])]
                incoming = []
                for value in wide:
                    incoming.append(value[:48])
                    incoming.append(value[48:])

        gain = ln_gain[pl.ds(layer, 1), :]
        sum_gain = jnp.zeros((8, LANES), F32)
        sum_off = jnp.zeros((8, LANES), F32)
        for scale, height, number in slabs:
            half = SIZES[scale] // 2
            for j in range(number):
                value = gathered[scale][j]
                if scale == 0:
                    moved = -season_grad[0][j]
                    value = value + season_grad[0][j]
                elif scale == 3:
                    moved = trend_grad[3][j]
                else:
                    moved = trend_grad[scale][j] - season_grad[scale][j]
                    value = value + season_grad[scale][j]
                value = value + dot(count_matrix(scale, True), moved.astype(BF16)) * taps
                for side in range(2):
                    start = STARTS[scale] + side * half + j * height
                    d = value[:, side * LANES : (side + 1) * LANES]
                    n = unit[layer, start : start + height, :]
                    sum_gain = sum_gain + fold_rows(d * n)
                    sum_off = sum_off + fold_rows(d)
                    q = d * gain
                    mean_q = jnp.mean(q, -1, keepdims=True)
                    mean_qn = jnp.mean(q * n, -1, keepdims=True)
                    grad[start : start + height, :] = grad[start : start + height, :] + inverse[
                        layer, start : start + height, :
                    ] * (q - mean_q - n * mean_qn)
        d_gain[layer] += sum_gain
        d_off[layer] += sum_off

    def one_chunk(chunk, carry):
        inbound_wait(0, chunk)
        field[...] = tok_buf[chunk].astype(F32)

        def one_forward(layer, inner):
            forward(layer, 0)
            ffn_forward(layer, live.at[chunk])
            return inner

        lax.fori_loop(0, NL, one_forward, 0)
        out_buf[chunk] = field[...].astype(BF16)
        outbound_start(0, chunk)
        inbound_wait(1, chunk)
        grad[...] = cot_buf[chunk].astype(F32)

        def one_backward(step, inner):
            backward(NL - 1 - step, live.at[chunk])
            return inner

        lax.fori_loop(0, NL, one_backward, 0)
        grad_buf[chunk] = grad[...].astype(BF16)
        outbound_start(1, chunk)
        return carry

    lax.fori_loop(0, chunks, one_chunk, 0)

    for layer in range(NL):
        at = layer * LAYER_ROWS
        season_in_sum = season_out_sum = trend_in_sum = trend_out_sum = None
        for c in (1, 2, 3):
            count = 1 << (c - 1)
            fine, coarse = LENGTHS[c - 1], LENGTHS[c]
            at_season = L0 - fine
            at_trend = 2 * L0 - 2 * fine
            found = []
            for value, rows, height, width, base, lane in (
                (d_sa, 88, coarse, fine, at_season, 0),
                (d_sb, 88, coarse, coarse, at_season, SEASON_OUT_LANE),
                (d_ta, TREND_ROWS, fine, coarse, at_trend, 0),
                (d_tb, TREND_ROWS, fine, fine, at_trend, 0),
            ):
                masked = value[layer, c - 1] * block_mask(count, height, width)
                tall = dot_exact(selection(count * height, rows, count, height, base, True), masked)
                found.append(dot_exact(tall, selection(count * width, LANES, count, width, lane)))
            if season_in_sum is None:
                season_in_sum, season_out_sum, trend_in_sum, trend_out_sum = found
            else:
                season_in_sum += found[0]
                season_out_sum += found[1]
                trend_in_sum += found[2]
                trend_out_sum += found[3]
        pack[at : at + 1, :] = jnp.sum(d_gain[layer], 0, keepdims=True)
        pack[at + 1 : at + 2, :] = jnp.sum(d_off[layer], 0, keepdims=True)
        bias_sum = jnp.sum(d_bias[layer], 0, keepdims=True)
        pack[at + 2 : at + 3, :] = bias_sum[:, :LANES]
        pack[at + 3 : at + 4, :] = bias_sum[:, LANES:]
        pack[at + AT_SEASON_IN : at + AT_SEASON_IN + 88, :] = season_in_sum
        pack[at + AT_TREND_IN : at + AT_TREND_IN + 88, :] = trend_in_sum[:88] + season_out_sum
        pack[at + AT_TREND_IN + 88 : at + AT_TREND_IN + TREND_ROWS, :] = trend_in_sum[88:]
        pack[at + AT_TREND_OUT : at + AT_TREND_OUT + TREND_ROWS, :] = trend_out_sum
        for side in range(2):
            lanes = slice(side * LANES, (side + 1) * LANES)
            row = at + AT_FFN_IN + side * LANES
            pack[row : row + LANES, :] = d_win[layer, :, lanes]
            row = at + AT_FFN_OUT + side * LANES
            pack[row : row + LANES, :] = d_wout[layer, :, lanes]

    plane_dp = groups // 8
    plane_size = plane_dp * n_scale
    core = lax.rem(position, 2)
    place_dp = lax.rem(lax.div(position, 2), plane_dp)
    depth_index = lax.div(position, 2 * plane_dp)
    plane_index = scale_index * plane_dp + place_dp
    half_rows = pack_rows // 2
    plane_rows = half_rows // plane_size
    depth_rows = plane_rows // 4

    def core_id():
        return (scale_index, position + 1 - 2 * core)

    def plane_id(index):
        return (
            lax.div(index, plane_dp),
            depth_index * (2 * plane_dp) + lax.rem(index, plane_dp) * 2 + core,
        )

    def depth_id(index):
        return (scale_index, index * (2 * plane_dp) + place_dp * 2 + core)

    def remote(src, dst, stage, slot_out, slot_in, device):
        return pltpu.make_async_remote_copy(
            src_ref=src,
            dst_ref=dst,
            send_sem=ar_send.at[stage, slot_out],
            recv_sem=ar_recv.at[stage, slot_in],
            device_id=device,
            device_id_type=MESH,
        )

    def arrived(ref, stage, slot):
        pltpu.make_async_copy(ref, ref, ar_recv.at[stage, slot]).wait()

    mine = pl.multiple_of(core * half_rows, 16)
    theirs = pl.multiple_of((1 - core) * half_rows, 16)
    first_copy = remote(pack.at[pl.ds(theirs, half_rows)], half_in, 0, 0, 0, core_id())
    first_copy.start()
    first_copy.wait_send()
    arrived(half_in, 0, 0)
    half_bf[pl.ds(mine, half_rows)] = (pack[pl.ds(mine, half_rows)] + half_in[...]).astype(BF16)

    def plane_piece(index):
        return pl.ds(pl.multiple_of(mine + index * plane_rows, 16), plane_rows)

    def plane_round(stage, source_of, target_of, act):
        def one(k, carry):
            other = lax.rem(plane_index + k, plane_size)
            back = lax.rem(plane_index + plane_size - k, plane_size)
            act(other, back, k)
            return carry

        lax.fori_loop(1, plane_size, one, 0)

    def plane_scatter(other, back, k):
        remote(half_bf.at[plane_piece(other)], plane_in.at[k], 1, k, k, plane_id(other)).start()

    plane_round(1, None, None, plane_scatter)
    plane_sum = pack[plane_piece(plane_index)] + half_in[
        pl.ds(pl.multiple_of(plane_index * plane_rows, 16), plane_rows)
    ]

    def plane_wait(k, carry):
        remote(half_bf.at[plane_piece(0)], plane_in.at[k], 1, k, k, core_id()).wait_send()
        arrived(plane_in.at[k], 1, k)
        return carry

    lax.fori_loop(1, plane_size, plane_wait, 0)
    for k in range(1, plane_size):
        plane_sum = plane_sum + plane_in[k].astype(F32)
    plane_bf[...] = plane_sum.astype(BF16)

    def depth_piece(index):
        return pl.ds(pl.multiple_of(index * depth_rows, 16), depth_rows)

    for k in range(1, 4):
        other = lax.rem(depth_index + k, 4)
        remote(plane_bf.at[depth_piece(other)], depth_in.at[k], 2, k, k, depth_id(other)).start()
    for k in range(1, 4):
        remote(plane_bf.at[depth_piece(0)], depth_in.at[k], 2, k, k, core_id()).wait_send()
        arrived(depth_in.at[k], 2, k)
    total = plane_bf[depth_piece(depth_index)].astype(F32)
    for k in range(1, 4):
        total = total + depth_in[k].astype(F32)

    def final_piece(plane, depth):
        return pl.ds(pl.multiple_of(mine + plane * plane_rows + depth * depth_rows, 16), depth_rows)

    own = final_piece(plane_index, depth_index)
    packed_out[own] = total.astype(BF16)
    for k in range(1, 4):
        other = lax.rem(depth_index + k, 4)
        remote(packed_out.at[own], packed_out.at[own], 3, k, k, depth_id(other)).start()
    for k in range(1, 4):
        back = lax.rem(depth_index + 4 - k, 4)
        remote(packed_out.at[own], packed_out.at[own], 3, k, k, core_id()).wait_send()
        arrived(packed_out.at[final_piece(plane_index, back)], 3, k)
    own_plane = plane_piece(plane_index)

    def plane_gather(other, back, k):
        remote(packed_out.at[own_plane], packed_out.at[own_plane], 4, k, k, plane_id(other)).start()

    plane_round(4, None, None, plane_gather)

    def plane_gathered(other, back, k):
        remote(packed_out.at[own_plane], packed_out.at[own_plane], 4, k, k, core_id()).wait_send()
        arrived(packed_out.at[plane_piece(back)], 4, k)

    plane_round(4, None, None, plane_gathered)
    own_half = pl.ds(mine, half_rows)
    last_copy = remote(packed_out.at[own_half], packed_out.at[own_half], 5, 0, 0, core_id())
    last_copy.start()
    last_copy.wait_send()
    arrived(packed_out.at[pl.ds(theirs, half_rows)], 5, 0)

    def sent(copy, remote_copy):
        if remote_copy:
            copy.wait_send()

    each_inbound(sent)

    def finish(chunk, carry):
        for kind in range(2):
            for scale in range(4):
                home, local, remote_copy = outbound(kind, scale, chunk)

                @pl.when(home != position)
                def _():
                    remote_copy.wait_send()

            for scale in range(4):

                @pl.when((position >= bounds[scale]) & (position < bounds[scale + 1]))
                def _():
                    for slot in range(SLOTS[scale]):
                        for half in range(2):
                            first = (slot * per_device + half * half_items + chunk * ITEMS) * LENGTHS[scale]
                            ref = (mixed_out, input_grad)[kind].at[
                                pl.ds(pl.multiple_of(first, 16), SIZES[scale])
                            ]
                            pltpu.make_async_copy(ref, ref, out_recv.at[kind, chunk, slot * 2 + half]).wait()

        return carry

    lax.fori_loop(0, chunks, finish, 0)

    @pl.when(position >= bounds[3])
    def _():
        for copy in pad_copies():
            copy.wait()


def body(groups, n_scale, *args):
    tokens = args[0]
    hidden = args[9].shape[2]
    per_device = tokens.shape[0] // L0
    chunks = per_device // 2 // ITEMS
    devices = groups * n_scale
    unit_rows = 16 * devices
    pack_rows = -(-NL * LAYER_ROWS // unit_rows) * unit_rows
    plane_size = groups // 8 * n_scale
    plane_rows = pack_rows // 2 // plane_size
    anywhere = pl.BlockSpec(memory_space=pl.ANY)
    vmem = pl.BlockSpec(memory_space=pltpu.VMEM)
    dma = pltpu.SemaphoreType.DMA
    scratch = [
        pltpu.VMEM((chunks, CHUNK, LANES), BF16),
        pltpu.VMEM((chunks, CHUNK, LANES), BF16),
        pltpu.VMEM((chunks, CHUNK, LANES), BF16),
        pltpu.VMEM((chunks, CHUNK, LANES), BF16),
        pltpu.VMEM((chunks, CHUNK, LANES), F32),
        pltpu.VMEM((CHUNK, LANES), F32),
        pltpu.VMEM((CHUNK, LANES), F32),
        pltpu.VMEM((CHUNK, LANES), F32),
        pltpu.VMEM((NL, CHUNK, LANES), F32),
        pltpu.VMEM((NL, CHUNK, LANES), F32),
        pltpu.VMEM((NL, CHUNK, LANES), BF16),
        pltpu.VMEM((NL, CHUNK, hidden), BF16),
        pltpu.VMEM((NL, CHUNK, hidden), BF16),
        pltpu.VMEM((NL, 7, 96, 2 * LANES), BF16),
        pltpu.VMEM((NL, 7, 48, 2 * LANES), BF16),
        pltpu.VMEM((NL, 7, 48, 2 * LANES), BF16),
        pltpu.VMEM((NL, 7, 48, 2 * LANES), BF16),
        pltpu.VMEM((NL, 7, 96, 2 * LANES), BF16),
        pltpu.VMEM((NL, 7, 96, 2 * LANES), BF16),
        pltpu.VMEM((NL, 3, 48, 96), BF16),
        pltpu.VMEM((NL, 3, 48, 48), BF16),
        pltpu.VMEM((NL, 3, 96, 48), BF16),
        pltpu.VMEM((NL, 3, 96, 96), BF16),
        pltpu.VMEM((NL, 3, 96, 48), BF16),
        pltpu.VMEM((NL, 3, 48, 48), BF16),
        pltpu.VMEM((NL, 3, 48, 96), BF16),
        pltpu.VMEM((NL, 3, 96, 96), BF16),
        pltpu.VMEM((3, 96, 96), BF16),
        pltpu.VMEM((3, 96, 96), BF16),
        pltpu.VMEM((48, 48), BF16),
        pltpu.VMEM((48, 48), BF16),
        pltpu.VMEM((NL, hidden, LANES), BF16),
        pltpu.VMEM((NL, LANES, hidden), BF16),
        pltpu.VMEM((NL, 3, 48, 96), F32),
        pltpu.VMEM((NL, 3, 48, 48), F32),
        pltpu.VMEM((NL, 3, 96, 48), F32),
        pltpu.VMEM((NL, 3, 96, 96), F32),
        pltpu.VMEM((NL, LANES, hidden), F32),
        pltpu.VMEM((NL, LANES, hidden), F32),
        pltpu.VMEM((NL, 8, hidden), F32),
        pltpu.VMEM((NL, 8, LANES), F32),
        pltpu.VMEM((NL, 8, LANES), F32),
        pltpu.VMEM((pack_rows, LANES), F32),
        pltpu.VMEM((pack_rows // 2, LANES), F32),
        pltpu.VMEM((pack_rows, LANES), BF16),
        pltpu.VMEM((plane_size, plane_rows, LANES), BF16),
        pltpu.VMEM((plane_rows, LANES), BF16),
        pltpu.VMEM((4, plane_rows // 4, LANES), BF16),
        dma((2, chunks, 8)),
        dma((2, chunks, 4)),
        dma((2, chunks, 4)),
        dma((2, chunks, 8)),
        dma((2,)),
        dma((6, max(plane_size, 4))),
        dma((6, max(plane_size, 4))),
    ]
    mixed_out, input_grad, packed = pl.pallas_call(
        functools.partial(kernel_body, groups, n_scale, per_device, pack_rows),
        out_shape=[
            jax.ShapeDtypeStruct(tokens.shape, BF16),
            jax.ShapeDtypeStruct(tokens.shape, BF16),
            jax.ShapeDtypeStruct((pack_rows, LANES), BF16),
        ],
        in_specs=[anywhere, anywhere] + [vmem] * 10,
        out_specs=[anywhere, anywhere, vmem],
        scratch_shapes=scratch,
        compiler_params=pltpu.CompilerParams(
            collective_id=0, has_side_effects=True, vmem_limit_bytes=56 << 20
        ),
    )(*args)
    layers = packed[: NL * LAYER_ROWS].reshape(NL, LAYER_ROWS, LANES).astype(F32)
    ffn_in_grad = jnp.concatenate(
        [layers[:, AT_FFN_IN : AT_FFN_IN + LANES], layers[:, AT_FFN_IN + LANES : AT_FFN_OUT]], 2
    )
    ffn_out_grad = jnp.swapaxes(
        jnp.concatenate(
            [layers[:, AT_FFN_OUT : AT_FFN_OUT + LANES], layers[:, AT_FFN_OUT + LANES : LAYER_ROWS]], 2
        ),
        1,
        2,
    )
    return (
        mixed_out,
        input_grad,
        layers[:, 0],
        layers[:, 1],
        layers[:, AT_SEASON_IN : AT_SEASON_IN + SEASON_ROWS, :L0],
        layers[:, AT_TREND_IN : AT_TREND_IN + SEASON_ROWS, SEASON_OUT_LANE : SEASON_OUT_LANE + L0 // 2],
        layers[:, AT_TREND_IN : AT_TREND_IN + TREND_ROWS, : L0 // 2],
        layers[:, AT_TREND_OUT : AT_TREND_OUT + TREND_ROWS, :L0],
        ffn_in_grad,
        layers[:, 2:4].reshape(NL, hidden),
        ffn_out_grad,
    )


def solution(mesh):
    rows = P(("scale", "dp"), None)
    return jax.shard_map(
        functools.partial(body, mesh.shape["dp"], mesh.shape["scale"]),
        mesh=mesh,
        in_specs=(rows, rows, P("scale", None)) + (P(),) * 9,
        out_specs=(rows, rows) + (P(),) * 9,
        check_vma=False,
    )
```

time: 1430 us -> 139 us (0.10)
  waiting for transfers between devices: 498 us -> 0 us
  matrix products: 337 us -> 0 us
  starting transfers between devices: 297 us -> 0 us
  other arithmetic: 139 us -> 1.51 us
  Pallas kernels: 0 us -> 124 us
  local copies, waits for them, and re-layouts: 130 us -> 12.5 us
  between operations: 18.1 us -> 0.71 us
    dot_general x88 -> x0, matrix products: 337 us -> none  [the longest x12 102 us: mix_forward(): jnp.einsum('ts,bsd->btd', second_weight, hidden, preferred_element_type=j...]
    ppermute x40 -> x0, starting transfers between devices: 297 us -> none  [shifted(): return lax.ppermute(array, axis, pairs)]
    psum x2 -> x0, waiting for transfers between devices: 276 us -> none  [body(): lax.psum((stacked[0], stacked[1], stacked[2], stacked[3], stacked[4], sta...]
    ppermute x40 -> x0, waiting for transfers between devices: 223 us -> none  [shifted(): return lax.ppermute(array, axis, pairs)]
    pallas_call x0 -> x1, Pallas kernels: none -> 124 us  [body(): pl.pallas_call(functools.partial(kernel_body, groups, n_scale, per_device...]
    convert_element_type x19 -> x1, other arithmetic: 75 us -> 0.06 us  [body(): layers = packed[:NL * LAYER_ROWS].reshape(NL, LAYER_ROWS, LANES).astype(F32)]
    scatter-add x22 -> x0, local copies, waits for them, and re-layouts: 32.1 us -> none  [the longest x6 9.86 us: body(): trend_in_grad = trend_in_grad.at[row_start:row_start + first_weight.shape...]
    gather x1 -> x0, local copies, waits for them, and re-layouts: 27.8 us -> none  [row_weights(): jnp.take(item_mask[0], item_global)]
  transfers between devices with their start and end apart: 42 -> 0, of which waited for: 21 -> 0; matrix products, arithmetic and copies ran while one was open for 22% -> 0% of each run, Pallas kernels for 0% -> 0%
where the time goes in v1:
time: 139 us
  Pallas kernels  124 us (89%)
  local copies, waits for them, and re-layouts  12.5 us (9%)
  other arithmetic  1.51 us (1%)
    pallas_call x1, Pallas kernels, body(): pl.pallas_call(functools.partial(kernel_body, groups, n_scale, per_device...  124 us
    unnamed x16, local copies, waits for them, and re-layouts  10 us

profile of v1, /device:TPU:0, one launch (start us, length us, event | category | flops | bytes accessed | tf_op | source)
XLA Modules:
  0.0 138.8 jit_solution(2428785019780468518)
XLA Ops:
  0.6 1.5 %copy.25.trend_in = bf16[2,168,48]{2,1,0:T(8,128)(2,1)} copy(bf16[2,168,48]{1,2,0:T(8,128)(2,1)} %param.19) | data formatting | bytes 64512 | tf_op args[7]
  2.2 1.4 %copy.23.season_in = bf16[2,84,96]{2,1,0:T(8,128)(2,1)} copy(bf16[2,84,96]{2,0,1:T(2,128)(2,1)} %param.17) | data formatting | bytes 64512 | tf_op args[5]
  3.6 1.5 %copy.24.season_out = bf16[2,84,48]{2,1,0:T(8,128)(2,1)} copy(bf16[2,84,48]{1,2,0:T(8,128)(2,1)} %param.18) | data formatting | bytes 32256 | tf_op args[6]
  5.1 124.1 %shard_map.203 = (bf16[4608,128]{1,0:T(8,128)(2,1)}, bf16[4608,128]{1,0:T(8,128)(2,1)}, bf16[2048,128]{1,0:T(8,128)(2,1)}) custom-call(bf16[4608,128]{1,0:T(8,128)(2,1)} %tokens.1, bf16[4608,128]{1,0:T(8,128)(2,1)} %cotangent.1, s32[1,384]{1,0:T(1,128)} %item_mask.1, f32[2,128]{1,0:T(2,128)} %ln_gain.1, f32[2,128]{1,0:T(2,128)} %ln_bias.1, ...), custom_call_target="tpu_custom_call" | custom-call | tf_op jit(solution)/shard_map/pallas_call | solution.py:848
  129.2 1.1 slice.36
  130.3 0.1 copy.31
  130.4 0.1 copy.32
  130.5 0.7 maximum_bitcast_fusion
  131.2 0.7 pad_maximum_fusion
  131.9 0.6 fusion.1
  132.5 0.1 convert.1
  132.6 0.0 copy-start.1
  132.6 0.6 copy.35
  133.2 0.8 copy.30
  133.9 0.7 copy.28
  134.6 0.7 slice.53
  135.3 0.1 slice.51
  135.4 0.7 copy.29
  136.1 0.0 copy-done.1
  136.1 0.0 copy-start
  136.1 1.0 copy.38
  137.1 0.7 copy-done
  137.8 1.0 copy.39
  (4 shorter events, 0.1 us)
Async XLA Ops:
  132.6 3.5 %copy-start.1 = (bf16[4608,128]{1,0:T(8,128)(2,1)S(1)}, bf16[4608,128]{1,0:T(8,128)(2,1)}, u32[]{:S(2)}) copy-start(bf16[4608,128]{1,0:T(8,128)(2,1)} %get-tuple-element.45) | copy-start | bytes 3538948
  136.1 1.7 %copy-start = (bf16[4608,128]{1,0:T(8,128)(2,1)S(1)}, bf16[4608,128]{1,0:T(8,128)(2,1)}, u32[]{:S(2)}) copy-start(bf16[4608,128]{1,0:T(8,128)(2,1)} %get-tuple-element.46) | copy-start | bytes 3538948

commit v2 on v1

v2 whole, which is shorter than its diff:
```python
import functools

import jax
import jax.numpy as jnp
from jax import lax
from jax.experimental import pallas as pl
from jax.experimental.pallas import tpu as pltpu
from jax.sharding import PartitionSpec as P

L0 = 96
KERNEL = 25
NL = 2
SEASON_ROWS = 84
TREND_ROWS = 168
EPS = 1e-05
LANES = 128
ITEMS = 8
PAIR = 4
MESH = pl.DeviceIdType.MESH
F32 = jnp.float32
BF16 = jnp.bfloat16

LENGTHS = [L0 >> i for i in range(4)]
SIZES = [ITEMS * n for n in LENGTHS]
STARTS = [sum(SIZES[:i]) for i in range(4)]
CHUNK = sum(SIZES)
SLOTS = [1, 2, 4, 4]
SELF = [(0, 0), (0, 1), (1, 1), (3, 1)]
TILE = 480
SLABS = [(0, 192, 2), (1, 192, 1), (2, 96, 1), (3, 48, 1)]
UNITS = {1: (0, 1), 2: (2,), 3: (3,)}
WEIGHT_COUNT = {1: 2, 2: 4, 3: 4}
GRAD_COUNT = {1: 1, 2: 2, 3: 4}
DUE_FAR = {
    ("forward", 2): [(0, 0), (1, 0), (0, 1), (1, 1)],
    ("scattered", 0): [(0, 2)],
    ("gathered", 0): [(1, 2)],
}
DUE_NEAR = {
    ("forward", 0): [(0, 0)],
    ("backward", 0): [(1, 0)],
    ("forward", 1): [(0, 1)],
    ("backward", 1): [(1, 1)],
    ("scattered", 0): [(0, 2)],
    ("gathered", 0): [(1, 2)],
}

AT_SEASON_IN = 8
AT_TREND_IN = AT_SEASON_IN + NL * SEASON_ROWS
AT_SEASON_OUT = AT_TREND_IN + NL * L0
AT_TREND_OUT = AT_SEASON_OUT + NL * L0 // 2
AT_FFN_IN = AT_TREND_OUT + NL * TREND_ROWS
AT_FFN_OUT = AT_FFN_IN + NL * 2 * LANES
USED_ROWS = AT_FFN_OUT + NL * 2 * LANES
PIECES = 4


def dot(a, b):
    return jnp.dot(a, b, preferred_element_type=F32)


def dot_nt(a, b):
    return lax.dot_general(a, b, (((1,), (1,)), ((), ())), preferred_element_type=F32)


def dot_tn(a, b):
    return lax.dot_general(a, b, (((0,), (0,)), ((), ())), preferred_element_type=F32)


def gelu_parts(v):
    cumulative = 0.5 * (1.0 + lax.erf(v * 0.7071067811865476))
    density = jnp.exp(-0.5 * (v * v)) * 0.3989422804014327
    return v * cumulative, cumulative + v * density


def iota(shape, dim):
    return lax.broadcasted_iota(jnp.int32, shape, dim)


def selection(rows, columns, count, length, base, turned=False, stride=1):
    shape = (columns, rows) if turned else (rows, columns)
    r = iota(shape, 1 if turned else 0)
    c = iota(shape, 0 if turned else 1)
    found = jnp.zeros(shape, jnp.bool_)
    for k in range(count):
        near = c == (r - k * length) * stride + base
        found = found | (near & (r >= k * length) & (r < (k + 1) * length))
    return found.astype(F32)


def block_mask(count, height, width, turned=False):
    shape = (count * width, count * height) if turned else (count * height, count * width)
    r = iota(shape, 1 if turned else 0)
    c = iota(shape, 0 if turned else 1)
    found = jnp.zeros(shape, jnp.bool_)
    for k in range(count):
        found = found | (
            (r >= k * height) & (r < (k + 1) * height) & (c >= k * width) & (c < (k + 1) * width)
        )
    return found.astype(F32)


def moving_counts(count, length, turned):
    size = count * length
    t = iota((size, size), 1 if turned else 0)
    u = iota((size, size), 0 if turned else 1)
    total = jnp.zeros((size, size), F32)
    half = (KERNEL - 1) // 2
    for k in range(count):
        low, high = k * length, (k + 1) * length - 1
        inside = (t >= low) & (t <= high) & (u >= low) & (u <= high)
        near = (jnp.abs(t - u) <= half).astype(F32)
        first = jnp.where(u == low, jnp.maximum(half - (t - low), 0), 0).astype(F32)
        last = jnp.where(u == high, jnp.maximum(half - (high - t), 0), 0).astype(F32)
        total = total + jnp.where(inside, near + first + last, 0.0)
    return total


def beside(value, height):
    return jnp.concatenate([value[k : k + height] for k in range(0, value.shape[0], height)], 1)


def drive(threads):
    active = list(threads)
    while active:
        rest = []
        for thread in active:
            if next(thread, None) is not None:
                rest.append(thread)
        active = rest


def fold_rows(value):
    return jnp.sum(value.reshape(-1, 8, value.shape[-1]), 0)


def group_of(groups, scale, slot, position):
    bounds = [0, groups // 2, 3 * groups // 4, 7 * groups // 8]
    offsets = [0, groups // 4, groups // 8, 3 * groups // 8]
    return position - bounds[scale] + offsets[slot]


def home_of(groups, scale, group):
    if scale == 0:
        return group, 0
    if scale == 1:
        return groups // 2 + lax.rem(group, groups // 4), lax.div(group, groups // 4)
    part = lax.div(group, groups // 8)
    slot = jnp.where(part == 1, 2, jnp.where(part == 2, 1, part))
    first = 3 * groups // 4 if scale == 2 else 7 * groups // 8
    return first + lax.rem(group, groups // 8), slot


def kernel_body(
    groups,
    n_scale,
    per_device,
    pack_rows,
    tokens,
    cotangent,
    item_mask_hbm,
    ln_gain_hbm,
    ln_bias_hbm,
    season_in_hbm,
    season_out_hbm,
    trend_in_hbm,
    trend_out_hbm,
    ffn_in_hbm,
    ffn_bias_hbm,
    ffn_out_hbm,
    mixed_out,
    input_grad,
    packed_out,
    item_mask,
    ln_gain,
    ln_bias,
    season_in,
    season_out,
    trend_in,
    trend_out,
    ffn_in,
    ffn_bias,
    ffn_out,
    param_sem,
    tok_buf,
    cot_buf,
    out_buf,
    grad_buf,
    live,
    field,
    grad,
    df_keep,
    da_keep,
    unit,
    inverse,
    z_keep,
    hidden,
    slope,
    season_src,
    trend_src,
    season_hid,
    season_slope,
    trend_hid,
    trend_slope,
    sa,
    sb,
    ta,
    tb,
    sa_t,
    sb_t,
    ta_t,
    tb_t,
    moving,
    moving_t,
    win_t,
    wout_t,
    d_sa,
    d_sb,
    d_ta,
    d_tb,
    d_win,
    d_wout,
    d_bias,
    d_gain,
    d_off,
    pack,
    half_in,
    half_bf,
    plane_in,
    plane_bf,
    depth_in,
    relay_buf,
    relay_send,
    relay_recv,
    in_send,
    in_recv,
    out_send,
    out_recv,
    ar_send,
    ar_recv,
):
    scale_index = lax.axis_index("scale")
    position = lax.axis_index("dp")
    worker_group = lax.rem(position, groups // 2)
    worker_half = lax.div(position, groups // 2)
    half_items = per_device // 2
    chunks = half_items // ITEMS
    bounds = [0, groups // 2, 3 * groups // 4, 7 * groups // 8, groups]

    params = [
        pltpu.make_async_copy(source, target, param_sem.at[k])
        for k, (source, target) in enumerate(
            (
                (item_mask_hbm, item_mask),
                (ln_gain_hbm, ln_gain),
                (ln_bias_hbm, ln_bias),
                (season_in_hbm, season_in),
                (season_out_hbm, season_out),
                (trend_in_hbm, trend_in),
                (trend_out_hbm, trend_out),
                (ffn_in_hbm, ffn_in),
                (ffn_bias_hbm, ffn_bias),
                (ffn_out_hbm, ffn_out),
            )
        )
    ]

    barrier = pltpu.get_barrier_semaphore()

    plane_dp = groups // 8
    plane_size = plane_dp * n_scale
    core = lax.rem(position, 2)
    place_dp = lax.rem(lax.div(position, 2), plane_dp)
    depth_index = lax.div(position, 2 * plane_dp)

    def greet(device):
        pl.semaphore_signal(barrier, inc=1, device_id=device, device_id_type=MESH)

    def greet_row(k, carry):
        greet((scale_index, lax.rem(position + k, groups)))
        return carry

    def greet_plane(k, carry):
        other = lax.rem(scale_index + 1 + lax.div(k, plane_dp), n_scale)
        greet((other, (depth_index * plane_dp + lax.rem(k, plane_dp)) * 2 + core))
        return carry

    lax.fori_loop(1, groups, greet_row, 0)
    lax.fori_loop(0, (n_scale - 1) * plane_dp, greet_plane, 0)
    pl.semaphore_wait(barrier, groups - 1 + (n_scale - 1) * plane_dp)

    def relayed(scale, slot, half):
        return half == 0 and ((scale == 2 and slot >= 2) or (scale == 3 and slot < 2))

    def inbound(kind, scale, slot, half, chunk):
        source = (tokens, cotangent)[kind]
        target = (tok_buf, cot_buf)[kind]
        length, size = LENGTHS[scale], SIZES[scale]
        first = (slot * per_device + half * half_items + chunk * ITEMS) * length
        src = source.at[pl.ds(pl.multiple_of(first, 16), size)]
        dst = target.at[chunk, pl.ds(STARTS[scale], size)]
        recv = in_recv.at[kind, chunk, scale]
        if (slot, half) == SELF[scale]:
            return pltpu.make_async_copy(src, dst, recv), False
        owner = half * (groups // 2) + group_of(groups, scale, slot, position)
        if relayed(scale, slot, half):
            owner = position + (groups // 8 if scale == 2 else -(groups // 8))
            dst = relay_buf.at[kind, chunk, slot % 2, pl.ds(0, size)]
            recv = relay_recv.at[kind, chunk, slot % 2]
        return (
            pltpu.make_async_remote_copy(
                src_ref=src,
                dst_ref=dst,
                send_sem=in_send.at[kind, chunk, slot * 2 + half],
                recv_sem=recv,
                device_id=(scale_index, owner),
                device_id_type=MESH,
            ),
            True,
        )

    def relay(kind, scale, slot, chunk):
        length, size = LENGTHS[scale], SIZES[scale]
        src = relay_buf.at[kind, chunk, slot % 2, pl.ds(0, size)]
        target = (tok_buf, cot_buf)[kind]
        partner = position + (groups // 8 if scale == 3 else -(groups // 8))
        return pltpu.make_async_remote_copy(
            src_ref=src,
            dst_ref=target.at[chunk, pl.ds(STARTS[scale], size)],
            send_sem=relay_send.at[kind, chunk, slot % 2],
            recv_sem=in_recv.at[kind, chunk, scale],
            device_id=(scale_index, group_of(groups, scale, slot, partner)),
            device_id_type=MESH,
        )

    def order(scale):
        moves = [(kind, slot, half) for kind in range(2) for slot in range(SLOTS[scale]) for half in (1, 0)]
        return sorted(moves, key=lambda move: (move[0], not relayed(scale, move[1], move[2])))

    def each_inbound(act, act_relay, low, high):
        for scale in range(4):

            @pl.when((position >= bounds[scale]) & (position < bounds[scale + 1]))
            def _():
                def one_chunk(chunk, carry):
                    for kind, slot, half in order(scale):
                        act(*inbound(kind, scale, slot, half, chunk))
                    if scale >= 2:
                        other = 5 - scale
                        for kind in range(2):
                            for slot in range(4):
                                if relayed(other, slot, 0):
                                    act_relay(relay(kind, other, slot, chunk), kind, slot, chunk)
                    return carry

                lax.fori_loop(low, high, one_chunk, 0)

    def pass_on(copy, kind, slot, chunk):
        size = SIZES[2 if slot >= 2 else 3]
        ref = relay_buf.at[kind, chunk, slot % 2, pl.ds(0, size)]
        pltpu.make_async_copy(ref, ref, relay_recv.at[kind, chunk, slot % 2]).wait()
        copy.start()

    def inbound_start(low, high):
        each_inbound(lambda copy, remote: copy.start(), pass_on, low, high)

    far = (position < groups // 4) | (position >= bounds[2])
    inbound_start(0, jnp.where(far, 1, chunks))
    for copy in params:
        copy.start()
    for copy in params:
        copy.wait()

    def inbound_wait(kind, chunk):
        target = (tok_buf, cot_buf)[kind]
        for scale in range(4):
            ref = target.at[chunk, pl.ds(STARTS[scale], SIZES[scale])]
            pltpu.make_async_copy(ref, ref, in_recv.at[kind, chunk, scale]).wait()

    def outbound(kind, scale, chunk):
        source = (out_buf, grad_buf)[kind]
        target = (mixed_out, input_grad)[kind]
        home, slot = home_of(groups, scale, worker_group)
        length, size = LENGTHS[scale], SIZES[scale]
        first = (slot * per_device + worker_half * half_items + chunk * ITEMS) * length
        src = source.at[chunk, pl.ds(STARTS[scale], size)]
        dst = target.at[pl.ds(pl.multiple_of(first, 16), size)]
        recv = out_recv.at[kind, chunk, slot * 2 + worker_half]
        local = pltpu.make_async_copy(src, dst, recv)
        remote = pltpu.make_async_remote_copy(
            src_ref=src,
            dst_ref=dst,
            send_sem=out_send.at[kind, chunk, scale],
            recv_sem=recv,
            device_id=(scale_index, home),
            device_id_type=MESH,
        )
        return home, local, remote

    def outbound_start(kind, chunk):
        for scale in range(4):
            home, local, remote = outbound(kind, scale, chunk)

            @pl.when(home == position)
            def _():
                local.start()

            @pl.when(home != position)
            def _():
                remote.start()

    def results_out(event, chunk):
        for is_far, due in ((True, DUE_FAR), (False, DUE_NEAR)):
            for at, sends in due.items():
                if at[0] == event:

                    @pl.when((far if is_far else jnp.logical_not(far)) & (chunk == at[1]))
                    def _():
                        for kind, done in sends:
                            outbound_start(kind, done)

    for layer in range(NL):
        for c in (1, 2, 3):
            count = WEIGHT_COUNT[c]
            fine, coarse = LENGTHS[c - 1], LENGTHS[c]
            at_season = L0 - fine
            at_trend = 2 * L0 - 2 * fine
            for whole, normal, turned, height, width, row, column, stride in (
                (season_in[...], sa, sa_t, coarse, fine, NL * at_season + layer, 0, NL),
                (season_out[layer], sb_t, sb, coarse, coarse, 0, at_season, 1),
                (trend_in[layer], ta_t, ta, coarse, fine, 0, at_trend, 1),
                (trend_out[layer], tb, tb_t, fine, fine, at_trend, 0, 1),
            ):
                rows = selection(count * height, whole.shape[0], count, height, row, stride=stride)
                columns = selection(count * width, whole.shape[1], count, width, column).astype(BF16)
                tall = dot(rows.astype(BF16), whole).astype(BF16)
                normal[layer, c - 1, : count * height, : count * width] = (
                    dot_nt(tall, columns) * block_mask(count, height, width)
                ).astype(BF16)
                turned[layer, c - 1, : count * width, : count * height] = (
                    dot_nt(columns, tall) * block_mask(count, height, width, True)
                ).astype(BF16)
        eye_in = selection(ffn_in.shape[2], ffn_in.shape[2], 1, ffn_in.shape[2], 0).astype(BF16)
        eye_out = selection(LANES, LANES, 1, LANES, 0).astype(BF16)
        win_t[layer] = dot_nt(eye_in, ffn_in[layer]).astype(BF16)
        wout_t[layer] = dot_nt(eye_out, ffn_out[layer]).astype(BF16)
    for scale, height, number in SLABS:
        for ref, is_turned in ((moving, False), (moving_t, True)):
            counts = moving_counts(height // LENGTHS[scale], LENGTHS[scale], is_turned)
            ref[scale, :height, :height] = counts.astype(BF16)
    mean_lanes = jnp.full((LANES, LANES), 1.0 / LANES, BF16)

    mask_rows = jnp.broadcast_to(item_mask[...].astype(F32), (LANES, item_mask.shape[1])).astype(BF16)
    first_item = worker_group * per_device + worker_half * half_items
    chosen = iota((32, item_mask.shape[1]), 1) == iota((32, item_mask.shape[1]), 0) + first_item
    item_live = dot_nt(chosen.astype(F32).astype(BF16), mask_rows).astype(BF16)
    for chunk in range(chunks):
        for i in range(4):
            place = (iota((SIZES[i], 32), 0).astype(F32) + 0.5) * (1.0 / LENGTHS[i])
            column = iota((SIZES[i], 32), 1).astype(F32) - float(chunk * ITEMS)
            one = ((place >= column) & (place < column + 1.0)).astype(F32).astype(BF16)
            live[chunk, STARTS[i] : STARTS[i] + SIZES[i], :] = dot(one, item_live)

    for total in (d_sa, d_sb, d_ta, d_tb, d_win, d_wout, d_bias, d_gain, d_off, pack):
        total[...] = jnp.zeros(total.shape, F32)

    taps = 1.0 / KERNEL

    def matrix(ref, layer, c, rows, columns):
        return ref[layer, c - 1, :rows, :columns]

    def sides(scale, height, j):
        half = SIZES[scale] // 2
        return [STARTS[scale] + side * half + j * height for side in range(2)]

    def forward(layer, chunk, found):
        gain = ln_gain[layer : layer + 1, :]
        offset = ln_bias[layer : layer + 1, :]
        offset_pair = jnp.concatenate([offset, offset], 1)
        bias = ffn_bias[layer : layer + 1, :]

        def rows_of(start, height):
            if layer == 0:
                return tok_buf[chunk, start : start + height, :].astype(F32)
            return field[start : start + height, :]

        def norm(scale, height, j):
            while layer > 0 and ("y", layer - 1, scale, j) not in found:
                yield 1
            parts = []
            for start in sides(scale, height, j):
                x = rows_of(start, height)
                centered = x - jnp.mean(x, -1, keepdims=True)
                yield 1
                inv = lax.rsqrt(dot((centered * centered).astype(BF16), mean_lanes) + EPS)
                n = centered * inv
                unit[layer, start : start + height, :] = n
                inverse[layer, start : start + height, :] = inv
                parts.append(n * gain)
                yield 1
            both = jnp.concatenate(parts, 1)
            average = dot(moving[scale, :height, :height], both.astype(BF16)) * taps
            found["n", layer, scale, j] = both + offset_pair
            found["s", layer, scale, j] = both - average
            found["t", layer, scale, j] = average + offset_pair

        def mixed(source, first, second, kept, hid, slp, u, layer_at, c, fine_to_coarse):
            a = source.astype(BF16)
            rows_in = a.shape[0]
            rows_out = rows_in // 2 if fine_to_coarse else rows_in * 2
            kept[layer_at, u, :rows_in, :] = a
            p = dot(matrix(first, layer_at, c, rows_out, rows_in), a)
            yield None
            h, slope_value = gelu_parts(p)
            h = h.astype(BF16)
            hid[layer_at, u, :rows_out, :] = h
            slp[layer_at, u, :rows_out, :] = slope_value.astype(BF16)
            yield None
            yield dot(matrix(second, layer_at, c, rows_out, rows_out), h)

        def season(c):
            results = []
            for j, u in enumerate(UNITS[c]):
                while ("S", layer, c - 1, j) not in found and not (
                    c == 1 and ("s", layer, 0, j) in found
                ):
                    yield 1
                source = found["s", layer, 0, j] if c == 1 else found["S", layer, c - 1, j]
                for value in mixed(
                    source, sa, sb, season_src, season_hid, season_slope, u, layer, c, True
                ):
                    if value is None:
                        yield 1
                    else:
                        results.append(value)
            mix = results[0] if len(results) == 1 else jnp.concatenate(results, 0)
            found["sm", layer, c, 0] = mix
            while ("s", layer, c, 0) not in found:
                yield 1
            found["S", layer, c, 0] = found["s", layer, c, 0] + mix

        def trend(c):
            while ("t" if c == 3 else "T", layer, c, 0) not in found:
                yield 1
            source = found["t" if c == 3 else "T", layer, c, 0]
            for j, u in enumerate(UNITS[c]):
                part = source[96 * j : 96 * (j + 1)] if c == 1 else source
                for value in mixed(part, ta, tb, trend_src, trend_hid, trend_slope, u, layer, c, False):
                    if value is None:
                        yield 1
                    else:
                        found["tm", layer, c - 1, j] = value
            if c > 1:
                while ("t", layer, c - 1, 0) not in found:
                    yield 1
                found["T", layer, c - 1, 0] = found["t", layer, c - 1, 0] + found["tm", layer, c - 1, 0]

        def ffn(scale, height, j):
            needed = [("n", layer, scale, j)]
            if scale > 0:
                needed.append(("sm", layer, scale, j))
            if scale < 3:
                needed.append(("tm", layer, scale, j))
            while not all(key in found for key in needed):
                yield 1
            value = found[needed[0]]
            for key in needed[1:]:
                value = value + found[key]
            value = value.astype(BF16)
            starts = sides(scale, height, j)
            halves = [value[:, :LANES], value[:, LANES:]]
            for start, z in zip(starts, halves):
                z_keep[layer, start : start + height, :] = z
            a = dot(jnp.concatenate(halves, 0), ffn_in[layer]) + bias
            yield 1
            h, slope_value = gelu_parts(a)
            h = h.astype(BF16)
            slope_value = slope_value.astype(BF16)
            for k, start in enumerate(starts):
                hidden[layer, start : start + height, :] = h[k * height : (k + 1) * height]
                slope[layer, start : start + height, :] = slope_value[k * height : (k + 1) * height]
            yield 1
            f = dot(h, ffn_out[layer])
            yield 1
            for k, start in enumerate(starts):
                y = rows_of(start, height) + live[chunk, start : start + height, :] * f[
                    k * height : (k + 1) * height
                ]
                if layer == NL - 1:
                    out_buf[chunk, start : start + height, :] = y.astype(BF16)
                else:
                    field[start : start + height, :] = y
            found["y", layer, scale, j] = True

        for scale, height, number in reversed(SLABS):
            for j in range(number):
                yield norm(scale, height, j)
        for c in (3, 2, 1):
            yield trend(c)
        for c in (1, 2, 3):
            yield season(c)
        for scale, height, number in (SLABS[1], SLABS[2], SLABS[0], SLABS[3]):
            for j in range(number):
                yield ffn(scale, height, j)

    def backward(layer, chunk, found):
        gain = ln_gain[layer : layer + 1, :]

        def rows_of(start, height):
            if layer == NL - 1:
                return cot_buf[chunk, start : start + height, :].astype(F32)
            return grad[start : start + height, :]

        def ffn(scale, height, j):
            while layer < NL - 1 and ("x", layer + 1, scale, j) not in found:
                yield 1
            starts = sides(scale, height, j)
            parts = []
            for start in starts:
                df = (live[chunk, start : start + height, :] * rows_of(start, height)).astype(BF16)
                df_keep[start : start + height, :] = df
                parts.append(df)
            dh = dot(jnp.concatenate(parts, 0), wout_t[layer])
            yield 1
            parts = []
            for k, start in enumerate(starts):
                da = dh[k * height : (k + 1) * height] * slope[layer, start : start + height, :].astype(F32)
                d_bias[layer] += fold_rows(da)
                da = da.astype(BF16)
                da_keep[start : start + height, :] = da
                parts.append(da)
            yield 1
            dz = dot(jnp.concatenate(parts, 0), win_t[layer])
            found["dz", layer, scale, j] = jnp.concatenate([dz[:height], dz[height:]], 1)

        def weight_grads():
            while not all(("dz", layer, scale, j) in found for scale, _, number in SLABS for j in range(number)):
                yield 1
            for t in range(0, CHUNK, TILE):
                d_win[layer] += dot_tn(z_keep[layer, t : t + TILE, :], da_keep[t : t + TILE, :])
                yield 1
                d_wout[layer] += dot_tn(df_keep[t : t + TILE, :], hidden[layer, t : t + TILE, :])
                yield 1

        def mixed(g, first_t, second_t, slp, u, c, fine_to_coarse):
            rows = g.shape[0]
            rows_out = rows * 2 if fine_to_coarse else rows // 2
            dh = dot(matrix(second_t, layer, c, rows, rows), g)
            yield None
            dp = (dh * slp[layer, u, :rows, :].astype(F32)).astype(BF16)
            yield dp
            yield dot(matrix(first_t, layer, c, rows_out, rows), dp)

        def trend(c):
            results, gs, dps = [], [], []
            for j, u in enumerate(UNITS[c]):
                key = ("dz", layer, 0, j) if c == 1 else ("dT", layer, c - 1, 0)
                while key not in found:
                    yield 1
                g = found[key].astype(BF16)
                gs.append(beside(g, 96))
                steps = []
                for value in mixed(g, ta_t, tb_t, trend_slope, u, c, False):
                    if value is not None:
                        steps.append(value)
                    yield 1
                dps.append(beside(steps[0], 96))
                results.append(steps[1])
            total = results[0] if len(results) == 1 else jnp.concatenate(results, 0)
            found["gT", layer, c, 0] = total
            while ("dz", layer, c, 0) not in found:
                yield 1
            found["dT", layer, c, 0] = found["dz", layer, c, 0] + total
            rows = 48 if c == 3 else 96
            kept = [beside(trend_hid[layer, u, : 2 * rows, :], 96) for u in UNITS[c]]
            d_tb[layer, c - 1] += dot_nt(jnp.concatenate(gs, 1), jnp.concatenate(kept, 1))
            yield 1
            kept = [beside(trend_src[layer, u, :rows, :], 48) for u in UNITS[c]]
            d_ta[layer, c - 1] += dot_nt(jnp.concatenate(kept, 1), jnp.concatenate(dps, 1))

        def season(c):
            key = ("dz", layer, 3, 0) if c == 3 else ("dS", layer, c, 0)
            while key not in found:
                yield 1
            gs, dps = [], []
            for j, u in enumerate(UNITS[c]):
                g = found[key].astype(BF16)
                if c == 1:
                    g = g[96 * j : 96 * (j + 1)]
                gs.append(beside(g, 48))
                steps = []
                for value in mixed(g, sa_t, sb_t, season_slope, u, c, True):
                    if value is not None:
                        steps.append(value)
                    yield 1
                dps.append(beside(steps[0], 48))
                found["gS", layer, c - 1, j] = steps[1]
            if c > 1:
                while ("dz", layer, c - 1, 0) not in found:
                    yield 1
                found["dS", layer, c - 1, 0] = found["dz", layer, c - 1, 0] + found["gS", layer, c - 1, 0]
            rows = 48 if c == 3 else 96
            kept = [beside(season_hid[layer, u, :rows, :], 48) for u in UNITS[c]]
            d_sb[layer, c - 1] += dot_nt(jnp.concatenate(kept, 1), jnp.concatenate(gs, 1))
            yield 1
            kept = [beside(season_src[layer, u, : 2 * rows, :], 96) for u in UNITS[c]]
            d_sa[layer, c - 1] += dot_nt(jnp.concatenate(dps, 1), jnp.concatenate(kept, 1))

        def norm(scale, height, j):
            needed = [("dz", layer, scale, j)]
            if scale < 3:
                needed.append(("gS", layer, scale, j))
            if scale > 0:
                needed.append(("gT", layer, scale, j))
            while not all(key in found for key in needed):
                yield 1
            value = found[needed[0]]
            if scale == 0:
                moved = -found[needed[1]]
                value = value + found[needed[1]]
            elif scale == 3:
                moved = found[needed[1]]
            else:
                moved = found[needed[2]] - found[needed[1]]
                value = value + found[needed[1]]
            value = value + dot(moving_t[scale, :height, :height], moved.astype(BF16)) * taps
            yield 1
            for side, start in enumerate(sides(scale, height, j)):
                d = value[:, side * LANES : (side + 1) * LANES]
                n = unit[layer, start : start + height, :]
                dn = d * n
                d_gain[layer] += fold_rows(dn)
                d_off[layer] += fold_rows(d)
                q = d * gain
                qn = dn * gain
                mean_q = dot(q.astype(BF16), mean_lanes)
                mean_qn = dot(qn.astype(BF16), mean_lanes)
                yield 1
                x = rows_of(start, height) + inverse[layer, start : start + height, :] * (
                    q - mean_q - n * mean_qn
                )
                if layer == 0:
                    grad_buf[chunk, start : start + height, :] = x.astype(BF16)
                else:
                    grad[start : start + height, :] = x
                yield 1
            found["x", layer, scale, j] = True

        for scale, height, number in (SLABS[0], SLABS[3], SLABS[1], SLABS[2]):
            for j in range(number):
                yield ffn(scale, height, j)
        for c in (1, 2, 3):
            yield trend(c)
        for c in (3, 2, 1):
            yield season(c)
        for scale, height, number in reversed(SLABS):
            for j in range(number):
                yield norm(scale, height, j)
        yield weight_grads()

    def one_chunk(chunk, carry):
        inbound_wait(0, chunk)
        found = {}
        drive([thread for layer in range(NL) for thread in forward(layer, chunk, found)])
        inbound_start(chunk + 1, jnp.where(far & (chunk < chunks - 1), chunk + 2, chunk + 1))

        results_out("forward", chunk)
        inbound_wait(1, chunk)
        found = {}
        drive([thread for layer in reversed(range(NL)) for thread in backward(layer, chunk, found)])
        results_out("backward", chunk)
        return carry

    lax.fori_loop(0, chunks, one_chunk, 0)

    for layer in range(NL):
        parts = [None] * 4
        for c in (1, 2, 3):
            count = GRAD_COUNT[c]
            fine, coarse = LENGTHS[c - 1], LENGTHS[c]
            at_season = L0 - fine
            at_trend = 2 * L0 - 2 * fine
            for k, (value, height, width, rows, row, lanes, lane, stride) in enumerate(
                (
                    (d_sa, coarse, fine, NL * SEASON_ROWS, NL * at_season + layer, LANES, 0, NL),
                    (d_sb, coarse, coarse, L0 // 2, 0, LANES, at_season, 1),
                    (d_ta, coarse, fine, L0 // 2, 0, 2 * LANES, at_trend, 1),
                    (d_tb, fine, fine, TREND_ROWS, at_trend, LANES, 0, 1),
                )
            ):
                masked = (value[layer, c - 1] * block_mask(count, height, width)).astype(BF16)
                place = selection(count * height, rows, count, height, row, True, stride).astype(BF16)
                lay = selection(count * width, lanes, count, width, lane).astype(BF16)
                found = dot(dot(place, masked).astype(BF16), lay)
                parts[k] = found if parts[k] is None else parts[k] + found
        pack[layer : layer + 1, :] = jnp.sum(d_gain[layer], 0, keepdims=True)
        pack[NL + layer : NL + layer + 1, :] = jnp.sum(d_off[layer], 0, keepdims=True)
        bias_sum = jnp.sum(d_bias[layer], 0, keepdims=True)
        pack[AT_SEASON_IN : AT_SEASON_IN + NL * SEASON_ROWS, :] += parts[0]
        row = AT_SEASON_OUT + layer * L0 // 2
        pack[row : row + L0 // 2, :] = parts[1]
        row = AT_TREND_OUT + layer * TREND_ROWS
        pack[row : row + TREND_ROWS, :] = parts[3]
        for side in range(2):
            lanes = slice(side * LANES, (side + 1) * LANES)
            row = 2 * NL + 2 * layer + side
            pack[row : row + 1, :] = bias_sum[:, lanes]
            row = AT_TREND_IN + layer * L0 + side * L0 // 2
            pack[row : row + L0 // 2, :] = parts[2][:, lanes]
            row = AT_FFN_IN + (2 * layer + side) * LANES
            pack[row : row + LANES, :] = d_win[layer, :, lanes]
            row = AT_FFN_OUT + (2 * layer + side) * LANES
            pack[row : row + LANES, :] = d_wout[layer, :, lanes].T

    plane_index = scale_index * plane_dp + place_dp
    half_rows = pack_rows // 2
    plane_rows = half_rows // plane_size
    depth_rows = plane_rows // 4

    def core_id():
        return (scale_index, position + 1 - 2 * core)

    def plane_id(index):
        return (
            lax.div(index, plane_dp),
            depth_index * (2 * plane_dp) + lax.rem(index, plane_dp) * 2 + core,
        )

    def depth_id(index):
        return (scale_index, index * (2 * plane_dp) + place_dp * 2 + core)

    def remote(src, dst, stage, slot_out, slot_in, device):
        return pltpu.make_async_remote_copy(
            src_ref=src,
            dst_ref=dst,
            send_sem=ar_send.at[stage, slot_out],
            recv_sem=ar_recv.at[stage, slot_in],
            device_id=device,
            device_id_type=MESH,
        )

    def arrived(ref, stage, slot):
        pltpu.make_async_copy(ref, ref, ar_recv.at[stage, slot]).wait()

    mine = pl.multiple_of(core * half_rows, 16)
    theirs = pl.multiple_of((1 - core) * half_rows, 16)
    first_copy = remote(pack.at[pl.ds(theirs, half_rows)], half_in, 0, 0, 0, core_id())
    first_copy.start()
    first_copy.wait_send()
    arrived(half_in, 0, 0)
    half_bf[pl.ds(mine, half_rows)] = (pack[pl.ds(mine, half_rows)] + half_in[...]).astype(BF16)

    def plane_piece(index):
        return pl.ds(pl.multiple_of(mine + index * plane_rows, 16), plane_rows)

    def plane_round(stage, source_of, target_of, act):
        def one(k, carry):
            other = lax.rem(plane_index + k, plane_size)
            back = lax.rem(plane_index + plane_size - k, plane_size)
            act(other, back, k)
            return carry

        lax.fori_loop(1, plane_size, one, 0)

    def plane_scatter(other, back, k):
        remote(half_bf.at[plane_piece(other)], plane_in.at[k], 1, k, k, plane_id(other)).start()

    plane_round(1, None, None, plane_scatter)
    plane_sum = pack[plane_piece(plane_index)] + half_in[
        pl.ds(pl.multiple_of(plane_index * plane_rows, 16), plane_rows)
    ]

    def plane_wait(k, carry):
        remote(half_bf.at[plane_piece(0)], plane_in.at[k], 1, k, k, core_id()).wait_send()
        arrived(plane_in.at[k], 1, k)
        return carry

    lax.fori_loop(1, plane_size, plane_wait, 0)
    for k in range(1, plane_size):
        plane_sum = plane_sum + plane_in[k].astype(F32)
    plane_bf[...] = plane_sum.astype(BF16)

    def depth_piece(index):
        return pl.ds(pl.multiple_of(index * depth_rows, 16), depth_rows)

    for k in range(1, 4):
        other = lax.rem(depth_index + k, 4)
        remote(plane_bf.at[depth_piece(other)], depth_in.at[k], 2, k, k, depth_id(other)).start()
    results_out("scattered", 0)
    for k in range(1, 4):
        remote(plane_bf.at[depth_piece(0)], depth_in.at[k], 2, k, k, core_id()).wait_send()
        arrived(depth_in.at[k], 2, k)
    total = plane_bf[depth_piece(depth_index)].astype(F32)
    for k in range(1, 4):
        total = total + depth_in[k].astype(F32)

    def final_piece(plane, depth):
        return pl.ds(pl.multiple_of(mine + plane * plane_rows + depth * depth_rows, 16), depth_rows)

    own = final_piece(plane_index, depth_index)
    packed_out[own] = total.astype(BF16)
    for k in range(1, 4):
        other = lax.rem(depth_index + k, 4)
        remote(packed_out.at[own], packed_out.at[own], 3, k, k, depth_id(other)).start()
    results_out("gathered", 0)
    for k in range(1, 4):
        back = lax.rem(depth_index + 4 - k, 4)
        remote(packed_out.at[own], packed_out.at[own], 3, k, k, core_id()).wait_send()
        arrived(packed_out.at[final_piece(plane_index, back)], 3, k)
    own_plane = plane_piece(plane_index)

    def plane_gather(other, back, k):
        remote(packed_out.at[own_plane], packed_out.at[own_plane], 4, k, k, plane_id(other)).start()

    plane_round(4, None, None, plane_gather)

    def plane_gathered(other, back, k):
        remote(packed_out.at[own_plane], packed_out.at[own_plane], 4, k, k, core_id()).wait_send()
        arrived(packed_out.at[plane_piece(back)], 4, k)

    plane_round(4, None, None, plane_gathered)
    own_half = pl.ds(mine, half_rows)
    last_copy = remote(packed_out.at[own_half], packed_out.at[own_half], 5, 0, 0, core_id())
    last_copy.start()
    last_copy.wait_send()
    arrived(packed_out.at[pl.ds(theirs, half_rows)], 5, 0)

    def sent(copy, remote_copy):
        if remote_copy:
            copy.wait_send()

    each_inbound(sent, lambda copy, kind, slot, chunk: copy.wait_send(), 0, chunks)

    def finish(chunk, carry):
        for kind in range(2):
            for scale in range(4):
                home, local, remote_copy = outbound(kind, scale, chunk)

                @pl.when(home != position)
                def _():
                    remote_copy.wait_send()

            for scale in range(4):

                @pl.when((position >= bounds[scale]) & (position < bounds[scale + 1]))
                def _():
                    for slot in range(SLOTS[scale]):
                        for half in range(2):
                            first = (slot * per_device + half * half_items + chunk * ITEMS) * LENGTHS[scale]
                            ref = (mixed_out, input_grad)[kind].at[
                                pl.ds(pl.multiple_of(first, 16), SIZES[scale])
                            ]
                            pltpu.make_async_copy(ref, ref, out_recv.at[kind, chunk, slot * 2 + half]).wait()

        return carry

    lax.fori_loop(0, chunks, finish, 0)


def unpack_body(
    groups,
    tokens,
    cotangent,
    mixed,
    grad,
    packed_hbm,
    mixed_out,
    input_grad,
    *refs,
):
    finals, (packed, staged, in_sem, out_sem, small_sem) = refs[:9], refs[18:]
    (
        gain_grad,
        bias_grad,
        season_in_grad,
        season_out_grad,
        trend_in_grad,
        trend_out_grad,
        ffn_in_grad,
        ffn_bias_grad,
        ffn_out_grad,
    ) = refs[9:18]
    packed_copy = pltpu.make_async_copy(packed_hbm, packed, small_sem.at[9])
    packed_copy.start()
    padded = lax.axis_index("dp") >= 7 * groups // 8
    size = tokens.shape[0] // PIECES
    for kind, (own, other) in enumerate(((mixed, tokens), (grad, cotangent))):
        for k in range(PIECES):
            rows = pl.ds(k * size, size)
            usual = pltpu.make_async_copy(own.at[rows], staged.at[kind, rows], in_sem.at[kind, k])
            if k < PIECES // 2:
                usual.start()
            else:
                rest = pltpu.make_async_copy(other.at[rows], staged.at[kind, rows], in_sem.at[kind, k])

                @pl.when(padded)
                def _():
                    rest.start()

                @pl.when(jnp.logical_not(padded))
                def _():
                    usual.start()

    def piece_out(kind, k):
        rows = pl.ds(k * size, size)
        target = (mixed_out, input_grad)[kind]
        return pltpu.make_async_copy(staged.at[kind, rows], target.at[rows], out_sem.at[kind, k])

    packed_copy.wait()
    top = packed[0:16, :].astype(F32)
    gain_grad[...] = top[0:NL]
    bias_grad[...] = top[NL : 2 * NL]
    for layer in range(NL):
        for side in range(2):
            lanes = slice(side * LANES, (side + 1) * LANES)
            row = 2 * NL + 2 * layer + side
            ffn_bias_grad[layer : layer + 1, lanes] = top[row : row + 1]
            row = AT_FFN_IN + (2 * layer + side) * LANES
            ffn_in_grad[layer, :, lanes] = packed[row : row + LANES, :].astype(F32)
            row = AT_FFN_OUT + (2 * layer + side) * LANES
            ffn_out_grad[layer, side * LANES : (side + 1) * LANES, :] = packed[row : row + LANES, :].astype(F32)
        row = AT_SEASON_OUT + layer * L0 // 2
        season_out_grad[layer] = packed[row : row + L0 // 2, :SEASON_ROWS].astype(F32)
        row = AT_TREND_IN + layer * L0
        trend_in_grad[layer, :, :LANES] = packed[row : row + L0 // 2, :].astype(F32)
        trend_in_grad[layer, :, LANES:] = packed[
            row + L0 // 2 : row + L0, : TREND_ROWS - LANES
        ].astype(F32)
        row = AT_TREND_OUT + layer * TREND_ROWS
        trend_out_grad[layer] = packed[row : row + TREND_ROWS, :L0].astype(F32)
    season_in_grad[...] = packed[AT_SEASON_IN : AT_SEASON_IN + NL * SEASON_ROWS, :L0].astype(F32)
    small = [
        pltpu.make_async_copy(source, target, small_sem.at[k])
        for k, (source, target) in enumerate(zip(refs[9:18], finals))
    ]
    for copy in small:
        copy.start()
    for kind in range(2):
        for k in range(PIECES):
            rows = pl.ds(k * size, size)
            pltpu.make_async_copy(mixed.at[rows], staged.at[kind, rows], in_sem.at[kind, k]).wait()
            piece_out(kind, k).start()
    for copy in small:
        copy.wait()
    for kind in range(2):
        for k in range(PIECES):
            piece_out(kind, k).wait()


def body(groups, n_scale, *args):
    tokens = args[0]
    hidden = args[9].shape[2]
    per_device = tokens.shape[0] // L0
    chunks = per_device // 2 // ITEMS
    devices = groups * n_scale
    unit_rows = 16 * devices
    pack_rows = -(-USED_ROWS // unit_rows) * unit_rows
    plane_size = groups // 8 * n_scale
    plane_rows = pack_rows // 2 // plane_size
    anywhere = pl.BlockSpec(memory_space=pl.ANY)
    vmem = pl.BlockSpec(memory_space=pltpu.VMEM)
    dma = pltpu.SemaphoreType.DMA
    turned = (
        args[:5]
        + (jnp.swapaxes(args[5], 0, 1).reshape(NL * SEASON_ROWS, L0),)
        + tuple(jnp.swapaxes(member, 1, 2) for member in args[6:8])
        + args[8:]
    )
    scratch = [pltpu.VMEM(member.shape, member.dtype) for member in turned[2:]]
    scratch += [
        dma((len(turned) - 2,)),
        pltpu.VMEM((chunks, CHUNK, LANES), BF16),
        pltpu.VMEM((chunks, CHUNK, LANES), BF16),
        pltpu.VMEM((chunks, CHUNK, LANES), BF16),
        pltpu.VMEM((chunks, CHUNK, LANES), BF16),
        pltpu.VMEM((chunks, CHUNK, LANES), F32),
        pltpu.VMEM((CHUNK, LANES), F32),
        pltpu.VMEM((CHUNK, LANES), F32),
        pltpu.VMEM((CHUNK, LANES), BF16),
        pltpu.VMEM((CHUNK, hidden), BF16),
        pltpu.VMEM((NL, CHUNK, LANES), F32),
        pltpu.VMEM((NL, CHUNK, LANES), F32),
        pltpu.VMEM((NL, CHUNK, LANES), BF16),
        pltpu.VMEM((NL, CHUNK, hidden), BF16),
        pltpu.VMEM((NL, CHUNK, hidden), BF16),
        pltpu.VMEM((NL, 4, 192, 2 * LANES), BF16),
        pltpu.VMEM((NL, 4, 96, 2 * LANES), BF16),
        pltpu.VMEM((NL, 4, 96, 2 * LANES), BF16),
        pltpu.VMEM((NL, 4, 96, 2 * LANES), BF16),
        pltpu.VMEM((NL, 4, 192, 2 * LANES), BF16),
        pltpu.VMEM((NL, 4, 192, 2 * LANES), BF16),
        pltpu.VMEM((NL, 3, 96, 192), BF16),
        pltpu.VMEM((NL, 3, 96, 96), BF16),
        pltpu.VMEM((NL, 3, 192, 96), BF16),
        pltpu.VMEM((NL, 3, 192, 192), BF16),
        pltpu.VMEM((NL, 3, 192, 96), BF16),
        pltpu.VMEM((NL, 3, 96, 96), BF16),
        pltpu.VMEM((NL, 3, 96, 192), BF16),
        pltpu.VMEM((NL, 3, 192, 192), BF16),
        pltpu.VMEM((4, 192, 192), BF16),
        pltpu.VMEM((4, 192, 192), BF16),
        pltpu.VMEM((NL, hidden, LANES), BF16),
        pltpu.VMEM((NL, LANES, hidden), BF16),
        pltpu.VMEM((NL, 3, 48, 96), F32),
        pltpu.VMEM((NL, 3, 48, 48), F32),
        pltpu.VMEM((NL, 3, 48, 96), F32),
        pltpu.VMEM((NL, 3, 96, 96), F32),
        pltpu.VMEM((NL, LANES, hidden), F32),
        pltpu.VMEM((NL, LANES, hidden), F32),
        pltpu.VMEM((NL, 8, hidden), F32),
        pltpu.VMEM((NL, 8, LANES), F32),
        pltpu.VMEM((NL, 8, LANES), F32),
        pltpu.VMEM((pack_rows, LANES), F32),
        pltpu.VMEM((pack_rows // 2, LANES), F32),
        pltpu.VMEM((pack_rows, LANES), BF16),
        pltpu.VMEM((plane_size, plane_rows, LANES), BF16),
        pltpu.VMEM((plane_rows, LANES), BF16),
        pltpu.VMEM((4, plane_rows // 4, LANES), BF16),
        pltpu.VMEM((2, chunks, 2, SIZES[2], LANES), BF16),
        dma((2, chunks, 2)),
        dma((2, chunks, 2)),
        dma((2, chunks, 8)),
        dma((2, chunks, 4)),
        dma((2, chunks, 4)),
        dma((2, chunks, 8)),
        dma((6, max(plane_size, 4))),
        dma((6, max(plane_size, 4))),
    ]
    mixed_out, input_grad, packed = pl.pallas_call(
        functools.partial(kernel_body, groups, n_scale, per_device, pack_rows),
        out_shape=[
            jax.ShapeDtypeStruct(tokens.shape, BF16),
            jax.ShapeDtypeStruct(tokens.shape, BF16),
            jax.ShapeDtypeStruct((pack_rows, LANES), BF16),
        ],
        in_specs=[anywhere] * len(turned),
        out_specs=[anywhere, anywhere, vmem],
        scratch_shapes=scratch,
        compiler_params=pltpu.CompilerParams(
            collective_id=0, has_side_effects=True, vmem_limit_bytes=58 << 20
        ),
    )(*turned)
    finals = [
        jax.ShapeDtypeStruct(shape, F32)
        for shape in (
            (NL, LANES),
            (NL, LANES),
            (NL * SEASON_ROWS, L0),
            (NL, L0 // 2, SEASON_ROWS),
            (NL, L0 // 2, TREND_ROWS),
            (NL, TREND_ROWS, L0),
            (NL, LANES, hidden),
            (NL, hidden),
            (NL, hidden, LANES),
        )
    ]
    outs = pl.pallas_call(
        functools.partial(unpack_body, groups),
        out_shape=[
            jax.ShapeDtypeStruct(tokens.shape, BF16),
            jax.ShapeDtypeStruct(tokens.shape, BF16),
            *finals,
        ],
        in_specs=[anywhere] * 5,
        out_specs=[anywhere] * 11,
        scratch_shapes=[pltpu.VMEM(member.shape, F32) for member in finals]
        + [
            pltpu.VMEM((pack_rows, LANES), BF16),
            pltpu.VMEM((2,) + tokens.shape, BF16),
            dma((2, PIECES)),
            dma((2, PIECES)),
            dma((len(finals) + 1,)),
        ],
        compiler_params=pltpu.CompilerParams(vmem_limit_bytes=58 << 20),
    )(tokens, args[1], mixed_out, input_grad, packed)
    return (
        *outs[:4],
        jnp.swapaxes(outs[4].reshape(SEASON_ROWS, NL, L0), 0, 1),
        jnp.swapaxes(outs[5], 1, 2),
        jnp.swapaxes(outs[6], 1, 2),
        *outs[7:],
    )


def solution(mesh):
    rows = P(("scale", "dp"), None)
    return jax.shard_map(
        functools.partial(body, mesh.shape["dp"], mesh.shape["scale"]),
        mesh=mesh,
        in_specs=(rows, rows, P("scale", None)) + (P(),) * 9,
        out_specs=(rows, rows) + (P(),) * 9,
        check_vma=False,
    )
```

time: 139 us -> 114 us (0.82)
  local copies, waits for them, and re-layouts: 12.5 us -> 0 us
  Pallas kernels: 124 us -> 113 us
  other arithmetic: 1.51 us -> 0 us
    pallas_call x1, Pallas kernels: 124 us -> 109 us  [body(): pl.pallas_call(functools.partial(kernel_body, groups, n_scale, per_device...]
    unnamed x16 -> x0, local copies, waits for them, and re-layouts: 10 us -> none
    pallas_call x0 -> x1, Pallas kernels: none -> 3.61 us  [body(): pl.pallas_call(functools.partial(unpack_body, groups), out_shape=[jax.Sha...]
    slice x7 -> x0, local copies, waits for them, and re-layouts: 2.45 us -> none  [the longest x1 1.06 us: body(): layers = packed[:NL * LAYER_ROWS].reshape(NL, LAYER_ROWS, LANES).astype(F32)]
where the time goes in v2:
time: 114 us; the launch traced here: 113 us
  Pallas kernels  113 us (99%)
    pallas_call x1, Pallas kernels, body(): pl.pallas_call(functools.partial(kernel_body, groups, n_scale, per_device...  109 us
    pallas_call x1, Pallas kernels, body(): pl.pallas_call(functools.partial(unpack_body, groups), out_shape=[jax.Sha...  3.61 us

profile of v2, /device:TPU:0, one launch (start us, length us, event | category | flops | bytes accessed | tf_op | source)
XLA Modules:
  0.0 113.3 jit_solution(4135857919032423086)
XLA Ops:
  0.6 108.9 %shard_map.203 = (bf16[4608,128]{1,0:T(8,128)(2,1)}, bf16[4608,128]{1,0:T(8,128)(2,1)}, bf16[2048,128]{1,0:T(8,128)(2,1)}) custom-call(bf16[4608,128]{1,0:T(8,128)(2,1)} %tokens.3, bf16[4608,128]{1,0:T(8,128)(2,1)} %cotangent.3, s32[1,384]{1,0:T(1,128)} %item_mask_hbm.1, f32[2,128]{1,0:T(2,128)} %ln_gain_hbm.1, f32[2,128]{1,0:T(2,128)} %ln_bias_hbm.1, ...), custom_call_target="tpu_custom_call" | custom-call | tf_op jit(solution)/shard_map/pallas_call | solution.py:1129
  109.6 3.6 %shard_map.204 = (bf16[4608,128]{1,0:T(8,128)(2,1)}, bf16[4608,128]{1,0:T(8,128)(2,1)}, f32[2,128]{1,0:T(2,128)}, f32[2,128]{1,0:T(2,128)}, f32[168,96]{1,0:T(8,...) custom-call(bf16[4608,128]{1,0:T(8,128)(2,1)} %tokens.3, ...), custom_call_target="tpu_custom_call" | custom-call | tf_op jit(solution)/shard_map/pallas_call | solution.py:1157

commit v3 on v2

--- a/solution.py
+++ b/solution.py
@@ -33,18 +33,16 @@
 GRAD_COUNT = {1: 1, 2: 2, 3: 4}
 DUE_FAR = {
     ("forward", 2): [(0, 0), (1, 0), (0, 1), (1, 1)],
-    ("scattered", 0): [(0, 2)],
-    ("gathered", 0): [(1, 2)],
+    ("gathered", 0): [(0, 2), (1, 2)],
 }
 DUE_NEAR = {
     ("forward", 0): [(0, 0)],
     ("backward", 0): [(1, 0)],
     ("forward", 1): [(0, 1)],
     ("backward", 1): [(1, 1)],
-    ("scattered", 0): [(0, 2)],
-    ("gathered", 0): [(1, 2)],
+    ("forward", 2): [(0, 2)],
+    ("backward", 2): [(1, 2)],
 }
-
 AT_SEASON_IN = 8
 AT_TREND_IN = AT_SEASON_IN + NL * SEASON_ROWS
 AT_SEASON_OUT = AT_TREND_IN + NL * L0
@@ -228,7 +226,9 @@
     half_bf,
     plane_in,
     plane_bf,
-    depth_in,
+    pair_in,
+    across_out,
+    across_in,
     relay_buf,
     relay_send,
     relay_recv,
@@ -815,7 +815,6 @@
     plane_index = scale_index * plane_dp + place_dp
     half_rows = pack_rows // 2
     plane_rows = half_rows // plane_size
-    depth_rows = plane_rows // 4
 
     def core_id():
         return (scale_index, position + 1 - 2 * core)
@@ -846,6 +845,7 @@
     theirs = pl.multiple_of((1 - core) * half_rows, 16)
     first_copy = remote(pack.at[pl.ds(theirs, half_rows)], half_in, 0, 0, 0, core_id())
     first_copy.start()
+    results_out("packed", 0)
     first_copy.wait_send()
     arrived(half_in, 0, 0)
     half_bf[pl.ds(mine, half_rows)] = (pack[pl.ds(mine, half_rows)] + half_in[...]).astype(BF16)
@@ -853,7 +853,7 @@
     def plane_piece(index):
         return pl.ds(pl.multiple_of(mine + index * plane_rows, 16), plane_rows)
 
-    def plane_round(stage, source_of, target_of, act):
+    def plane_round(act):
         def one(k, carry):
             other = lax.rem(plane_index + k, plane_size)
             back = lax.rem(plane_index + plane_size - k, plane_size)
@@ -865,7 +865,8 @@
     def plane_scatter(other, back, k):
         remote(half_bf.at[plane_piece(other)], plane_in.at[k], 1, k, k, plane_id(other)).start()
 
-    plane_round(1, None, None, plane_scatter)
+    plane_round(plane_scatter)
+    results_out("planed", 0)
     plane_sum = pack[plane_piece(plane_index)] + half_in[
         pl.ds(pl.multiple_of(plane_index * plane_rows, 16), plane_rows)
     ]
@@ -880,50 +881,56 @@
         plane_sum = plane_sum + plane_in[k].astype(F32)
     plane_bf[...] = plane_sum.astype(BF16)
 
-    def depth_piece(index):
-        return pl.ds(pl.multiple_of(index * depth_rows, 16), depth_rows)
-
-    for k in range(1, 4):
-        other = lax.rem(depth_index + k, 4)
-        remote(plane_bf.at[depth_piece(other)], depth_in.at[k], 2, k, k, depth_id(other)).start()
-    results_out("scattered", 0)
-    for k in range(1, 4):
-        remote(plane_bf.at[depth_piece(0)], depth_in.at[k], 2, k, k, core_id()).wait_send()
-        arrived(depth_in.at[k], 2, k)
-    total = plane_bf[depth_piece(depth_index)].astype(F32)
-    for k in range(1, 4):
-        total = total + depth_in[k].astype(F32)
-
-    def final_piece(plane, depth):
-        return pl.ds(pl.multiple_of(mine + plane * plane_rows + depth * depth_rows, 16), depth_rows)
-
-    own = final_piece(plane_index, depth_index)
-    packed_out[own] = total.astype(BF16)
-    for k in range(1, 4):
-        other = lax.rem(depth_index + k, 4)
-        remote(packed_out.at[own], packed_out.at[own], 3, k, k, depth_id(other)).start()
+    outer = jnp.where(depth_index < 2, 0, 3)
+    inner = jnp.where(depth_index < 2, 1, 2)
+    own_plane = plane_piece(plane_index)
+    give = remote(plane_bf, pair_in, 2, 0, 0, depth_id(outer))
+    across = remote(across_out, across_in, 3, 0, 0, depth_id(3 - outer))
+    back = remote(packed_out.at[own_plane], packed_out.at[own_plane], 4, 0, 0, depth_id(inner))
+
+    @pl.when(depth_index == inner)
+    def _():
+        give.start()
+
+    results_out("paired", 0)
+
+    @pl.when(depth_index == inner)
+    def _():
+        give.wait_send()
+        arrived(packed_out.at[own_plane], 4, 0)
+
+    @pl.when(depth_index == outer)
+    def _():
+        arrived(pair_in, 2, 0)
+        across_out[...] = (plane_bf[...].astype(F32) + pair_in[...].astype(F32)).astype(BF16)
+        across.start()
+        across.wait_send()
+        arrived(across_in, 3, 0)
+        packed_out[own_plane] = (across_out[...].astype(F32) + across_in[...].astype(F32)).astype(BF16)
+        back.start()
+
     results_out("gathered", 0)
-    for k in range(1, 4):
-        back = lax.rem(depth_index + 4 - k, 4)
-        remote(packed_out.at[own], packed_out.at[own], 3, k, k, core_id()).wait_send()
-        arrived(packed_out.at[final_piece(plane_index, back)], 3, k)
-    own_plane = plane_piece(plane_index)
+
+    @pl.when(depth_index == outer)
+    def _():
+        back.wait_send()
+
 
     def plane_gather(other, back, k):
-        remote(packed_out.at[own_plane], packed_out.at[own_plane], 4, k, k, plane_id(other)).start()
-
-    plane_round(4, None, None, plane_gather)
+        remote(packed_out.at[own_plane], packed_out.at[own_plane], 5, k, k, plane_id(other)).start()
+
+    plane_round(plane_gather)
 
     def plane_gathered(other, back, k):
-        remote(packed_out.at[own_plane], packed_out.at[own_plane], 4, k, k, core_id()).wait_send()
-        arrived(packed_out.at[plane_piece(back)], 4, k)
-
-    plane_round(4, None, None, plane_gathered)
+        remote(packed_out.at[own_plane], packed_out.at[own_plane], 5, k, k, core_id()).wait_send()
+        arrived(packed_out.at[plane_piece(back)], 5, k)
+
+    plane_round(plane_gathered)
     own_half = pl.ds(mine, half_rows)
-    last_copy = remote(packed_out.at[own_half], packed_out.at[own_half], 5, 0, 0, core_id())
+    last_copy = remote(packed_out.at[own_half], packed_out.at[own_half], 6, 0, 0, core_id())
     last_copy.start()
     last_copy.wait_send()
-    arrived(packed_out.at[pl.ds(theirs, half_rows)], 5, 0)
+    arrived(packed_out.at[pl.ds(theirs, half_rows)], 6, 0)
 
     def sent(copy, remote_copy):
         if remote_copy:
@@ -1115,7 +1122,9 @@
         pltpu.VMEM((pack_rows, LANES), BF16),
         pltpu.VMEM((plane_size, plane_rows, LANES), BF16),
         pltpu.VMEM((plane_rows, LANES), BF16),
-        pltpu.VMEM((4, plane_rows // 4, LANES), BF16),
+        pltpu.VMEM((plane_rows, LANES), BF16),
+        pltpu.VMEM((plane_rows, LANES), BF16),
+        pltpu.VMEM((plane_rows, LANES), BF16),
         pltpu.VMEM((2, chunks, 2, SIZES[2], LANES), BF16),
         dma((2, chunks, 2)),
         dma((2, chunks, 2)),
@@ -1123,8 +1132,8 @@
         dma((2, chunks, 4)),
         dma((2, chunks, 4)),
         dma((2, chunks, 8)),
-        dma((6, max(plane_size, 4))),
-        dma((6, max(plane_size, 4))),
+        dma((7, plane_size)),
+        dma((7, plane_size)),
     ]
     mixed_out, input_grad, packed = pl.pallas_call(
         functools.partial(kernel_body, groups, n_scale, per_device, pack_rows),

time: 114 us -> 111 us (0.974); the launches traced: 113 us -> 109 us
  Pallas kernels: 113 us -> 108 us
    pallas_call x1, Pallas kernels: 109 us -> 104 us  [body(): pl.pallas_call(functools.partial(kernel_body, groups, n_scale, per_device...]
where the time goes in v3:
time: 111 us; the launch traced here: 109 us
  Pallas kernels  108 us (97%)
    pallas_call x1, Pallas kernels, body(): pl.pallas_call(functools.partial(kernel_body, groups, n_scale, per_device...  104 us
    pallas_call x1, Pallas kernels, body(): pl.pallas_call(functools.partial(unpack_body, groups), out_shape=[jax.Sha...  3.61 us

profile of v3, /device:TPU:0, one launch (start us, length us, event | category | flops | bytes accessed | tf_op | source)
XLA Modules:
  0.0 108.8 jit_solution(12835851074300837845)
XLA Ops:
  0.6 104.3 %shard_map.203 = (bf16[4608,128]{1,0:T(8,128)(2,1)}, bf16[4608,128]{1,0:T(8,128)(2,1)}, bf16[2048,128]{1,0:T(8,128)(2,1)}) custom-call(bf16[4608,128]{1,0:T(8,128)(2,1)} %tokens.3, bf16[4608,128]{1,0:T(8,128)(2,1)} %cotangent.3, s32[1,384]{1,0:T(1,128)} %item_mask_hbm.1, f32[2,128]{1,0:T(2,128)} %ln_gain_hbm.1, f32[2,128]{1,0:T(2,128)} %ln_bias_hbm.1, ...), custom_call_target="tpu_custom_call" | custom-call | tf_op jit(solution)/shard_map/pallas_call | solution.py:1138
  105.0 3.6 %shard_map.204 = (bf16[4608,128]{1,0:T(8,128)(2,1)}, bf16[4608,128]{1,0:T(8,128)(2,1)}, f32[2,128]{1,0:T(2,128)}, f32[2,128]{1,0:T(2,128)}, f32[168,96]{1,0:T(8,...) custom-call(bf16[4608,128]{1,0:T(8,128)(2,1)} %tokens.3, ...), custom_call_target="tpu_custom_call" | custom-call | tf_op jit(solution)/shard_map/pallas_call | solution.py:1166

commit v4 on v3

--- a/solution.py
+++ b/solution.py
@@ -229,6 +229,7 @@
     pair_in,
     across_out,
     across_in,
+    pad_sem,
     relay_buf,
     relay_send,
     relay_recv,
@@ -376,6 +377,20 @@
         for scale in range(4):
             ref = target.at[chunk, pl.ds(STARTS[scale], SIZES[scale])]
             pltpu.make_async_copy(ref, ref, in_recv.at[kind, chunk, scale]).wait()
+
+    pad_rows = SLOTS[3] * per_device * LENGTHS[3]
+
+    def padding():
+        rows = pl.ds(pad_rows, tokens.shape[0] - pad_rows)
+        return [
+            pltpu.make_async_copy(tokens.at[rows], mixed_out.at[rows], pad_sem.at[0]),
+            pltpu.make_async_copy(cotangent.at[rows], input_grad.at[rows], pad_sem.at[1]),
+        ]
+
+    @pl.when(position >= bounds[3])
+    def _():
+        for copy in padding():
+            copy.start()
 
     def outbound(kind, scale, chunk):
         source = (out_buf, grad_buf)[kind]
@@ -932,6 +947,11 @@
     last_copy.wait_send()
     arrived(packed_out.at[pl.ds(theirs, half_rows)], 6, 0)
 
+    @pl.when(position >= bounds[3])
+    def _():
+        for copy in padding():
+            copy.wait()
+
     def sent(copy, remote_copy):
         if remote_copy:
             copy.wait_send()
@@ -964,18 +984,8 @@
     lax.fori_loop(0, chunks, finish, 0)
 
 
-def unpack_body(
-    groups,
-    tokens,
-    cotangent,
-    mixed,
-    grad,
-    packed_hbm,
-    mixed_out,
-    input_grad,
-    *refs,
-):
-    finals, (packed, staged, in_sem, out_sem, small_sem) = refs[:9], refs[18:]
+def unpack_body(mixed, grad, packed, mixed_out, input_grad, *refs):
+    finals, small_sem, big_sem = refs[:9], refs[18], refs[19]
     (
         gain_grad,
         bias_grad,
@@ -987,33 +997,14 @@
         ffn_bias_grad,
         ffn_out_grad,
     ) = refs[9:18]
-    packed_copy = pltpu.make_async_copy(packed_hbm, packed, small_sem.at[9])
-    packed_copy.start()
-    padded = lax.axis_index("dp") >= 7 * groups // 8
-    size = tokens.shape[0] // PIECES
-    for kind, (own, other) in enumerate(((mixed, tokens), (grad, cotangent))):
+    size = mixed.shape[0] // PIECES
+    big = []
+    for kind, (source, target) in enumerate(((mixed, mixed_out), (grad, input_grad))):
         for k in range(PIECES):
             rows = pl.ds(k * size, size)
-            usual = pltpu.make_async_copy(own.at[rows], staged.at[kind, rows], in_sem.at[kind, k])
-            if k < PIECES // 2:
-                usual.start()
-            else:
-                rest = pltpu.make_async_copy(other.at[rows], staged.at[kind, rows], in_sem.at[kind, k])
-
-                @pl.when(padded)
-                def _():
-                    rest.start()
-
-                @pl.when(jnp.logical_not(padded))
-                def _():
-                    usual.start()
-
-    def piece_out(kind, k):
-        rows = pl.ds(k * size, size)
-        target = (mixed_out, input_grad)[kind]
-        return pltpu.make_async_copy(staged.at[kind, rows], target.at[rows], out_sem.at[kind, k])
-
-    packed_copy.wait()
+            big.append(pltpu.make_async_copy(source.at[rows], target.at[rows], big_sem.at[kind, k]))
+    for copy in big:
+        copy.start()
     top = packed[0:16, :].astype(F32)
     gain_grad[...] = top[0:NL]
     bias_grad[...] = top[NL : 2 * NL]
@@ -1042,16 +1033,8 @@
     ]
     for copy in small:
         copy.start()
-    for kind in range(2):
-        for k in range(PIECES):
-            rows = pl.ds(k * size, size)
-            pltpu.make_async_copy(mixed.at[rows], staged.at[kind, rows], in_sem.at[kind, k]).wait()
-            piece_out(kind, k).start()
-    for copy in small:
+    for copy in small + big:
         copy.wait()
-    for kind in range(2):
-        for k in range(PIECES):
-            piece_out(kind, k).wait()
 
 
 def body(groups, n_scale, *args):
@@ -1125,6 +1108,7 @@
         pltpu.VMEM((plane_rows, LANES), BF16),
         pltpu.VMEM((plane_rows, LANES), BF16),
         pltpu.VMEM((plane_rows, LANES), BF16),
+        dma((2,)),
         pltpu.VMEM((2, chunks, 2, SIZES[2], LANES), BF16),
         dma((2, chunks, 2)),
         dma((2, chunks, 2)),
@@ -1138,12 +1122,12 @@
     mixed_out, input_grad, packed = pl.pallas_call(
         functools.partial(kernel_body, groups, n_scale, per_device, pack_rows),
         out_shape=[
-            jax.ShapeDtypeStruct(tokens.shape, BF16),
-            jax.ShapeDtypeStruct(tokens.shape, BF16),
-            jax.ShapeDtypeStruct((pack_rows, LANES), BF16),
+            pltpu.VMEM(tokens.shape, BF16),
+            pltpu.VMEM(tokens.shape, BF16),
+            pltpu.VMEM((pack_rows, LANES), BF16),
         ],
         in_specs=[anywhere] * len(turned),
-        out_specs=[anywhere, anywhere, vmem],
+        out_specs=[vmem, vmem, vmem],
         scratch_shapes=scratch,
         compiler_params=pltpu.CompilerParams(
             collective_id=0, has_side_effects=True, vmem_limit_bytes=58 << 20
@@ -1164,24 +1148,18 @@
         )
     ]
     outs = pl.pallas_call(
-        functools.partial(unpack_body, groups),
+        unpack_body,
         out_shape=[
             jax.ShapeDtypeStruct(tokens.shape, BF16),
             jax.ShapeDtypeStruct(tokens.shape, BF16),
             *finals,
         ],
-        in_specs=[anywhere] * 5,
+        in_specs=[vmem] * 3,
         out_specs=[anywhere] * 11,
         scratch_shapes=[pltpu.VMEM(member.shape, F32) for member in finals]
-        + [
-            pltpu.VMEM((pack_rows, LANES), BF16),
-            pltpu.VMEM((2,) + tokens.shape, BF16),
-            dma((2, PIECES)),
-            dma((2, PIECES)),
-            dma((len(finals) + 1,)),
-        ],
-        compiler_params=pltpu.CompilerParams(vmem_limit_bytes=58 << 20),
-    )(tokens, args[1], mixed_out, input_grad, packed)
+        + [dma((len(finals),)), dma((2, PIECES))],
+        compiler_params=pltpu.CompilerParams(vmem_limit_bytes=16 << 20),
+    )(*(pltpu.with_memory_space_constraint(member, pltpu.VMEM) for member in (mixed_out, input_grad, packed)))
     return (
         *outs[:4],
         jnp.swapaxes(outs[4].reshape(SEASON_ROWS, NL, L0), 0, 1),

time: 111 us -> 108 us (0.973)
  Pallas kernels: 108 us -> 105 us
    pallas_call x1, Pallas kernels: 3.61 us -> 1.88 us  [body(): pl.pallas_call(unpack_body, out_shape=[jax.ShapeDtypeStruct(tokens.shape,...]
where the time goes in v4:
time: 108 us; the launch traced here: 106 us
  Pallas kernels  105 us (97%)
    pallas_call x1, Pallas kernels, body(): pl.pallas_call(functools.partial(kernel_body, groups, n_scale, per_device...  104 us

profile of v4, /device:TPU:0, one launch (start us, length us, event | category | flops | bytes accessed | tf_op | source)
XLA Modules:
  0.0 106.2 jit_solution(2394569880484896517)
XLA Ops:
  0.6 103.5 %shard_map.203 = (bf16[4608,128]{1,0:T(8,128)(2,1)S(1)}, bf16[4608,128]{1,0:T(8,128)(2,1)S(1)}, bf16[2048,128]{1,0:T(8,128)(2,1)S(1)}) custom-call(bf16[4608,128]{1,0:T(8,128)(2,1)} %tokens.1, bf16[4608,128]{1,0:T(8,128)(2,1)} %cotangent.1, s32[1,384]{1,0:T(1,128)} %item_mask_hbm.1, f32[2,128]{1,0:T(2,128)} %ln_gain_hbm.1, f32[2,128]{1,0:T(2,128)} %ln_bias_hbm.1, ...), custom_call_target="tpu_custom_call" | custom-call | tf_op jit(solution)/shard_map/pallas_call | solution.py:1122
  104.2 1.9 %shard_map.204 = (bf16[4608,128]{1,0:T(8,128)(2,1)}, bf16[4608,128]{1,0:T(8,128)(2,1)}, f32[2,128]{1,0:T(2,128)}, f32[2,128]{1,0:T(2,128)}, f32[168,96]{1,0:T(8,...) custom-call(bf16[4608,128]{1,0:T(8,128)(2,1)S(1)} %get-tuple-element, ...), custom_call_target="tpu_custom_call" | custom-call | tf_op jit(solution)/shard_map/pallas_call | solution.py:1150

commit v5 on v4

--- a/solution.py
+++ b/solution.py
@@ -31,18 +31,6 @@
 UNITS = {1: (0, 1), 2: (2,), 3: (3,)}
 WEIGHT_COUNT = {1: 2, 2: 4, 3: 4}
 GRAD_COUNT = {1: 1, 2: 2, 3: 4}
-DUE_FAR = {
-    ("forward", 2): [(0, 0), (1, 0), (0, 1), (1, 1)],
-    ("gathered", 0): [(0, 2), (1, 2)],
-}
-DUE_NEAR = {
-    ("forward", 0): [(0, 0)],
-    ("backward", 0): [(1, 0)],
-    ("forward", 1): [(0, 1)],
-    ("backward", 1): [(1, 1)],
-    ("forward", 2): [(0, 2)],
-    ("backward", 2): [(1, 2)],
-}
 AT_SEASON_IN = 8
 AT_TREND_IN = AT_SEASON_IN + NL * SEASON_ROWS
 AT_SEASON_OUT = AT_TREND_IN + NL * L0
@@ -51,6 +39,7 @@
 AT_FFN_OUT = AT_FFN_IN + NL * 2 * LANES
 USED_ROWS = AT_FFN_OUT + NL * 2 * LANES
 PIECES = 4
+FIRST_STEPS = 3
 
 
 def dot(a, b):
@@ -147,6 +136,31 @@
     slot = jnp.where(part == 1, 2, jnp.where(part == 2, 1, part))
     first = 3 * groups // 4 if scale == 2 else 7 * groups // 8
     return first + lax.rem(group, groups // 8), slot
+
+
+def chunk_counts(per_device):
+    total = per_device // ITEMS
+    return total - total // 3, total // 3
+
+
+def due_results(per_device):
+    lower_chunks, upper_chunks = chunk_counts(per_device)
+
+    def at_once(count):
+        return {("forward", c): [(0, c)] for c in range(count)} | {("backward", c): [(1, c)] for c in range(count)}
+
+    last, top = lower_chunks - 1, upper_chunks - 1
+    return {
+        (True, False): {("forward", c + 1): [(0, c)] for c in range(last)}
+        | {("backward", c): [(1, c)] for c in range(last)}
+        | {("gathered", 0): [(0, last), (1, last)]},
+        (False, False): at_once(lower_chunks),
+        (False, True): at_once(upper_chunks) | {("backward", top): [], ("paired", 0): [(1, top)]},
+        (True, True): {
+            ("crossed", 0): [(kind, c) for c in range(upper_chunks) for kind in range(2)][:-1],
+            ("gathered", 0): [(1, top)],
+        },
+    }
 
 
 def kernel_body(
@@ -189,17 +203,17 @@
     grad,
     df_keep,
     da_keep,
-    unit,
-    inverse,
-    z_keep,
-    hidden,
-    slope,
-    season_src,
-    trend_src,
-    season_hid,
-    season_slope,
-    trend_hid,
-    trend_slope,
+    unit_all,
+    inverse_all,
+    z_keep_all,
+    hidden_all,
+    slope_all,
+    season_src_all,
+    trend_src_all,
+    season_hid_all,
+    season_slope_all,
+    trend_hid_all,
+    trend_slope_all,
     sa,
     sb,
     ta,
@@ -230,6 +244,7 @@
     across_out,
     across_in,
     pad_sem,
+    come_down,
     relay_buf,
     relay_send,
     relay_recv,
@@ -239,15 +254,18 @@
     out_recv,
     ar_send,
     ar_recv,
+    *pack_refs,
 ):
     scale_index = lax.axis_index("scale")
     position = lax.axis_index("dp")
     worker_group = lax.rem(position, groups // 2)
     worker_half = lax.div(position, groups // 2)
-    half_items = per_device // 2
-    chunks = half_items // ITEMS
+    upper = position >= groups // 2
+    lower_chunks, upper_chunks = chunk_counts(per_device)
+    chunks = jnp.where(upper, upper_chunks, lower_chunks)
     bounds = [0, groups // 2, 3 * groups // 4, 7 * groups // 8, groups]
 
+    masks, places, lays = pack_refs[0:4], pack_refs[4:8], pack_refs[8:12]
     params = [
         pltpu.make_async_copy(source, target, param_sem.at[k])
         for k, (source, target) in enumerate(
@@ -297,7 +315,7 @@
         source = (tokens, cotangent)[kind]
         target = (tok_buf, cot_buf)[kind]
         length, size = LENGTHS[scale], SIZES[scale]
-        first = (slot * per_device + half * half_items + chunk * ITEMS) * length
+        first = (slot * per_device + (half * lower_chunks + chunk) * ITEMS) * length
         src = source.at[pl.ds(pl.multiple_of(first, 16), size)]
         dst = target.at[chunk, pl.ds(STARTS[scale], size)]
         recv = in_recv.at[kind, chunk, scale]
@@ -343,18 +361,28 @@
 
             @pl.when((position >= bounds[scale]) & (position < bounds[scale + 1]))
             def _():
-                def one_chunk(chunk, carry):
+                def one_step(step, carry):
                     for kind, slot, half in order(scale):
-                        act(*inbound(kind, scale, slot, half, chunk))
+                        chunk = step - kind
+
+                        @pl.when((chunk >= 0) & (chunk < (upper_chunks if half else lower_chunks)))
+                        def _():
+                            act(*inbound(kind, scale, slot, half, chunk))
+
                     if scale >= 2:
                         other = 5 - scale
                         for kind in range(2):
-                            for slot in range(4):
-                                if relayed(other, slot, 0):
-                                    act_relay(relay(kind, other, slot, chunk), kind, slot, chunk)
+                            chunk = step - kind
+
+                            @pl.when((chunk >= 0) & (chunk < lower_chunks))
+                            def _():
+                                for slot in range(4):
+                                    if relayed(other, slot, 0):
+                                        act_relay(relay(kind, other, slot, chunk), kind, slot, chunk)
+
                     return carry
 
-                lax.fori_loop(low, high, one_chunk, 0)
+                lax.fori_loop(low, high, one_step, 0)
 
     def pass_on(copy, kind, slot, chunk):
         size = SIZES[2 if slot >= 2 else 3]
@@ -366,7 +394,7 @@
         each_inbound(lambda copy, remote: copy.start(), pass_on, low, high)
 
     far = (position < groups // 4) | (position >= bounds[2])
-    inbound_start(0, jnp.where(far, 1, chunks))
+    inbound_start(0, jnp.where(far, FIRST_STEPS, lower_chunks + 1))
     for copy in params:
         copy.start()
     for copy in params:
@@ -397,7 +425,7 @@
         target = (mixed_out, input_grad)[kind]
         home, slot = home_of(groups, scale, worker_group)
         length, size = LENGTHS[scale], SIZES[scale]
-        first = (slot * per_device + worker_half * half_items + chunk * ITEMS) * length
+        first = (slot * per_device + (worker_half * lower_chunks + chunk) * ITEMS) * length
         src = source.at[chunk, pl.ds(STARTS[scale], size)]
         dst = target.at[pl.ds(pl.multiple_of(first, 16), size)]
         recv = out_recv.at[kind, chunk, slot * 2 + worker_half]
@@ -425,11 +453,11 @@
                 remote.start()
 
     def results_out(event, chunk):
-        for is_far, due in ((True, DUE_FAR), (False, DUE_NEAR)):
+        for (is_far, is_upper), due in due_results(per_device).items():
             for at, sends in due.items():
-                if at[0] == event:
-
-                    @pl.when((far if is_far else jnp.logical_not(far)) & (chunk == at[1]))
+                if at[0] == event and sends:
+
+                    @pl.when((far == is_far) & (upper == is_upper) & (chunk == at[1]))
                     def _():
                         for kind, done in sends:
                             outbound_start(kind, done)
@@ -459,6 +487,26 @@
         eye_out = selection(LANES, LANES, 1, LANES, 0).astype(BF16)
         win_t[layer] = dot_nt(eye_in, ffn_in[layer]).astype(BF16)
         wout_t[layer] = dot_nt(eye_out, ffn_out[layer]).astype(BF16)
+    for c in (1, 2, 3):
+        count = GRAD_COUNT[c]
+        fine, coarse = LENGTHS[c - 1], LENGTHS[c]
+        at_season = L0 - fine
+        at_trend = 2 * L0 - 2 * fine
+        for k, (height, width, row, lane, stride) in enumerate(
+            (
+                (coarse, fine, NL * at_season, 0, NL),
+                (coarse, coarse, 0, at_season, 1),
+                (coarse, fine, 0, at_trend, 1),
+                (fine, fine, at_trend, 0, 1),
+            )
+        ):
+            masks[k][c - 1] = block_mask(count, height, width)
+            rows, lanes = places[k].shape[2], lays[k].shape[2]
+            for layer in range(NL):
+                start = row + layer if stride > 1 else row
+                place = selection(count * height, rows, count, height, start, True, stride)
+                places[k][layer, c - 1] = place.astype(BF16)
+            lays[k][c - 1] = selection(count * width, lanes, count, width, lane).astype(BF16)
     for scale, height, number in SLABS:
         for ref, is_turned in ((moving, False), (moving_t, True)):
             counts = moving_counts(height // LENGTHS[scale], LENGTHS[scale], is_turned)
@@ -466,10 +514,10 @@
     mean_lanes = jnp.full((LANES, LANES), 1.0 / LANES, BF16)
 
     mask_rows = jnp.broadcast_to(item_mask[...].astype(F32), (LANES, item_mask.shape[1])).astype(BF16)
-    first_item = worker_group * per_device + worker_half * half_items
+    first_item = worker_group * per_device + worker_half * lower_chunks * ITEMS
     chosen = iota((32, item_mask.shape[1]), 1) == iota((32, item_mask.shape[1]), 0) + first_item
     item_live = dot_nt(chosen.astype(F32).astype(BF16), mask_rows).astype(BF16)
-    for chunk in range(chunks):
+    for chunk in range(lower_chunks):
         for i in range(4):
             place = (iota((SIZES[i], 32), 0).astype(F32) + 0.5) * (1.0 / LENGTHS[i])
             column = iota((SIZES[i], 32), 1).astype(F32) - float(chunk * ITEMS)
@@ -488,7 +536,38 @@
         half = SIZES[scale] // 2
         return [STARTS[scale] + side * half + j * height for side in range(2)]
 
+    def kept_of(chunk):
+        return [
+            ref.at[lax.rem(chunk, 2)]
+            for ref in (
+                unit_all,
+                inverse_all,
+                z_keep_all,
+                hidden_all,
+                slope_all,
+                season_src_all,
+                trend_src_all,
+                season_hid_all,
+                season_slope_all,
+                trend_hid_all,
+                trend_slope_all,
+            )
+        ]
+
     def forward(layer, chunk, found):
+        (
+            unit,
+            inverse,
+            z_keep,
+            hidden,
+            slope,
+            season_src,
+            trend_src,
+            season_hid,
+            season_slope,
+            trend_hid,
+            trend_slope,
+        ) = kept_of(chunk)
         gain = ln_gain[layer : layer + 1, :]
         offset = ln_bias[layer : layer + 1, :]
         offset_pair = jnp.concatenate([offset, offset], 1)
@@ -619,6 +698,19 @@
                 yield ffn(scale, height, j)
 
     def backward(layer, chunk, found):
+        (
+            unit,
+            inverse,
+            z_keep,
+            hidden,
+            slope,
+            season_src,
+            trend_src,
+            season_hid,
+            season_slope,
+            trend_hid,
+            trend_slope,
+        ) = kept_of(chunk)
         gain = ln_gain[layer : layer + 1, :]
 
         def rows_of(start, height):
@@ -773,40 +865,46 @@
                 yield norm(scale, height, j)
         yield weight_grads()
 
-    def one_chunk(chunk, carry):
-        inbound_wait(0, chunk)
-        found = {}
-        drive([thread for layer in range(NL) for thread in forward(layer, chunk, found)])
-        inbound_start(chunk + 1, jnp.where(far & (chunk < chunks - 1), chunk + 2, chunk + 1))
-
-        results_out("forward", chunk)
-        inbound_wait(1, chunk)
-        found = {}
-        drive([thread for layer in reversed(range(NL)) for thread in backward(layer, chunk, found)])
-        results_out("backward", chunk)
+    def one_step(step, carry):
+        @pl.when(step < chunks)
+        def _():
+            inbound_wait(0, step)
+            found = {}
+            drive([thread for layer in range(NL) for thread in forward(layer, step, found)])
+            later = step + FIRST_STEPS
+            inbound_start(later, jnp.where(far & (later <= lower_chunks), later + 1, later))
+            results_out("forward", step)
+
+        @pl.when(step > 0)
+        def _():
+            chunk = step - 1
+            inbound_wait(1, chunk)
+
+            @pl.when(jnp.logical_not(upper | far) & (chunk == lower_chunks - 1))
+            def _():
+                pl.semaphore_signal(
+                    come_down,
+                    inc=1,
+                    device_id=(scale_index, position + groups // 2),
+                    device_id_type=MESH,
+                )
+
+            found = {}
+            drive([thread for layer in reversed(range(NL)) for thread in backward(layer, chunk, found)])
+            results_out("backward", chunk)
+
         return carry
 
-    lax.fori_loop(0, chunks, one_chunk, 0)
+    lax.fori_loop(0, chunks + 1, one_step, 0)
+    rest = chunks + FIRST_STEPS
+    inbound_start(rest, jnp.where(far & upper, lower_chunks + 1, rest))
 
     for layer in range(NL):
         parts = [None] * 4
         for c in (1, 2, 3):
-            count = GRAD_COUNT[c]
-            fine, coarse = LENGTHS[c - 1], LENGTHS[c]
-            at_season = L0 - fine
-            at_trend = 2 * L0 - 2 * fine
-            for k, (value, height, width, rows, row, lanes, lane, stride) in enumerate(
-                (
-                    (d_sa, coarse, fine, NL * SEASON_ROWS, NL * at_season + layer, LANES, 0, NL),
-                    (d_sb, coarse, coarse, L0 // 2, 0, LANES, at_season, 1),
-                    (d_ta, coarse, fine, L0 // 2, 0, 2 * LANES, at_trend, 1),
-                    (d_tb, fine, fine, TREND_ROWS, at_trend, LANES, 0, 1),
-                )
-            ):
-                masked = (value[layer, c - 1] * block_mask(count, height, width)).astype(BF16)
-                place = selection(count * height, rows, count, height, row, True, stride).astype(BF16)
-                lay = selection(count * width, lanes, count, width, lane).astype(BF16)
-                found = dot(dot(place, masked).astype(BF16), lay)
+            for k, value in enumerate((d_sa, d_sb, d_ta, d_tb)):
+                masked = (value[layer, c - 1] * masks[k][c - 1]).astype(BF16)
+                found = dot(dot(places[k][layer, c - 1], masked).astype(BF16), lays[k][c - 1])
                 parts[k] = found if parts[k] is None else parts[k] + found
         pack[layer : layer + 1, :] = jnp.sum(d_gain[layer], 0, keepdims=True)
         pack[NL + layer : NL + layer + 1, :] = jnp.sum(d_off[layer], 0, keepdims=True)
@@ -919,6 +1017,15 @@
         arrived(pair_in, 2, 0)
         across_out[...] = (plane_bf[...].astype(F32) + pair_in[...].astype(F32)).astype(BF16)
         across.start()
+
+    @pl.when(far & upper)
+    def _():
+        pl.semaphore_wait(come_down, 1)
+
+    results_out("crossed", 0)
+
+    @pl.when(depth_index == outer)
+    def _():
         across.wait_send()
         arrived(across_in, 3, 0)
         packed_out[own_plane] = (across_out[...].astype(F32) + across_in[...].astype(F32)).astype(BF16)
@@ -956,14 +1063,14 @@
         if remote_copy:
             copy.wait_send()
 
-    each_inbound(sent, lambda copy, kind, slot, chunk: copy.wait_send(), 0, chunks)
+    each_inbound(sent, lambda copy, kind, slot, chunk: copy.wait_send(), 0, lower_chunks + 1)
 
     def finish(chunk, carry):
         for kind in range(2):
             for scale in range(4):
                 home, local, remote_copy = outbound(kind, scale, chunk)
 
-                @pl.when(home != position)
+                @pl.when((home != position) & (chunk < chunks))
                 def _():
                     remote_copy.wait_send()
 
@@ -973,15 +1080,20 @@
                 def _():
                     for slot in range(SLOTS[scale]):
                         for half in range(2):
-                            first = (slot * per_device + half * half_items + chunk * ITEMS) * LENGTHS[scale]
-                            ref = (mixed_out, input_grad)[kind].at[
-                                pl.ds(pl.multiple_of(first, 16), SIZES[scale])
-                            ]
-                            pltpu.make_async_copy(ref, ref, out_recv.at[kind, chunk, slot * 2 + half]).wait()
+
+                            @pl.when(chunk < (upper_chunks if half else lower_chunks))
+                            def _():
+                                place = half * lower_chunks + chunk
+                                first = (slot * per_device + place * ITEMS) * LENGTHS[scale]
+                                ref = (mixed_out, input_grad)[kind].at[
+                                    pl.ds(pl.multiple_of(first, 16), SIZES[scale])
+                                ]
+                                sem = out_recv.at[kind, chunk, slot * 2 + half]
+                                pltpu.make_async_copy(ref, ref, sem).wait()
 
         return carry
 
-    lax.fori_loop(0, chunks, finish, 0)
+    lax.fori_loop(0, lower_chunks, finish, 0)
 
 
 def unpack_body(mixed, grad, packed, mixed_out, input_grad, *refs):
@@ -1041,9 +1153,8 @@
     tokens = args[0]
     hidden = args[9].shape[2]
     per_device = tokens.shape[0] // L0
-    chunks = per_device // 2 // ITEMS
-    devices = groups * n_scale
-    unit_rows = 16 * devices
+    chunks = max(chunk_counts(per_device))
+    unit_rows = 16 * 2 * (groups // 8) * n_scale
     pack_rows = -(-USED_ROWS // unit_rows) * unit_rows
     plane_size = groups // 8 * n_scale
     plane_rows = pack_rows // 2 // plane_size
@@ -1068,17 +1179,17 @@
         pltpu.VMEM((CHUNK, LANES), F32),
         pltpu.VMEM((CHUNK, LANES), BF16),
         pltpu.VMEM((CHUNK, hidden), BF16),
-        pltpu.VMEM((NL, CHUNK, LANES), F32),
-        pltpu.VMEM((NL, CHUNK, LANES), F32),
-        pltpu.VMEM((NL, CHUNK, LANES), BF16),
-        pltpu.VMEM((NL, CHUNK, hidden), BF16),
-        pltpu.VMEM((NL, CHUNK, hidden), BF16),
-        pltpu.VMEM((NL, 4, 192, 2 * LANES), BF16),
-        pltpu.VMEM((NL, 4, 96, 2 * LANES), BF16),
-        pltpu.VMEM((NL, 4, 96, 2 * LANES), BF16),
-        pltpu.VMEM((NL, 4, 96, 2 * LANES), BF16),
-        pltpu.VMEM((NL, 4, 192, 2 * LANES), BF16),
-        pltpu.VMEM((NL, 4, 192, 2 * LANES), BF16),
+        pltpu.VMEM((2, NL, CHUNK, LANES), F32),
+        pltpu.VMEM((2, NL, CHUNK, LANES), F32),
+        pltpu.VMEM((2, NL, CHUNK, LANES), BF16),
+        pltpu.VMEM((2, NL, CHUNK, hidden), BF16),
+        pltpu.VMEM((2, NL, CHUNK, hidden), BF16),
+        pltpu.VMEM((2, NL, 4, 192, 2 * LANES), BF16),
+        pltpu.VMEM((2, NL, 4, 96, 2 * LANES), BF16),
+        pltpu.VMEM((2, NL, 4, 96, 2 * LANES), BF16),
+        pltpu.VMEM((2, NL, 4, 96, 2 * LANES), BF16),
+        pltpu.VMEM((2, NL, 4, 192, 2 * LANES), BF16),
+        pltpu.VMEM((2, NL, 4, 192, 2 * LANES), BF16),
         pltpu.VMEM((NL, 3, 96, 192), BF16),
         pltpu.VMEM((NL, 3, 96, 96), BF16),
         pltpu.VMEM((NL, 3, 192, 96), BF16),
@@ -1109,6 +1220,7 @@
         pltpu.VMEM((plane_rows, LANES), BF16),
         pltpu.VMEM((plane_rows, LANES), BF16),
         dma((2,)),
+        pltpu.SemaphoreType.REGULAR,
         pltpu.VMEM((2, chunks, 2, SIZES[2], LANES), BF16),
         dma((2, chunks, 2)),
         dma((2, chunks, 2)),
@@ -1118,6 +1230,18 @@
         dma((2, chunks, 8)),
         dma((7, plane_size)),
         dma((7, plane_size)),
+        pltpu.VMEM((3, 48, 96), F32),
+        pltpu.VMEM((3, 48, 48), F32),
+        pltpu.VMEM((3, 48, 96), F32),
+        pltpu.VMEM((3, 96, 96), F32),
+        pltpu.VMEM((NL, 3, NL * SEASON_ROWS, 48), BF16),
+        pltpu.VMEM((NL, 3, L0 // 2, 48), BF16),
+        pltpu.VMEM((NL, 3, L0 // 2, 48), BF16),
+        pltpu.VMEM((NL, 3, TREND_ROWS, 96), BF16),
+        pltpu.VMEM((3, 96, LANES), BF16),
+        pltpu.VMEM((3, 48, LANES), BF16),
+        pltpu.VMEM((3, 96, 2 * LANES), BF16),
+        pltpu.VMEM((3, 96, LANES), BF16),
     ]
     mixed_out, input_grad, packed = pl.pallas_call(
         functools.partial(kernel_body, groups, n_scale, per_device, pack_rows),

time: 108 us -> 108 us (level); the launches traced: 106 us -> 107 us
  Pallas kernels: 105 us -> 107 us
    pallas_call x1, Pallas kernels: 104 us -> 105 us  [body(): pl.pallas_call(functools.partial(kernel_body, groups, n_scale, per_device...]
where the time goes in v5:
time: 108 us; the launch traced here: 107 us
  Pallas kernels  107 us (99%)
    pallas_call x1, Pallas kernels, body(): pl.pallas_call(functools.partial(kernel_body, groups, n_scale, per_device...  105 us

profile of v5, /device:TPU:0, one launch (start us, length us, event | category | flops | bytes accessed | tf_op | source)
XLA Modules:
  0.0 107.4 jit_solution(3162172311376491416)
XLA Ops:
  0.6 104.6 %shard_map.203 = (bf16[4608,128]{1,0:T(8,128)(2,1)S(1)}, bf16[4608,128]{1,0:T(8,128)(2,1)S(1)}, bf16[1920,128]{1,0:T(8,128)(2,1)S(1)}) custom-call(bf16[4608,128]{1,0:T(8,128)(2,1)} %tokens.1, bf16[4608,128]{1,0:T(8,128)(2,1)} %cotangent.1, s32[1,384]{1,0:T(1,128)} %item_mask_hbm.1, f32[2,128]{1,0:T(2,128)} %ln_gain_hbm.1, f32[2,128]{1,0:T(2,128)} %ln_bias_hbm.1, ...), custom_call_target="tpu_custom_call" | custom-call | tf_op jit(solution)/shard_map/pallas_call | solution.py:1246
  105.3 1.9 %shard_map.204 = (bf16[4608,128]{1,0:T(8,128)(2,1)}, bf16[4608,128]{1,0:T(8,128)(2,1)}, f32[2,128]{1,0:T(2,128)}, f32[2,128]{1,0:T(2,128)}, f32[168,96]{1,0:T(8,...) custom-call(bf16[4608,128]{1,0:T(8,128)(2,1)S(1)} %get-tuple-element, ...), custom_call_target="tpu_custom_call" | custom-call | tf_op jit(solution)/shard_map/pallas_call | solution.py:1274

commit v6 on v5

--- a/solution.py
+++ b/solution.py
@@ -31,11 +31,12 @@
 UNITS = {1: (0, 1), 2: (2,), 3: (3,)}
 WEIGHT_COUNT = {1: 2, 2: 4, 3: 4}
 GRAD_COUNT = {1: 1, 2: 2, 3: 4}
-AT_SEASON_IN = 8
-AT_TREND_IN = AT_SEASON_IN + NL * SEASON_ROWS
+AT_SEASON_IN = 16
+AT_TREND_IN = AT_SEASON_IN + 176
 AT_SEASON_OUT = AT_TREND_IN + NL * L0
 AT_TREND_OUT = AT_SEASON_OUT + NL * L0 // 2
-AT_FFN_IN = AT_TREND_OUT + NL * TREND_ROWS
+TREND_STEP = 176
+AT_FFN_IN = AT_TREND_OUT + NL * TREND_STEP
 AT_FFN_OUT = AT_FFN_IN + NL * 2 * LANES
 USED_ROWS = AT_FFN_OUT + NL * 2 * LANES
 PIECES = 4
@@ -153,8 +154,8 @@
     return {
         (True, False): {("forward", c + 1): [(0, c)] for c in range(last)}
         | {("backward", c): [(1, c)] for c in range(last)}
-        | {("gathered", 0): [(0, last), (1, last)]},
-        (False, False): at_once(lower_chunks),
+        | {("forward", last): [(0, last - 1), (0, last)], ("gathered", 0): [(1, last)]},
+        (False, False): at_once(lower_chunks) | {("backward", last): [], ("paired", 0): [(1, last)]},
         (False, True): at_once(upper_chunks) | {("backward", top): [], ("paired", 0): [(1, top)]},
         (True, True): {
             ("crossed", 0): [(kind, c) for c in range(upper_chunks) for kind in range(2)][:-1],
@@ -173,7 +174,7 @@
     item_mask_hbm,
     ln_gain_hbm,
     ln_bias_hbm,
-    season_in_hbm,
+    season_in,
     season_out_hbm,
     trend_in_hbm,
     trend_out_hbm,
@@ -186,7 +187,6 @@
     item_mask,
     ln_gain,
     ln_bias,
-    season_in,
     season_out,
     trend_in,
     trend_out,
@@ -273,7 +273,6 @@
                 (item_mask_hbm, item_mask),
                 (ln_gain_hbm, ln_gain),
                 (ln_bias_hbm, ln_bias),
-                (season_in_hbm, season_in),
                 (season_out_hbm, season_out),
                 (trend_in_hbm, trend_in),
                 (trend_out_hbm, trend_out),
@@ -472,7 +471,7 @@
                 (season_in[...], sa, sa_t, coarse, fine, NL * at_season + layer, 0, NL),
                 (season_out[layer], sb_t, sb, coarse, coarse, 0, at_season, 1),
                 (trend_in[layer], ta_t, ta, coarse, fine, 0, at_trend, 1),
-                (trend_out[layer], tb, tb_t, fine, fine, at_trend, 0, 1),
+                (trend_out[...], tb, tb_t, fine, fine, TREND_ROWS * layer + at_trend, 0, 1),
             ):
                 rows = selection(count * height, whole.shape[0], count, height, row, stride=stride)
                 columns = selection(count * width, whole.shape[1], count, width, column).astype(BF16)
@@ -912,7 +911,7 @@
         pack[AT_SEASON_IN : AT_SEASON_IN + NL * SEASON_ROWS, :] += parts[0]
         row = AT_SEASON_OUT + layer * L0 // 2
         pack[row : row + L0 // 2, :] = parts[1]
-        row = AT_TREND_OUT + layer * TREND_ROWS
+        row = AT_TREND_OUT + layer * TREND_STEP
         pack[row : row + TREND_ROWS, :] = parts[3]
         for side in range(2):
             lanes = slice(side * LANES, (side + 1) * LANES)
@@ -1136,7 +1135,7 @@
         trend_in_grad[layer, :, LANES:] = packed[
             row + L0 // 2 : row + L0, : TREND_ROWS - LANES
         ].astype(F32)
-        row = AT_TREND_OUT + layer * TREND_ROWS
+        row = AT_TREND_OUT + layer * TREND_STEP
         trend_out_grad[layer] = packed[row : row + TREND_ROWS, :L0].astype(F32)
     season_in_grad[...] = packed[AT_SEASON_IN : AT_SEASON_IN + NL * SEASON_ROWS, :L0].astype(F32)
     small = [
@@ -1165,11 +1164,12 @@
         args[:5]
         + (jnp.swapaxes(args[5], 0, 1).reshape(NL * SEASON_ROWS, L0),)
         + tuple(jnp.swapaxes(member, 1, 2) for member in args[6:8])
-        + args[8:]
+        + (args[8].reshape(NL * TREND_ROWS, L0),)
+        + args[9:]
     )
-    scratch = [pltpu.VMEM(member.shape, member.dtype) for member in turned[2:]]
+    scratch = [pltpu.VMEM(member.shape, member.dtype) for k, member in enumerate(turned) if k not in (0, 1, 5)]
     scratch += [
-        dma((len(turned) - 2,)),
+        dma((len(turned) - 3,)),
         pltpu.VMEM((chunks, CHUNK, LANES), BF16),
         pltpu.VMEM((chunks, CHUNK, LANES), BF16),
         pltpu.VMEM((chunks, CHUNK, LANES), BF16),
@@ -1250,7 +1250,7 @@
             pltpu.VMEM(tokens.shape, BF16),
             pltpu.VMEM((pack_rows, LANES), BF16),
         ],
-        in_specs=[anywhere] * len(turned),
+        in_specs=[vmem if k == 5 else anywhere for k in range(len(turned))],
         out_specs=[vmem, vmem, vmem],
         scratch_shapes=scratch,
         compiler_params=pltpu.CompilerParams(

time: 108 us -> 108 us (level)
  no operation moved by 1% of the time
where the time goes in v6:
time: 108 us
  Pallas kernels  107 us (99%)
    pallas_call x1, Pallas kernels, body(): pl.pallas_call(functools.partial(kernel_body, groups, n_scale, per_device...  105 us

profile of v6, /device:TPU:0, one launch (start us, length us, event | category | flops | bytes accessed | tf_op | source)
XLA Modules:
  0.0 108.0 jit_solution(12042867740598764597)
XLA Ops:
  0.6 105.3 %shard_map.203 = (bf16[4608,128]{1,0:T(8,128)(2,1)S(1)}, bf16[4608,128]{1,0:T(8,128)(2,1)S(1)}, bf16[1920,128]{1,0:T(8,128)(2,1)S(1)}) custom-call(bf16[4608,128]{1,0:T(8,128)(2,1)} %tokens.1, bf16[4608,128]{1,0:T(8,128)(2,1)} %cotangent.1, s32[1,384]{1,0:T(1,128)} %item_mask_hbm.1, f32[2,128]{1,0:T(2,128)} %ln_gain_hbm.1, f32[2,128]{1,0:T(2,128)} %ln_bias_hbm.1, ...), custom_call_target="tpu_custom_call" | custom-call | tf_op jit(solution)/shard_map/pallas_call | solution.py:1246
  105.9 1.9 %shard_map.204 = (bf16[4608,128]{1,0:T(8,128)(2,1)}, bf16[4608,128]{1,0:T(8,128)(2,1)}, f32[2,128]{1,0:T(2,128)}, f32[2,128]{1,0:T(2,128)}, f32[168,96]{1,0:T(8,...) custom-call(bf16[4608,128]{1,0:T(8,128)(2,1)S(1)} %get-tuple-element, ...), custom_call_target="tpu_custom_call" | custom-call | tf_op jit(solution)/shard_map/pallas_call | solution.py:1274

commit v7 on v6

--- a/solution.py
+++ b/solution.py
@@ -294,17 +294,11 @@
     def greet(device):
         pl.semaphore_signal(barrier, inc=1, device_id=device, device_id_type=MESH)
 
-    def greet_row(k, carry):
+    for k in range(1, groups):
         greet((scale_index, lax.rem(position + k, groups)))
-        return carry
-
-    def greet_plane(k, carry):
-        other = lax.rem(scale_index + 1 + lax.div(k, plane_dp), n_scale)
-        greet((other, (depth_index * plane_dp + lax.rem(k, plane_dp)) * 2 + core))
-        return carry
-
-    lax.fori_loop(1, groups, greet_row, 0)
-    lax.fori_loop(0, (n_scale - 1) * plane_dp, greet_plane, 0)
+    for k in range((n_scale - 1) * plane_dp):
+        other = lax.rem(scale_index + 1 + k // plane_dp, n_scale)
+        greet((other, (depth_index * plane_dp + k % plane_dp) * 2 + core))
     pl.semaphore_wait(barrier, groups - 1 + (n_scale - 1) * plane_dp)
 
     def relayed(scale, slot, half):

time: 108 us -> 108 us (level)
  no operation moved by 1% of the time
where the time goes in v7:
time: 108 us
  Pallas kernels  107 us (99%)
    pallas_call x1, Pallas kernels, body(): pl.pallas_call(functools.partial(kernel_body, groups, n_scale, per_device...  105 us

profile of v7, /device:TPU:0, one launch (start us, length us, event | category | flops | bytes accessed | tf_op | source)
XLA Modules:
  0.0 108.0 jit_solution(9884342887121108301)
XLA Ops:
  0.6 105.3 %shard_map.203 = (bf16[4608,128]{1,0:T(8,128)(2,1)S(1)}, bf16[4608,128]{1,0:T(8,128)(2,1)S(1)}, bf16[1920,128]{1,0:T(8,128)(2,1)S(1)}) custom-call(bf16[4608,128]{1,0:T(8,128)(2,1)} %tokens.1, bf16[4608,128]{1,0:T(8,128)(2,1)} %cotangent.1, s32[1,384]{1,0:T(1,128)} %item_mask_hbm.1, f32[2,128]{1,0:T(2,128)} %ln_gain_hbm.1, f32[2,128]{1,0:T(2,128)} %ln_bias_hbm.1, ...), custom_call_target="tpu_custom_call" | custom-call | tf_op jit(solution)/shard_map/pallas_call | solution.py:1240
  105.9 1.9 %shard_map.204 = (bf16[4608,128]{1,0:T(8,128)(2,1)}, bf16[4608,128]{1,0:T(8,128)(2,1)}, f32[2,128]{1,0:T(2,128)}, f32[2,128]{1,0:T(2,128)}, f32[168,96]{1,0:T(8,...) custom-call(bf16[4608,128]{1,0:T(8,128)(2,1)S(1)} %get-tuple-element, ...), custom_call_target="tpu_custom_call" | custom-call | tf_op jit(solution)/shard_map/pallas_call | solution.py:1268

commit v8 on v6

--- a/solution.py
+++ b/solution.py
@@ -156,7 +156,7 @@
         | {("backward", c): [(1, c)] for c in range(last)}
         | {("forward", last): [(0, last - 1), (0, last)], ("gathered", 0): [(1, last)]},
         (False, False): at_once(lower_chunks) | {("backward", last): [], ("paired", 0): [(1, last)]},
-        (False, True): at_once(upper_chunks) | {("backward", top): [], ("paired", 0): [(1, top)]},
+        (False, True): at_once(upper_chunks) | {("forward", top): [], ("backward", top): [], ("paired", 0): [(0, top), (1, top)]},
         (True, True): {
             ("crossed", 0): [(kind, c) for c in range(upper_chunks) for kind in range(2)][:-1],
             ("gathered", 0): [(1, top)],

time: 108 us -> 108 us (level)
  no operation moved by 1% of the time
where the time goes in v8:
time: 108 us
  Pallas kernels  107 us (99%)
    pallas_call x1, Pallas kernels, body(): pl.pallas_call(functools.partial(kernel_body, groups, n_scale, per_device...  105 us

profile of v8, /device:TPU:0, one launch (start us, length us, event | category | flops | bytes accessed | tf_op | source)
XLA Modules:
  0.0 108.0 jit_solution(16014614791914921715)
XLA Ops:
  0.6 105.3 %shard_map.203 = (bf16[4608,128]{1,0:T(8,128)(2,1)S(1)}, bf16[4608,128]{1,0:T(8,128)(2,1)S(1)}, bf16[1920,128]{1,0:T(8,128)(2,1)S(1)}) custom-call(bf16[4608,128]{1,0:T(8,128)(2,1)} %tokens.1, bf16[4608,128]{1,0:T(8,128)(2,1)} %cotangent.1, s32[1,384]{1,0:T(1,128)} %item_mask_hbm.1, f32[2,128]{1,0:T(2,128)} %ln_gain_hbm.1, f32[2,128]{1,0:T(2,128)} %ln_bias_hbm.1, ...), custom_call_target="tpu_custom_call" | custom-call | tf_op jit(solution)/shard_map/pallas_call | solution.py:1246
  105.9 1.9 %shard_map.204 = (bf16[4608,128]{1,0:T(8,128)(2,1)}, bf16[4608,128]{1,0:T(8,128)(2,1)}, f32[2,128]{1,0:T(2,128)}, f32[2,128]{1,0:T(2,128)}, f32[168,96]{1,0:T(8,...) custom-call(bf16[4608,128]{1,0:T(8,128)(2,1)S(1)} %get-tuple-element, ...), custom_call_target="tpu_custom_call" | custom-call | tf_op jit(solution)/shard_map/pallas_call | solution.py:1274
